TPU v7x, 32 devices: a whole 2x2x4 slice. The times are simulated.
32 devices in a mesh: blk: 4 (over z), dp: 2 (over x), head: 4 (over y, core).
Axes of the slice: x: 2, y: 2, z: 4, core: 2. Of those that a mesh axis runs over, the one named last changes fastest.
Arguments:
- tokens: bfloat16 [2, 2, 4, 196608], P(None, 'dp', 'head', 'blk'), may hold values from -6 to 6
- doc_lengths: int32 [2, 2, 4], P(None, 'dp'), may hold values from 0 to 1024, as said below
- cotangent: bfloat16 [2, 2, 4, 196608], P(None, 'dp', 'head', 'blk'), may hold values from -6 to 6
- query_weight: bfloat16 [4, 192, 192], P('head', ('blk', 'dp')), may hold values from -0.4375 to 0.4375
- query_bias: bfloat16 [4, 192], P('head', ('blk', 'dp')), may hold values from -1.75 to 1.75
- key_weight: bfloat16 [4, 192, 192], P('head', ('blk', 'dp')), may hold values from -0.4375 to 0.4375
- value_weight: bfloat16 [4, 192, 192], P('head', ('blk', 'dp')), may hold values from -0.4375 to 0.4375
- value_bias: bfloat16 [4, 192], P('head', ('blk', 'dp')), may hold values from -1.75 to 1.75
- out_weight: bfloat16 [768, 768], P(('blk', 'dp'), 'head'), may hold values from -3.5 to 3.5
- out_bias: bfloat16 [4, 192], P('head', ('blk', 'dp')), may hold values from -1.75 to 1.75
- first_gain: bfloat16 [4, 192], P('head', ('blk', 'dp')), may hold values from 0.5 to 1.5
- first_shift: bfloat16 [4, 192], P('head', ('blk', 'dp')), may hold values from -1.75 to 1.75
- up_weight: bfloat16 [4, 192, 768], P('head', ('blk', 'dp')), may hold values from -0.4375 to 0.4375
- up_bias: bfloat16 [4, 768], P('head', ('blk', 'dp')), may hold values from -1.75 to 1.75
- down_weight: bfloat16 [4, 768, 192], P('head', ('blk', 'dp')), may hold values from -0.21875 to 0.21875
- down_bias: bfloat16 [4, 192], P('head', ('blk', 'dp')), may hold values from -1.75 to 1.75
- second_gain: bfloat16 [4, 192], P('head', ('blk', 'dp')), may hold values from 0.5 to 1.5
- second_shift: bfloat16 [4, 192], P('head', ('blk', 'dp')), may hold values from -1.75 to 1.75
Outputs:
- mixed_out: bfloat16 [2, 2, 4, 196608], P(None, 'dp', 'head', 'blk')
- tokens_grad: float32 [2, 2, 4, 196608], P(None, 'dp', 'head', 'blk')
- query_weight_grad: float32 [4, 192, 192], P('head', ('blk', 'dp'))
- query_bias_grad: float32 [4, 192], P('head', ('blk', 'dp'))
- key_weight_grad: float32 [4, 192, 192], P('head', ('blk', 'dp'))
- value_weight_grad: float32 [4, 192, 192], P('head', ('blk', 'dp'))
- value_bias_grad: float32 [4, 192], P('head', ('blk', 'dp'))
- out_weight_grad: float32 [768, 768], P(('blk', 'dp'), 'head')
- out_bias_grad: float32 [4, 192], P('head', ('blk', 'dp'))
- first_gain_grad: float32 [4, 192], P('head', ('blk', 'dp'))
- first_shift_grad: float32 [4, 192], P('head', ('blk', 'dp'))
- up_weight_grad: float32 [4, 192, 768], P('head', ('blk', 'dp'))
- up_bias_grad: float32 [4, 768], P('head', ('blk', 'dp'))
- down_weight_grad: float32 [4, 768, 192], P('head', ('blk', 'dp'))
- down_bias_grad: float32 [4, 192], P('head', ('blk', 'dp'))
- second_gain_grad: float32 [4, 192], P('head', ('blk', 'dp'))
- second_shift_grad: float32 [4, 192], P('head', ('blk', 'dp'))
Inputs may be any that keep to these rules, and one draw needn't show every extreme that they name: `doc_lengths`: each row sums to 1024. In every micro-batch one group, drawn from the seed, holds one sequence of all 1024 tokens (its other entries 0); every other group holds 4 sequences, each of 128 to 384 tokens.
All inputs are finite; a program needn't handle non-finite values.
Results may differ from a plain program's by a relative error of at most 0.025.
Values may be sent and summed in bfloat16 or wider, within the bound.
A program may use at most 128 MiB of HBM per device.

v0:
```python
from functools import partial

import jax
import jax.numpy as jnp
from jax import lax
from jax.sharding import PartitionSpec as P

D = 768
HEAD_DIM = 64


EPS = 1e-05
NEGATIVE = -1e30


def matmul(left, right):
    return jnp.dot(left, right, preferred_element_type=jnp.float32)


def matmul_tn(left, right):
    return lax.dot_general(
        left, right, (((0,), (0,)), ((), ())), preferred_element_type=jnp.float32
    )


def matmul_nt(left, right):
    return lax.dot_general(
        left, right, (((1,), (1,)), ((), ())), preferred_element_type=jnp.float32
    )


def doc_index(positions, ends):
    return jnp.sum((positions[:, None] >= ends[None, :]).astype(jnp.int32), axis=1)


def norm_forward(hidden, gain, shift):
    row_sums = lax.psum((jnp.sum(hidden, axis=1), jnp.sum(hidden * hidden, axis=1)), "head")
    mean_val = row_sums[0] / D
    var_val = row_sums[1] / D - mean_val * mean_val
    inv_std = lax.rsqrt(var_val + EPS)
    normed = (hidden - mean_val[:, None]) * inv_std[:, None]
    return (normed * gain + shift, normed, inv_std)


def norm_backward(grad_out, normed, inv_std, gain):
    grad_normed = grad_out * gain
    row_sums = lax.psum(
        (jnp.sum(grad_normed, axis=1), jnp.sum(grad_normed * normed, axis=1)), "head"
    )
    grad_in = inv_std[:, None] * (
        grad_normed - row_sums[0][:, None] / D - normed * row_sums[1][:, None] / D
    )
    return (grad_in, jnp.sum(grad_out * normed, axis=0), jnp.sum(grad_out, axis=0))


def one_batch(tokens_flat, lengths_m, cotan_flat, weights):
    weight_q = weights[0][0]
    weight_k = weights[1][0]
    weight_v = weights[2][0]
    weight_o = weights[3]
    weight_up = weights[4][0]
    weight_down = weights[5][0]
    bias_q = weights[6][0].astype(jnp.float32)
    bias_v = weights[7][0].astype(jnp.float32)
    bias_o = weights[8][0].astype(jnp.float32)
    gain_one = weights[9][0].astype(jnp.float32)
    shift_one = weights[10][0].astype(jnp.float32)
    bias_up = weights[11][0].astype(jnp.float32)
    bias_down = weights[12][0].astype(jnp.float32)
    gain_two = weights[13][0].astype(jnp.float32)
    shift_two = weights[14][0].astype(jnp.float32)
    group_width = weight_q.shape[1]
    tokens_m = tokens_flat.reshape(-1, group_width)
    cotan_m = cotan_flat.reshape(-1, group_width)
    row_count = tokens_m.shape[0]
    heads_here = tokens_m.shape[1] // HEAD_DIM
    score_scale = HEAD_DIM ** (-0.5)
    ends = jnp.cumsum(lengths_m)
    positions = lax.axis_index("blk") * row_count + jnp.arange(row_count, dtype=jnp.int32)
    own_docs = doc_index(positions, ends)
    source = tokens_m.astype(jnp.float32)
    query_b = (matmul(tokens_m, weight_q) + bias_q).astype(jnp.bfloat16)
    key_b = matmul(tokens_m, weight_k).astype(jnp.bfloat16)
    value_b = (matmul(tokens_m, weight_v) + bias_v).astype(jnp.bfloat16)
    query_h = query_b.reshape(row_count, heads_here, HEAD_DIM)
    key_h = key_b.reshape(row_count, heads_here, HEAD_DIM)
    value_h = value_b.reshape(row_count, heads_here, HEAD_DIM)
    run_max = jnp.full((heads_here, row_count), NEGATIVE, jnp.float32)
    run_accum = jnp.zeros((row_count, heads_here, HEAD_DIM), jnp.float32)
    key_piece = lax.all_gather(key_b, "blk", axis=0, tiled=True)
    value_piece = lax.all_gather(value_b, "blk", axis=0, tiled=True)
    piece_rows = key_piece.shape[0]
    key_docs = doc_index(jnp.arange(piece_rows, dtype=jnp.int32), ends)
    allowed = (own_docs[:, None] == key_docs[None, :])[None]
    scores = (
        jnp.einsum(
            "qhd,khd->hqk",
            query_h,
            key_piece.reshape(piece_rows, heads_here, HEAD_DIM),
            preferred_element_type=jnp.float32,
        )
        * score_scale
    )
    masked = jnp.where(allowed, scores, NEGATIVE)
    new_max = jnp.maximum(run_max, jnp.max(masked, axis=2))
    expo = jnp.where(allowed, jnp.exp(masked - new_max[:, :, None]), 0.0)
    fade = jnp.exp(run_max - new_max)
    run_total = jnp.sum(expo, axis=2)
    added = jnp.einsum(
        "hqk,khd->qhd",
        expo.astype(jnp.bfloat16),
        value_piece.reshape(piece_rows, heads_here, HEAD_DIM),
        preferred_element_type=jnp.float32,
    )
    run_accum = run_accum * fade.T[:, :, None] + added
    attn_b = (run_accum / run_total.T[:, :, None]).reshape(row_count, -1).astype(jnp.bfloat16)
    log_sum = new_max + jnp.log(run_total)
    mixed_all = lax.all_gather(attn_b, "head", axis=1, tiled=True)
    hidden_one = source + matmul(mixed_all, weight_o) + bias_o
    first_out, normed_one, inv_one = norm_forward(hidden_one, gain_one, shift_one)
    first_b = first_out.astype(jnp.bfloat16)
    pre_up = matmul(first_b, weight_up) + bias_up
    activated, gelu_pullback = jax.vjp(partial(jax.nn.gelu, approximate=False), pre_up)
    act_b = activated.astype(jnp.bfloat16)
    hidden_two = first_out + matmul(act_b, weight_down) + bias_down
    result, normed_two, inv_two = norm_forward(hidden_two, gain_two, shift_two)
    grad_two, grad_gain_two, grad_shift_two = norm_backward(
        cotan_m.astype(jnp.float32), normed_two, inv_two, gain_two
    )
    grad_down_b = grad_two.astype(jnp.bfloat16)
    grad_w_down = matmul_tn(act_b, grad_down_b)
    grad_b_down = jnp.sum(grad_down_b.astype(jnp.float32), axis=0)
    grad_pre = gelu_pullback(matmul_nt(grad_down_b, weight_down))[0]
    grad_pre_b = grad_pre.astype(jnp.bfloat16)
    grad_w_up = matmul_tn(first_b, grad_pre_b)
    grad_b_up = jnp.sum(grad_pre_b.astype(jnp.float32), axis=0)
    grad_first = grad_two + matmul_nt(grad_pre_b, weight_up)
    grad_one, grad_gain_one, grad_shift_one = norm_backward(
        grad_first, normed_one, inv_one, gain_one
    )
    grad_proj_b = grad_one.astype(jnp.bfloat16)
    grad_w_out = matmul_tn(mixed_all, grad_proj_b)
    grad_b_out = jnp.sum(grad_proj_b.astype(jnp.float32), axis=0)
    grad_attn = lax.psum_scatter(
        matmul_nt(grad_proj_b, weight_o).astype(jnp.bfloat16),
        "head",
        scatter_dimension=1,
        tiled=True,
    )
    grad_h = grad_attn.reshape(row_count, heads_here, HEAD_DIM)
    delta = jnp.sum(
        grad_h.astype(jnp.float32)
        * attn_b.reshape(row_count, heads_here, HEAD_DIM).astype(jnp.float32),
        axis=2,
    ).T
    all_lse, all_delta = (
        lax.all_gather(log_sum, "blk", axis=1, tiled=True),
        lax.all_gather(delta, "blk", axis=1, tiled=True),
    )
    key_piece = lax.all_gather(key_b, "blk", axis=0, tiled=True)
    value_piece = lax.all_gather(value_b, "blk", axis=0, tiled=True)
    piece_rows = key_piece.shape[0]
    key_part = key_piece.reshape(piece_rows, heads_here, HEAD_DIM)
    key_docs = doc_index(jnp.arange(piece_rows, dtype=jnp.int32), ends)
    allowed = (own_docs[:, None] == key_docs[None, :])[None]
    scores = (
        jnp.einsum("qhd,khd->hqk", query_h, key_part, preferred_element_type=jnp.float32)
        * score_scale
    )
    prob = jnp.where(allowed, jnp.exp(scores - log_sum[:, :, None]), 0.0)
    grad_prob = jnp.einsum(
        "qhd,khd->hqk",
        grad_h,
        value_piece.reshape(piece_rows, heads_here, HEAD_DIM),
        preferred_element_type=jnp.float32,
    )
    grad_score = (prob * (grad_prob - delta[:, :, None])).astype(jnp.bfloat16)
    grad_query = jnp.einsum(
        "hqk,khd->qhd", grad_score, key_part, preferred_element_type=jnp.float32
    )
    query_piece = lax.all_gather(query_b, "blk", axis=0, tiled=True)
    grad_piece = lax.all_gather(grad_attn, "blk", axis=0, tiled=True)
    piece_rows = query_piece.shape[0]
    query_part = query_piece.reshape(piece_rows, heads_here, HEAD_DIM)
    grad_part = grad_piece.reshape(piece_rows, heads_here, HEAD_DIM)
    query_docs = doc_index(jnp.arange(piece_rows, dtype=jnp.int32), ends)
    allowed = (query_docs[:, None] == own_docs[None, :])[None]
    scores = (
        jnp.einsum("qhd,khd->hqk", query_part, key_h, preferred_element_type=jnp.float32)
        * score_scale
    )
    prob = jnp.where(allowed, jnp.exp(scores - all_lse[:, :, None]), 0.0)
    grad_value = jnp.einsum(
        "hqk,qhd->khd", prob.astype(jnp.bfloat16), grad_part, preferred_element_type=jnp.float32
    )
    grad_prob = jnp.einsum("qhd,khd->hqk", grad_part, value_h, preferred_element_type=jnp.float32)
    grad_score = (prob * (grad_prob - all_delta[:, :, None])).astype(jnp.bfloat16)
    grad_key = jnp.einsum(
        "hqk,qhd->khd", grad_score, query_part, preferred_element_type=jnp.float32
    )
    grad_query_b = (grad_query * score_scale).reshape(row_count, -1).astype(jnp.bfloat16)
    grad_key_b = (grad_key * score_scale).reshape(row_count, -1).astype(jnp.bfloat16)
    grad_value_b = grad_value.reshape(row_count, -1).astype(jnp.bfloat16)
    grad_tokens = (
        grad_one
        + matmul_nt(grad_query_b, weight_q)
        + matmul_nt(grad_key_b, weight_k)
        + matmul_nt(grad_value_b, weight_v)
    )
    grads = (
        matmul_tn(tokens_m, grad_query_b)[None],
        matmul_tn(tokens_m, grad_key_b)[None],
        matmul_tn(tokens_m, grad_value_b)[None],
        grad_w_out,
        grad_w_up[None],
        grad_w_down[None],
        jnp.sum(grad_query_b.astype(jnp.float32), axis=0)[None],
        jnp.sum(grad_value_b.astype(jnp.float32), axis=0)[None],
        grad_b_out[None],
        grad_gain_one[None],
        grad_shift_one[None],
        grad_b_up[None],
        grad_b_down[None],
        grad_gain_two[None],
        grad_shift_two[None],
    )
    return (result.astype(jnp.bfloat16).reshape(-1), grad_tokens.reshape(-1), grads)


def body(
    tokens,
    doc_lengths,
    cotangent,
    query_weight,
    query_bias,
    key_weight,
    value_weight,
    value_bias,
    out_weight,
    out_bias,
    first_gain,
    first_shift,
    up_weight,
    up_bias,
    down_weight,
    down_bias,
    second_gain,
    second_shift,
):
    stored = (
        query_weight,
        key_weight,
        value_weight,
        out_weight,
        up_weight,
        down_weight,
        query_bias,
        value_bias,
        out_bias,
        first_gain,
        first_shift,
        up_bias,
        down_bias,
        second_gain,
        second_shift,
    )
    start_totals = tuple((jnp.zeros(member.shape, jnp.float32) for member in stored))

    def step(totals, batch_item):
        current = (
            lax.all_gather(query_weight, ("blk", "dp"), axis=1, tiled=True),
            lax.all_gather(key_weight, ("blk", "dp"), axis=1, tiled=True),
            lax.all_gather(value_weight, ("blk", "dp"), axis=1, tiled=True),
            lax.all_gather(out_weight, ("blk", "dp"), axis=0, tiled=True),
            lax.all_gather(up_weight, ("blk", "dp"), axis=1, tiled=True),
            lax.all_gather(down_weight, ("blk", "dp"), axis=1, tiled=True),
            lax.all_gather(query_bias, ("blk", "dp"), axis=1, tiled=True),
            lax.all_gather(value_bias, ("blk", "dp"), axis=1, tiled=True),
            lax.all_gather(out_bias, ("blk", "dp"), axis=1, tiled=True),
            lax.all_gather(first_gain, ("blk", "dp"), axis=1, tiled=True),
            lax.all_gather(first_shift, ("blk", "dp"), axis=1, tiled=True),
            lax.all_gather(up_bias, ("blk", "dp"), axis=1, tiled=True),
            lax.all_gather(down_bias, ("blk", "dp"), axis=1, tiled=True),
            lax.all_gather(second_gain, ("blk", "dp"), axis=1, tiled=True),
            lax.all_gather(second_shift, ("blk", "dp"), axis=1, tiled=True),
        )
        result, grad_tokens, grads = one_batch(batch_item[0], batch_item[1], batch_item[2], current)
        grads = (
            lax.psum_scatter(grads[0], ("blk", "dp"), scatter_dimension=1, tiled=True),
            lax.psum_scatter(grads[1], ("blk", "dp"), scatter_dimension=1, tiled=True),
            lax.psum_scatter(grads[2], ("blk", "dp"), scatter_dimension=1, tiled=True),
            lax.psum_scatter(grads[3], ("blk", "dp"), scatter_dimension=0, tiled=True),
            lax.psum_scatter(grads[4], ("blk", "dp"), scatter_dimension=1, tiled=True),
            lax.psum_scatter(grads[5], ("blk", "dp"), scatter_dimension=1, tiled=True),
            lax.psum_scatter(grads[6], ("blk", "dp"), scatter_dimension=1, tiled=True),
            lax.psum_scatter(grads[7], ("blk", "dp"), scatter_dimension=1, tiled=True),
            lax.psum_scatter(grads[8], ("blk", "dp"), scatter_dimension=1, tiled=True),
            lax.psum_scatter(grads[9], ("blk", "dp"), scatter_dimension=1, tiled=True),
            lax.psum_scatter(grads[10], ("blk", "dp"), scatter_dimension=1, tiled=True),
            lax.psum_scatter(grads[11], ("blk", "dp"), scatter_dimension=1, tiled=True),
            lax.psum_scatter(grads[12], ("blk", "dp"), scatter_dimension=1, tiled=True),
            lax.psum_scatter(grads[13], ("blk", "dp"), scatter_dimension=1, tiled=True),
            lax.psum_scatter(grads[14], ("blk", "dp"), scatter_dimension=1, tiled=True),
        )
        new_totals = tuple((left + right for left, right in zip(totals, grads)))
        return (new_totals, (result, grad_tokens))

    totals, (results, input_grads) = lax.scan(
        step, start_totals, (tokens[:, 0, 0], doc_lengths[:, 0], cotangent[:, 0, 0])
    )
    return (
        results[:, None, None],
        input_grads[:, None, None],
        totals[0],
        totals[6],
        totals[1],
        totals[2],
        totals[7],
        totals[3],
        totals[8],
        totals[9],
        totals[10],
        totals[4],
        totals[11],
        totals[5],
        totals[12],
        totals[13],
        totals[14],
    )


def solution(mesh):
    placed = (
        P(None, "dp", "head", "blk"),
        P(None, "dp", None),
        P(None, "dp", "head", "blk"),
        P("head", ("blk", "dp"), None),
        P("head", ("blk", "dp")),
        P("head", ("blk", "dp"), None),
        P("head", ("blk", "dp"), None),
        P("head", ("blk", "dp")),
        P(("blk", "dp"), "head"),
        P("head", ("blk", "dp")),
        P("head", ("blk", "dp")),
        P("head", ("blk", "dp")),
        P("head", ("blk", "dp"), None),
        P("head", ("blk", "dp")),
        P("head", ("blk", "dp"), None),
        P("head", ("blk", "dp")),
        P("head", ("blk", "dp")),
        P("head", ("blk", "dp")),
    )
    return jax.shard_map(
        body,
        mesh=mesh,
        in_specs=placed,
        out_specs=(
            P(None, "dp", "head", "blk"),
            P(None, "dp", "head", "blk"),
            P("head", ("blk", "dp"), None),
            P("head", ("blk", "dp")),
            P("head", ("blk", "dp"), None),
            P("head", ("blk", "dp"), None),
            P("head", ("blk", "dp")),
            P(("blk", "dp"), "head"),
            P("head", ("blk", "dp")),
            P("head", ("blk", "dp")),
            P("head", ("blk", "dp")),
            P("head", ("blk", "dp"), None),
            P("head", ("blk", "dp")),
            P("head", ("blk", "dp"), None),
            P("head", ("blk", "dp")),
            P("head", ("blk", "dp")),
            P("head", ("blk", "dp")),
        ),
        check_vma=False,
    )
```

profile of v0, /device:TPU:0, one launch (start us, length us, event | category | flops | bytes accessed | tf_op | source)
XLA Modules:
  0.0 1602.8 jit_solution(13604828899273190183)
XLA Ops:
  7.3 1585.3 %while.43 = (s32[]{:T(128)}, f32[1,24,192]{2,1,0:T(8,128)}, f32[1,24,192]{2,1,0:T(8,128)}, f32[1,24,192]{2,1,0:T(8,128)}, f32[96,192]{1,0:T(8,128)}, /*index=5*/...) while((s32[]{:T(128)}, f32[1,24,192]{2,1,0:T(8,128)}, ...), condition=%wide.region_48.49_spmd.clone, body=%wide.region_0.48_spmd.clone.sunk | while | flops 1699280768 | bytes 96746496 | solution.py:308
  25.1 24.0 %all-reduce.38 = (bf16[192]{0:T(256)(128)(2,1)S(1)}, bf16[768]{0:T(1024)(128)(2,1)S(1)}, bf16[192]{0:T(256)(128)(2,1)S(1)}, bf16[192]{0:T(256)(128)(2,1)S(1)}, b...) all-reduce(bf16[192]{0:T(256)(128)(2,1)} %dynamic-update-slice.27, ...), channel_id=1, replica_groups=mesh['blk'=4,'dp'=2,'head'=4] {'blk','dp'}, use_global_device_ids=true, to_apply=%add | all-reduce | flops 2304 | bytes 9216 | tf_op jit(solution)/shard_map/while
  50.8 30.8 %all_gather.96 = bf16[1,192,192]{2,1,0:T(8,128)(2,1)S(1)} all-gather(bf16[1,24,192]{2,1,0:T(8,128)(2,1)} %get-tuple-element.1030), channel_id=1, replica_groups=mesh['blk'=4,'dp'=2,'head'=4] {'blk','dp'}, dimensions={1}, use_global_device_ids=true | all-gather | bytes 82944 | tf_op jit(solution)/shard_map/while/body/eval_jaxpr/all_gather | solution.py:271
  82.6 30.8 %all_gather.94 = bf16[1,192,192]{2,1,0:T(8,128)(2,1)S(1)} all-gather(bf16[1,24,192]{2,1,0:T(8,128)(2,1)} %get-tuple-element.1028), channel_id=1, replica_groups=mesh['blk'=4,'dp'=2,'head'=4] {'blk','dp'}, dimensions={1}, use_global_device_ids=true | all-gather | bytes 82944 | tf_op jit(solution)/shard_map/while/body/eval_jaxpr/all_gather | solution.py:272
  114.4 14.3 all_gather.95
  131.4 30.6 %all_gather.98 = bf16[1,192,192]{2,1,0:T(8,128)(2,1)S(1)} all-gather(bf16[1,24,192]{2,1,0:T(8,128)(2,1)S(1)} %copy-done.48), channel_id=1, replica_groups=mesh['blk'=4,'dp'=2,'head'=4] {'blk','dp'}, dimensions={1}, use_global_device_ids=true | all-gather | bytes 82944 | tf_op jit(solution)/shard_map/while/body/eval_jaxpr/all_gather | solution.py:273
  162.9 14.3 all_gather.99
  178.3 6.9 all_gather.100
  185.8 33.2 %all_gather.97 = bf16[768,192]{1,0:T(8,128)(2,1)} all-gather(bf16[96,192]{1,0:T(8,128)(2,1)S(1)} %copy-done.37), channel_id=1, replica_groups=mesh['blk'=4,'dp'=2,'head'=4] {'blk','dp'}, dimensions={0}, use_global_device_ids=true | all-gather | bytes 331776 | tf_op jit(solution)/shard_map/while/body/eval_jaxpr/all_gather | solution.py:274
  220.2 32.9 %all_gather.101 = bf16[1,192,768]{2,1,0:T(8,128)(2,1)} all-gather(bf16[1,24,768]{2,1,0:T(8,128)(2,1)S(1)} %copy-done.39), channel_id=1, replica_groups=mesh['blk'=4,'dp'=2,'head'=4] {'blk','dp'}, dimensions={1}, use_global_device_ids=true | all-gather | bytes 331776 | tf_op jit(solution)/shard_map/while/body/eval_jaxpr/all_gather | solution.py:275
  253.6 33.2 %all_gather.102 = bf16[1,768,192]{2,1,0:T(8,128)(2,1)} all-gather(bf16[1,96,192]{2,1,0:T(8,128)(2,1)S(1)} %copy-done.38), channel_id=1, replica_groups=mesh['blk'=4,'dp'=2,'head'=4] {'blk','dp'}, dimensions={1}, use_global_device_ids=true | all-gather | bytes 331776 | tf_op jit(solution)/shard_map/while/body/eval_jaxpr/all_gather | solution.py:276
  303.5 6.5 all-reduce.40
  311.2 5.7 all-reduce.41
  322.5 6.2 all-reduce.42
  333.6 15.4 all_gather.103
  349.9 13.1 all_gather.106
  366.2 14.8 all_gather.104
  387.1 13.1 all_gather.105
  425.5 17.5 %all-reduce.43 = (f32[1,192]{1,0:T(1,128)S(1)}, f32[1,192]{1,0:T(1,128)S(1)}, f32[1,192]{1,0:T(1,128)S(1)}, f32[1,192]{1,0:T(1,128)S(1)}, f32[1,192]{1,0:T(1,128...) all-reduce(f32[1,192]{1,0:T(1,128)S(1)} %broadcast_in_dim.333, ...), channel_id=9, replica_groups=mesh['blk'=4,'dp'=2,'head'=4] {'blk','dp'}, use_global_device_ids=true, to_apply=%region_31.31.clone | all-reduce | flops 1536 | bytes 12288 | tf_op jit(solution)/shard_map/while
  443.5 35.6 %reduce-scatter.31.cloned.1.call-done = f32[1,24,192]{2,1,0:T(8,128)} async-done(((f32[1,192,192]{2,1,0:T(8,128)}), f32[1,24,192]{2,1,0:T(8,128)}) %reduce-scatter.31.cloned.1.call-update) | async-done | bytes 18448 | tf_op jit(solution)/shard_map/while/body/eval_jaxpr/reduce_scatter | solution.py:291
  479.8 62.5 %reduce-scatter.29.cloned.1.call-done = f32[1,24,192]{2,1,0:T(8,128)} async-done(((f32[1,192,192]{2,1,0:T(8,128)}), f32[1,24,192]{2,1,0:T(8,128)}) %reduce-scatter.29.cloned.1.call-update) | async-done | bytes 18448 | tf_op jit(solution)/shard_map/while/body/eval_jaxpr/reduce_scatter | solution.py:290
  543.0 63.0 %reduce-scatter.27.cloned.1.call-done = f32[1,24,192]{2,1,0:T(8,128)} async-done(((f32[1,192,192]{2,1,0:T(8,128)}), f32[1,24,192]{2,1,0:T(8,128)}) %reduce-scatter.27.cloned.1.call-update) | async-done | bytes 18448 | tf_op jit(solution)/shard_map/while/body/eval_jaxpr/reduce_scatter | solution.py:289
  606.8 63.9 %reduce-scatter.37.cloned.1.call-done = f32[96,192]{1,0:T(8,128)} async-done(((f32[768,192]{1,0:T(8,128)}), f32[96,192]{1,0:T(8,128)}) %reduce-scatter.37.cloned.1.call-update) | async-done | bytes 73744 | tf_op jit(solution)/shard_map/while
  671.8 63.7 %reduce-scatter.35.cloned.1.call-done = f32[1,24,768]{2,1,0:T(8,128)} async-done(((f32[1,192,768]{2,1,0:T(8,128)}), f32[1,24,768]{2,1,0:T(8,128)}) %reduce-scatter.35.cloned.1.call-update) | async-done | bytes 73744 | tf_op jit(solution)/shard_map/while/body/eval_jaxpr/reduce_scatter | solution.py:293
  736.5 63.9 %reduce-scatter.33.cloned.1.call-done = f32[96,192]{1,0:T(8,128)} async-done(((f32[768,192]{1,0:T(8,128)}), f32[96,192]{1,0:T(8,128)}) %reduce-scatter.33.cloned.1.call-update) | async-done | bytes 73744 | tf_op jit(solution)/shard_map/while/body/eval_jaxpr/reduce_scatter | solution.py:292
  819.6 20.3 %all-reduce.38 = (bf16[192]{0:T(256)(128)(2,1)S(1)}, bf16[768]{0:T(1024)(128)(2,1)S(1)}, bf16[192]{0:T(256)(128)(2,1)S(1)}, bf16[192]{0:T(256)(128)(2,1)S(1)}, b...) all-reduce(bf16[192]{0:T(256)(128)(2,1)} %dynamic-update-slice.27, ...), channel_id=1, replica_groups=mesh['blk'=4,'dp'=2,'head'=4] {'blk','dp'}, use_global_device_ids=true, to_apply=%add | all-reduce | flops 2304 | bytes 9216 | tf_op jit(solution)/shard_map/while
  841.6 30.8 %all_gather.96 = bf16[1,192,192]{2,1,0:T(8,128)(2,1)S(1)} all-gather(bf16[1,24,192]{2,1,0:T(8,128)(2,1)} %get-tuple-element.1030), channel_id=1, replica_groups=mesh['blk'=4,'dp'=2,'head'=4] {'blk','dp'}, dimensions={1}, use_global_device_ids=true | all-gather | bytes 82944 | tf_op jit(solution)/shard_map/while/body/eval_jaxpr/all_gather | solution.py:271
  873.4 30.8 %all_gather.94 = bf16[1,192,192]{2,1,0:T(8,128)(2,1)S(1)} all-gather(bf16[1,24,192]{2,1,0:T(8,128)(2,1)} %get-tuple-element.1028), channel_id=1, replica_groups=mesh['blk'=4,'dp'=2,'head'=4] {'blk','dp'}, dimensions={1}, use_global_device_ids=true | all-gather | bytes 82944 | tf_op jit(solution)/shard_map/while/body/eval_jaxpr/all_gather | solution.py:272
  905.2 14.3 all_gather.95
  922.3 30.6 %all_gather.98 = bf16[1,192,192]{2,1,0:T(8,128)(2,1)S(1)} all-gather(bf16[1,24,192]{2,1,0:T(8,128)(2,1)S(1)} %copy-done.48), channel_id=1, replica_groups=mesh['blk'=4,'dp'=2,'head'=4] {'blk','dp'}, dimensions={1}, use_global_device_ids=true | all-gather | bytes 82944 | tf_op jit(solution)/shard_map/while/body/eval_jaxpr/all_gather | solution.py:273
  953.8 14.3 all_gather.99
  969.3 6.9 all_gather.100
  976.7 33.2 %all_gather.97 = bf16[768,192]{1,0:T(8,128)(2,1)} all-gather(bf16[96,192]{1,0:T(8,128)(2,1)S(1)} %copy-done.37), channel_id=1, replica_groups=mesh['blk'=4,'dp'=2,'head'=4] {'blk','dp'}, dimensions={0}, use_global_device_ids=true | all-gather | bytes 331776 | tf_op jit(solution)/shard_map/while/body/eval_jaxpr/all_gather | solution.py:274
  1011.1 32.9 %all_gather.101 = bf16[1,192,768]{2,1,0:T(8,128)(2,1)} all-gather(bf16[1,24,768]{2,1,0:T(8,128)(2,1)S(1)} %copy-done.39), channel_id=1, replica_groups=mesh['blk'=4,'dp'=2,'head'=4] {'blk','dp'}, dimensions={1}, use_global_device_ids=true | all-gather | bytes 331776 | tf_op jit(solution)/shard_map/while/body/eval_jaxpr/all_gather | solution.py:275
  1044.5 33.2 %all_gather.102 = bf16[1,768,192]{2,1,0:T(8,128)(2,1)} all-gather(bf16[1,96,192]{2,1,0:T(8,128)(2,1)S(1)} %copy-done.38), channel_id=1, replica_groups=mesh['blk'=4,'dp'=2,'head'=4] {'blk','dp'}, dimensions={1}, use_global_device_ids=true | all-gather | bytes 331776 | tf_op jit(solution)/shard_map/while/body/eval_jaxpr/all_gather | solution.py:276
  1094.3 6.5 all-reduce.40
  1113.4 6.2 all-reduce.42
  1124.5 15.4 all_gather.103
  1140.7 13.1 all_gather.106
  1157.0 14.8 all_gather.104
  1177.9 13.1 all_gather.105
  1216.4 17.7 %all-reduce.43 = (f32[1,192]{1,0:T(1,128)S(1)}, f32[1,192]{1,0:T(1,128)S(1)}, f32[1,192]{1,0:T(1,128)S(1)}, f32[1,192]{1,0:T(1,128)S(1)}, f32[1,192]{1,0:T(1,128...) all-reduce(f32[1,192]{1,0:T(1,128)S(1)} %broadcast_in_dim.333, ...), channel_id=9, replica_groups=mesh['blk'=4,'dp'=2,'head'=4] {'blk','dp'}, use_global_device_ids=true, to_apply=%region_31.31.clone | all-reduce | flops 1536 | bytes 12288 | tf_op jit(solution)/shard_map/while
  1234.5 35.2 %reduce-scatter.31.cloned.1.call-done = f32[1,24,192]{2,1,0:T(8,128)} async-done(((f32[1,192,192]{2,1,0:T(8,128)}), f32[1,24,192]{2,1,0:T(8,128)}) %reduce-scatter.31.cloned.1.call-update) | async-done | bytes 18448 | tf_op jit(solution)/shard_map/while/body/eval_jaxpr/reduce_scatter | solution.py:291
  1270.5 62.5 %reduce-scatter.29.cloned.1.call-done = f32[1,24,192]{2,1,0:T(8,128)} async-done(((f32[1,192,192]{2,1,0:T(8,128)}), f32[1,24,192]{2,1,0:T(8,128)}) %reduce-scatter.29.cloned.1.call-update) | async-done | bytes 18448 | tf_op jit(solution)/shard_map/while/body/eval_jaxpr/reduce_scatter | solution.py:290
  1333.7 63.2 %reduce-scatter.27.cloned.1.call-done = f32[1,24,192]{2,1,0:T(8,128)} async-done(((f32[1,192,192]{2,1,0:T(8,128)}), f32[1,24,192]{2,1,0:T(8,128)}) %reduce-scatter.27.cloned.1.call-update) | async-done | bytes 18448 | tf_op jit(solution)/shard_map/while/body/eval_jaxpr/reduce_scatter | solution.py:289
  1397.7 63.9 %reduce-scatter.37.cloned.1.call-done = f32[96,192]{1,0:T(8,128)} async-done(((f32[768,192]{1,0:T(8,128)}), f32[96,192]{1,0:T(8,128)}) %reduce-scatter.37.cloned.1.call-update) | async-done | bytes 73744 | tf_op jit(solution)/shard_map/while
  1462.6 63.6 %reduce-scatter.35.cloned.1.call-done = f32[1,24,768]{2,1,0:T(8,128)} async-done(((f32[1,192,768]{2,1,0:T(8,128)}), f32[1,24,768]{2,1,0:T(8,128)}) %reduce-scatter.35.cloned.1.call-update) | async-done | bytes 73744 | tf_op jit(solution)/shard_map/while/body/eval_jaxpr/reduce_scatter | solution.py:293
  1527.2 63.9 %reduce-scatter.33.cloned.1.call-done = f32[96,192]{1,0:T(8,128)} async-done(((f32[768,192]{1,0:T(8,128)}), f32[96,192]{1,0:T(8,128)}) %reduce-scatter.33.cloned.1.call-update) | async-done | bytes 73744 | tf_op jit(solution)/shard_map/while/body/eval_jaxpr/reduce_scatter | solution.py:292
  (558 shorter events, 200.7 us)
Async XLA Ops:
  7.4 358.8 %reduce-scatter.25.cloned.1.call-start = ((), (), s32[]{:S(2)}) async-start(), calls=%async_computation.8 | async-start | bytes 491520 | tf_op jit(solution)/shard_map/while/body/eval_jaxpr/reduce_scatter | solution.py:144
  332.5 88.5 %reduce-scatter.39.cloned.1.call-start = ((), (), s32[]{:S(2)}) async-start(), calls=%async_computation.15 | async-start | bytes 442368 | tf_op jit(solution)/shard_map/while
  333.5 145.5 %reduce-scatter.31.cloned.1.call-start = ((), (), s32[]{:S(2)}) async-start(), calls=%async_computation.11 | async-start | bytes 221184 | tf_op jit(solution)/shard_map/while/body/eval_jaxpr/reduce_scatter | solution.py:291
  400.3 142.0 %reduce-scatter.29.cloned.1.call-start = ((), (), s32[]{:S(2)}) async-start(), calls=%async_computation.10 | async-start | bytes 221184 | tf_op jit(solution)/shard_map/while/body/eval_jaxpr/reduce_scatter | solution.py:290
  406.4 199.6 %reduce-scatter.27.cloned.1.call-start = ((), (), s32[]{:S(2)}) async-start(), calls=%async_computation.9 | async-start | bytes 221184 | tf_op jit(solution)/shard_map/while/body/eval_jaxpr/reduce_scatter | solution.py:289
  411.7 259.0 %reduce-scatter.37.cloned.1.call-start = ((), (), s32[]{:S(2)}) async-start(), calls=%async_computation.14 | async-start | bytes 884736 | tf_op jit(solution)/shard_map/while
  414.2 321.2 %reduce-scatter.35.cloned.1.call-start = ((), (), s32[]{:S(2)}) async-start(), calls=%async_computation.13 | async-start | bytes 663552 | tf_op jit(solution)/shard_map/while/body/eval_jaxpr/reduce_scatter | solution.py:293
  416.8 383.6 %reduce-scatter.33.cloned.1.call-start = ((), (), s32[]{:S(2)}) async-start(), calls=%async_computation.12 | async-start | bytes 884736 | tf_op jit(solution)/shard_map/while/body/eval_jaxpr/reduce_scatter | solution.py:292
  418.0 317.5 %copy-start.35 = (f32[1,24,768]{2,1,0:T(8,128)S(1)}, f32[1,24,768]{2,1,0:T(8,128)}, u32[]{:S(2)}) copy-start(f32[1,24,768]{2,1,0:T(8,128)} %get-tuple-element.966) | copy-start | bytes 221188 | tf_op jit(solution)/shard_map/while
  418.0 318.4 %copy-start.31 = (f32[1,96,192]{1,2,0:T(8,128)S(1)}, f32[1,96,192]{1,2,0:T(8,128)}, u32[]{:S(2)}) copy-start(f32[1,96,192]{1,2,0:T(8,128)} %get-tuple-element.967) | copy-start | bytes 221188 | tf_op jit(solution)/shard_map/while
  418.0 382.3 %copy-start.33 = (f32[96,192]{1,0:T(8,128)S(1)}, f32[96,192]{1,0:T(8,128)}, u32[]{:S(2)}) copy-start(f32[96,192]{1,0:T(8,128)} %get-tuple-element.965) | copy-start | bytes 221188 | tf_op jit(solution)/shard_map/while
  421.0 380.3 %copy-start.73 = (bf16[2,49152]{1,0:T(2,128)(2,1)}, bf16[2,49152]{1,0:T(2,128)(2,1)S(1)}, u32[]{:S(2)}) copy-start(bf16[2,49152]{1,0:T(2,128)(2,1)S(1)} %dynamic_update_slice.12) | copy-start | bytes 589828 | tf_op jit(solution)/shard_map/while
  422.0 379.3 %copy-start.55 = (f32[1,96]{1,0:T(1,128)}, f32[1,96]{1,0:T(1,128)S(1)}, u32[]{:S(2)}) copy-start(f32[1,96]{1,0:T(1,128)S(1)} %fusion.227) | copy-start | bytes 1156 | tf_op jit(solution)/shard_map/while
  425.5 375.8 %copy-start.47 = (f32[2,49152]{1,0:T(2,128)}, f32[2,49152]{1,0:T(2,128)S(1)}, u32[]{:S(2)}) copy-start(f32[2,49152]{1,0:T(2,128)S(1)} %dynamic_update_slice.13) | copy-start | bytes 1179652 | tf_op jit(solution)/shard_map/while
  443.1 358.2 %copy-start.61 = (f32[1,24]{1,0:T(1,128)}, f32[1,24]{1,0:T(1,128)S(1)}, u32[]{:S(2)}) copy-start(f32[1,24]{1,0:T(1,128)S(1)} %get-tuple-element.1023) | copy-start | bytes 292 | tf_op jit(solution)/shard_map/while
  443.1 358.2 %copy-start.63 = (f32[1,24]{1,0:T(1,128)}, f32[1,24]{1,0:T(1,128)S(1)}, u32[]{:S(2)}) copy-start(f32[1,24]{1,0:T(1,128)S(1)} %get-tuple-element.1024) | copy-start | bytes 292 | tf_op jit(solution)/shard_map/while
  443.2 358.1 %copy-start.57 = (f32[1,24]{1,0:T(1,128)}, f32[1,24]{1,0:T(1,128)S(1)}, u32[]{:S(2)}) copy-start(f32[1,24]{1,0:T(1,128)S(1)} %get-tuple-element.1020) | copy-start | bytes 292 | tf_op jit(solution)/shard_map/while
  443.2 358.1 %copy-start.59 = (f32[1,24]{1,0:T(1,128)}, f32[1,24]{1,0:T(1,128)S(1)}, u32[]{:S(2)}) copy-start(f32[1,24]{1,0:T(1,128)S(1)} %get-tuple-element.1022) | copy-start | bytes 292 | tf_op jit(solution)/shard_map/while
  443.4 358.0 %copy-start.69 = (f32[1,24]{1,0:T(1,128)}, f32[1,24]{1,0:T(1,128)S(1)}, u32[]{:S(2)}) copy-start(f32[1,24]{1,0:T(1,128)S(1)} %get-tuple-element.1018) | copy-start | bytes 292 | tf_op jit(solution)/shard_map/while
  443.4 358.0 %copy-start.71 = (f32[1,24]{1,0:T(1,128)}, f32[1,24]{1,0:T(1,128)S(1)}, u32[]{:S(2)}) copy-start(f32[1,24]{1,0:T(1,128)S(1)} %get-tuple-element.1019) | copy-start | bytes 292 | tf_op jit(solution)/shard_map/while
  443.5 357.9 %copy-start.65 = (f32[1,24]{1,0:T(1,128)}, f32[1,24]{1,0:T(1,128)S(1)}, u32[]{:S(2)}) copy-start(f32[1,24]{1,0:T(1,128)S(1)} %get-tuple-element.1016) | copy-start | bytes 292 | tf_op jit(solution)/shard_map/while
  443.5 357.9 %copy-start.67 = (f32[1,24]{1,0:T(1,128)}, f32[1,24]{1,0:T(1,128)S(1)}, u32[]{:S(2)}) copy-start(f32[1,24]{1,0:T(1,128)S(1)} %get-tuple-element.1017) | copy-start | bytes 292 | tf_op jit(solution)/shard_map/while
  479.8 321.6 %copy-start.45 = (f32[1,24,192]{2,1,0:T(8,128)}, f32[1,24,192]{2,1,0:T(8,128)S(1)}, u32[]{:S(2)}) copy-start(f32[1,24,192]{2,1,0:T(8,128)S(1)} %select_add_fusion.14) | copy-start | bytes 55300 | tf_op jit(solution)/shard_map/while
  543.0 258.4 %copy-start.43 = (f32[1,24,192]{2,1,0:T(8,128)}, f32[1,24,192]{2,1,0:T(8,128)S(1)}, u32[]{:S(2)}) copy-start(f32[1,24,192]{2,1,0:T(8,128)S(1)} %select_add_fusion.13) | copy-start | bytes 55300 | tf_op jit(solution)/shard_map/while
  801.9 355.1 %reduce-scatter.25.cloned.1.call-start = ((), (), s32[]{:S(2)}) async-start(), calls=%async_computation.8 | async-start | bytes 491520 | tf_op jit(solution)/shard_map/while/body/eval_jaxpr/reduce_scatter | solution.py:144
  1123.4 88.5 %reduce-scatter.39.cloned.1.call-start = ((), (), s32[]{:S(2)}) async-start(), calls=%async_computation.15 | async-start | bytes 442368 | tf_op jit(solution)/shard_map/while
  1124.4 145.3 %reduce-scatter.31.cloned.1.call-start = ((), (), s32[]{:S(2)}) async-start(), calls=%async_computation.11 | async-start | bytes 221184 | tf_op jit(solution)/shard_map/while/body/eval_jaxpr/reduce_scatter | solution.py:291
  1191.1 141.9 %reduce-scatter.29.cloned.1.call-start = ((), (), s32[]{:S(2)}) async-start(), calls=%async_computation.10 | async-start | bytes 221184 | tf_op jit(solution)/shard_map/while/body/eval_jaxpr/reduce_scatter | solution.py:290
  1197.2 199.7 %reduce-scatter.27.cloned.1.call-start = ((), (), s32[]{:S(2)}) async-start(), calls=%async_computation.9 | async-start | bytes 221184 | tf_op jit(solution)/shard_map/while/body/eval_jaxpr/reduce_scatter | solution.py:289
  1202.6 259.0 %reduce-scatter.37.cloned.1.call-start = ((), (), s32[]{:S(2)}) async-start(), calls=%async_computation.14 | async-start | bytes 884736 | tf_op jit(solution)/shard_map/while
  1205.1 321.1 %reduce-scatter.35.cloned.1.call-start = ((), (), s32[]{:S(2)}) async-start(), calls=%async_computation.13 | async-start | bytes 663552 | tf_op jit(solution)/shard_map/while/body/eval_jaxpr/reduce_scatter | solution.py:293
  1207.6 383.5 %reduce-scatter.33.cloned.1.call-start = ((), (), s32[]{:S(2)}) async-start(), calls=%async_computation.12 | async-start | bytes 884736 | tf_op jit(solution)/shard_map/while/body/eval_jaxpr/reduce_scatter | solution.py:292
  1208.9 317.4 %copy-start.35 = (f32[1,24,768]{2,1,0:T(8,128)S(1)}, f32[1,24,768]{2,1,0:T(8,128)}, u32[]{:S(2)}) copy-start(f32[1,24,768]{2,1,0:T(8,128)} %get-tuple-element.966) | copy-start | bytes 221188 | tf_op jit(solution)/shard_map/while
  1208.9 318.3 %copy-start.31 = (f32[1,96,192]{1,2,0:T(8,128)S(1)}, f32[1,96,192]{1,2,0:T(8,128)}, u32[]{:S(2)}) copy-start(f32[1,96,192]{1,2,0:T(8,128)} %get-tuple-element.967) | copy-start | bytes 221188 | tf_op jit(solution)/shard_map/while
  1208.9 382.2 %copy-start.33 = (f32[96,192]{1,0:T(8,128)S(1)}, f32[96,192]{1,0:T(8,128)}, u32[]{:S(2)}) copy-start(f32[96,192]{1,0:T(8,128)} %get-tuple-element.965) | copy-start | bytes 221188 | tf_op jit(solution)/shard_map/while
  1211.8 380.2 %copy-start.73 = (bf16[2,49152]{1,0:T(2,128)(2,1)}, bf16[2,49152]{1,0:T(2,128)(2,1)S(1)}, u32[]{:S(2)}) copy-start(bf16[2,49152]{1,0:T(2,128)(2,1)S(1)} %dynamic_update_slice.12) | copy-start | bytes 589828 | tf_op jit(solution)/shard_map/while
  1212.8 379.2 %copy-start.55 = (f32[1,96]{1,0:T(1,128)}, f32[1,96]{1,0:T(1,128)S(1)}, u32[]{:S(2)}) copy-start(f32[1,96]{1,0:T(1,128)S(1)} %fusion.227) | copy-start | bytes 1156 | tf_op jit(solution)/shard_map/while
  1216.3 375.7 %copy-start.47 = (f32[2,49152]{1,0:T(2,128)}, f32[2,49152]{1,0:T(2,128)S(1)}, u32[]{:S(2)}) copy-start(f32[2,49152]{1,0:T(2,128)S(1)} %dynamic_update_slice.13) | copy-start | bytes 1179652 | tf_op jit(solution)/shard_map/while
  1234.2 357.8 %copy-start.61 = (f32[1,24]{1,0:T(1,128)}, f32[1,24]{1,0:T(1,128)S(1)}, u32[]{:S(2)}) copy-start(f32[1,24]{1,0:T(1,128)S(1)} %get-tuple-element.1023) | copy-start | bytes 292 | tf_op jit(solution)/shard_map/while
  1234.2 357.9 %copy-start.63 = (f32[1,24]{1,0:T(1,128)}, f32[1,24]{1,0:T(1,128)S(1)}, u32[]{:S(2)}) copy-start(f32[1,24]{1,0:T(1,128)S(1)} %get-tuple-element.1024) | copy-start | bytes 292 | tf_op jit(solution)/shard_map/while
  1234.3 357.8 %copy-start.57 = (f32[1,24]{1,0:T(1,128)}, f32[1,24]{1,0:T(1,128)S(1)}, u32[]{:S(2)}) copy-start(f32[1,24]{1,0:T(1,128)S(1)} %get-tuple-element.1020) | copy-start | bytes 292 | tf_op jit(solution)/shard_map/while
  1234.3 357.8 %copy-start.59 = (f32[1,24]{1,0:T(1,128)}, f32[1,24]{1,0:T(1,128)S(1)}, u32[]{:S(2)}) copy-start(f32[1,24]{1,0:T(1,128)S(1)} %get-tuple-element.1022) | copy-start | bytes 292 | tf_op jit(solution)/shard_map/while
  1234.4 357.7 %copy-start.69 = (f32[1,24]{1,0:T(1,128)}, f32[1,24]{1,0:T(1,128)S(1)}, u32[]{:S(2)}) copy-start(f32[1,24]{1,0:T(1,128)S(1)} %get-tuple-element.1018) | copy-start | bytes 292 | tf_op jit(solution)/shard_map/while
  1234.4 357.7 %copy-start.71 = (f32[1,24]{1,0:T(1,128)}, f32[1,24]{1,0:T(1,128)S(1)}, u32[]{:S(2)}) copy-start(f32[1,24]{1,0:T(1,128)S(1)} %get-tuple-element.1019) | copy-start | bytes 292 | tf_op jit(solution)/shard_map/while
  1234.5 357.6 %copy-start.65 = (f32[1,24]{1,0:T(1,128)}, f32[1,24]{1,0:T(1,128)S(1)}, u32[]{:S(2)}) copy-start(f32[1,24]{1,0:T(1,128)S(1)} %get-tuple-element.1016) | copy-start | bytes 292 | tf_op jit(solution)/shard_map/while
  1234.5 357.6 %copy-start.67 = (f32[1,24]{1,0:T(1,128)}, f32[1,24]{1,0:T(1,128)S(1)}, u32[]{:S(2)}) copy-start(f32[1,24]{1,0:T(1,128)S(1)} %get-tuple-element.1017) | copy-start | bytes 292 | tf_op jit(solution)/shard_map/while
  1270.5 321.6 %copy-start.45 = (f32[1,24,192]{2,1,0:T(8,128)}, f32[1,24,192]{2,1,0:T(8,128)S(1)}, u32[]{:S(2)}) copy-start(f32[1,24,192]{2,1,0:T(8,128)S(1)} %select_add_fusion.14) | copy-start | bytes 55300 | tf_op jit(solution)/shard_map/while
  1333.7 258.4 %copy-start.43 = (f32[1,24,192]{2,1,0:T(8,128)}, f32[1,24,192]{2,1,0:T(8,128)S(1)}, u32[]{:S(2)}) copy-start(f32[1,24,192]{2,1,0:T(8,128)S(1)} %select_add_fusion.13) | copy-start | bytes 55300 | tf_op jit(solution)/shard_map/while
  (118 other events, 3181.5 us)
Sparse Core Ops, SparseCore 0:
  332.6 17.7 reduce-scatter.24
  354.0 61.4 reduce-scatter.38
  418.8 60.1 reduce-scatter.30
  482.1 60.0 reduce-scatter.28
  545.9 60.0 reduce-scatter.26
  609.2 61.4 reduce-scatter.36
  674.4 61.0 reduce-scatter.34
  738.8 61.5 reduce-scatter.32
  1123.5 17.7 reduce-scatter.24
  1144.8 61.4 reduce-scatter.38
  1209.5 60.1 reduce-scatter.30
  1272.8 60.0 reduce-scatter.28
  1336.8 60.0 reduce-scatter.26
  1400.1 61.4 reduce-scatter.36
  1465.1 61.1 reduce-scatter.34
  1529.4 61.6 reduce-scatter.32
where the time goes:
time: 1610 us; the launch traced here: 1600 us
  waiting for transfers between devices  705 us (44%)
  blocking collectives  694 us (43%)
  matrix products  78.7 us (5%)
  local copies, waits for them, and re-layouts  71.2 us (4%)
  other arithmetic  32.9 us (2%)
    while x20, waiting for transfers between devices  128 us
    reduce_scatter x2, waiting for transfers between devices, step(): lax.psum_scatter(grads[3], ('blk', 'dp'), scatter_dimension=0, tiled=True)  128 us
    reduce_scatter x2, waiting for transfers between devices, step(): lax.psum_scatter(grads[4], ('blk', 'dp'), scatter_dimension=1, tiled=True)  127 us
    reduce_scatter x2, waiting for transfers between devices, step(): lax.psum_scatter(grads[0], ('blk', 'dp'), scatter_dimension=1, tiled=True)  126 us
    reduce_scatter x2, waiting for transfers between devices, step(): lax.psum_scatter(grads[1], ('blk', 'dp'), scatter_dimension=1, tiled=True)  125 us
    while x4, blocking collectives  79.5 us
    reduce_scatter x2, waiting for transfers between devices, step(): lax.psum_scatter(grads[2], ('blk', 'dp'), scatter_dimension=1, tiled=True)  70.8 us
    all_gather x2, blocking collectives, step(): lax.all_gather(down_weight, ('blk', 'dp'), axis=1, tiled=True)  66.4 us
  transfers between devices with their start and end apart: 16, of which 12 were waited for; matrix products, arithmetic and copies ran while one was open for 5% of the time, Pallas kernels for 0%

commit v1 on v0

v1 whole, which is shorter than its diff:
```python
import types

import jax
import jax.numpy as jnp
from jax import lax
from jax.experimental import pallas as pl
from jax.experimental.pallas import tpu as pltpu
from jax.sharding import PartitionSpec as P

HEAD_DIM = 64
EPS = 1e-05
BIG = 1e30
MESH = pl.DeviceIdType.MESH
F32 = jnp.float32
BF16 = jnp.bfloat16
V_BQ, V_BV, V_BO, V_G1, V_S1, V_BD, V_G2, V_S2, V_BU = range(9)
VROWS = 16


def up_to(n, m):
    return (n + m - 1) // m * m


def mm(a, b):
    return lax.dot_general(a, b, (((1,), (0,)), ((), ())), preferred_element_type=F32)


def mm_nt(a, b):
    return lax.dot_general(a, b, (((1,), (1,)), ((), ())), preferred_element_type=F32)


def loop(n, fn):
    if n <= 8:
        for i in range(n):
            fn(i)
    else:
        lax.fori_loop(0, n, lambda i, c: (fn(i), c)[1], 0)


def rcopy(src, dst, ss, rs, dev):
    return pltpu.make_async_remote_copy(
        src_ref=src, dst_ref=dst, send_sem=ss, recv_sem=rs, device_id=dev, device_id_type=MESH
    )


class Sizes:
    def __init__(self, mesh, tokens, query_weight, up_weight, doc_lengths):
        self.nb, self.nd, self.nh = mesh.shape["blk"], mesh.shape["dp"], mesh.shape["head"]
        self.W = self.nb * self.nd
        self.C, self.F = query_weight.shape[2], up_weight.shape[2]
        self.MB = tokens.shape[0]
        self.R = tokens.shape[3] // self.C
        self.S = self.nb // self.MB
        self.tb = self.nb // (self.MB * self.nd)
        self.Q = self.MB * self.R
        self.H = self.C // HEAD_DIM
        self.ND = doc_lengths.shape[2]
        self.r = query_weight.shape[1]
        self.rs = up_to(self.r, 8)
        self.rA = up_to(2 * self.rs, 16)
        self.rC = up_to(4 * self.r, 16)
        self.L = 2 * self.C
        self.XR = self.C + 16
        self.keep = self.nb * self.R * self.Q * self.H * 2 <= (8 << 20)
        assert self.F == 4 * self.C and self.F == self.nh * self.C


def main_scratch(z):
    dma = pltpu.SemaphoreType.DMA
    v = pltpu.VMEM
    nb, W, L, R, C, F, Q, H = z.nb, z.W, z.L, z.R, z.C, z.F, z.Q, z.H
    dd = max(z.nd - 1, 1)
    return dict(
        xs=v((z.MB, z.XR, R), BF16),
        xb=v((nb, z.XR, R), BF16),
        cs=v((z.MB, C, R), BF16),
        cb=v((z.MB, C, R), BF16),
        bufA=v((W, z.rA, L), BF16),
        bufB=v((W, z.rA, L), BF16),
        bufC=v((W, z.rC, L), BF16),
        bufV=v((W, VROWS, 128), BF16),
        fst=v((max(z.rA, z.rC), L), F32),
        vst=v((VROWS, 128), F32),
        fkv=v((C + 8, L), F32),
        fq=v((C + 8, L), F32),
        fup=v((C + 8, F), F32),
        fod=v((F + 16, L), F32),
        vcol=v((C + 8, 16), F32),
        ucol=v((F + 16, 16), F32),
        wkv=v((C, L), BF16),
        wkvt=v((L, C), BF16),
        wq=v((C, C), BF16),
        wqt=v((C, C), BF16),
        wup=v((C, F), BF16),
        wupt=v((F, C), BF16),
        wo=v((z.nh, C, C), BF16),
        wor=v((z.nh, C, C), BF16),
        wot=v((C, F), BF16),
        wdn=v((F, C), BF16),
        wdnt=v((C, F), BF16),
        xq=v((C, Q), BF16),
        qx=v((H, 128, Q), BF16),
        qt=v((H, Q, 128), BF16),
        kx=v((nb, H, HEAD_DIM, R), BF16),
        vx=v((nb, H, HEAD_DIM + 16, R), BF16),
        kt=v((nb, H, R, 128), BF16),
        vt=v((nb, H, R, 128), BF16),
        sbuf=v((nb if z.keep else 1, R, Q), F32),
        pbuf=v((H, nb if z.keep else 1, R, Q), BF16),
        mrow=v((H, 8, Q), F32),
        oall=v((z.nh, C, Q), BF16),
        pall=v((z.nh, C, Q), BF16),
        stats=v((3, z.nh, 8, Q), F32),
        u=v((F, Q), F32),
        act=v((F, Q), BF16),
        du=v((F, Q), BF16),
        mo=v((z.MB, C, R), BF16),
        dox=v((H, 128, Q), BF16),
        dot=v((H, Q, 128), BF16),
        dqacc=v((H, HEAD_DIM, Q), F32),
        dkv=v((L, R), BF16),
        dq=v((C, Q), BF16),
        tgs=v((nb, C, R), BF16),
        gkv=v((C + 8, L), F32),
        gq=v((C + 8, L), F32),
        gup=v((C + 8, F), F32),
        god=v((F + 16, L), F32),
        vg=v((VROWS, C), F32),
        vgu=v((VROWS, F), F32),
        pA=v((W, z.rA, L), BF16),
        pB=v((W, z.rA, L), BF16),
        pC=v((W, z.rC, L), BF16),
        pV=v((W, VROWS, 128), BF16),
        r1A=v((dd, nb, z.rA, L), BF16),
        r1B=v((dd, nb, z.rA, L), BF16),
        r1C=v((dd, nb, z.rC, L), BF16),
        r1V=v((dd, nb, VROWS, 128), BF16),
        s2A=v((nb, z.rA, L), BF16),
        s2B=v((nb, z.rA, L), BF16),
        s2C=v((nb, z.rC, L), BF16),
        s2V=v((nb, VROWS, 128), BF16),
        r2A=v((nb, z.rA, L), BF16),
        r2B=v((nb, z.rA, L), BF16),
        r2C=v((nb, z.rC, L), BF16),
        r2V=v((nb, VROWS, 128), BF16),
        x_ss=dma((z.MB * z.S,)),
        x_rs=dma((nb,)),
        c_ss=dma((z.MB,)),
        c_rs=dma((z.MB,)),
        g1_ss=dma((4, nb)),
        g1_rs=dma((4, nb)),
        g2_ss=dma((4, dd, nb)),
        g2_rs=dma((4, dd, nb)),
        o_ss=dma((z.nh, H)),
        o_rs=dma((z.nh, H)),
        w_ss=dma((z.nh,)),
        w_rs=dma((z.nh,)),
        st_ss=dma((3, z.nh)),
        st_rs=dma((3, z.nh)),
        p_ss=dma((z.nh,)),
        p_rs=dma((z.nh,)),
        mo_ss=dma((z.MB,)),
        mo_rs=dma((z.MB,)),
        t_ss=dma((nb,)),
        t_rs=dma((z.MB * z.S,)),
        s1_ss=dma((4, dd, nb)),
        s1_rs=dma((4, dd, nb)),
        s2_ss=dma((4, nb)),
        s2_rs=dma((4, nb)),
    )


INPUTS = [
    "lens", "tok", "cot", "wq_in", "bq", "wk_in", "wv_in", "bv", "wo_in", "bo", "g1", "s1", "wup_in", "bu",
    "wdn_in", "bd", "g2", "s2",
]
OUTPUTS = ["o_mo", "o_tg", "o_A", "o_B", "o_C", "o_V"]


def main_kernel(z, names, *refs):
    k = types.SimpleNamespace(**dict(zip(names, refs)))
    nb, nd, nh, W, MB, R, C, F, Q, H, L, S = (
        z.nb, z.nd, z.nh, z.W, z.MB, z.R, z.C, z.F, z.Q, z.H, z.L, z.S,
    )
    b, d, h = lax.axis_index("blk"), lax.axis_index("dp"), lax.axis_index("head")
    w_me = b * nd + d
    team = b // z.tb
    m_t, d_t = team // nd, team % nd
    s_me = (b - team * z.tb) * nd + d
    D = nh * C
    hpeer = [lax.rem(h + i, nh) for i in range(nh)]
    hsrc = [lax.rem(h + nh - i, nh) for i in range(nh)]

    bar = pltpu.get_barrier_semaphore()
    for i in range(1, W):
        w = lax.rem(w_me + i, W)
        pl.semaphore_signal(bar, inc=1, device_id=(w // nd, w % nd, h), device_id_type=MESH)
    for i in range(1, nh):
        pl.semaphore_signal(bar, inc=1, device_id=(b, d, hpeer[i]), device_id_type=MESH)

    k.fst[...] = jnp.zeros_like(k.fst)
    k.fst[0 : z.r, 0:C] = k.wk_in[0].astype(F32)
    k.fst[0 : z.r, C:L] = k.wv_in[0].astype(F32)
    k.fst[z.rs : z.rs + z.r, 0:C] = k.wq_in[0].astype(F32)
    k.bufA[w_me] = k.fst[0 : z.rA].astype(BF16)
    k.fst[0 : z.r] = k.wup_in[0, :, 0:L].astype(F32)
    k.fst[z.rs : z.rs + z.r] = k.wup_in[0, :, L : 2 * L].astype(F32)
    k.bufB[w_me] = k.fst[0 : z.rA].astype(BF16)
    k.fst[0 : 4 * z.r, 0:C] = k.wo_in[...].astype(F32)
    k.fst[0 : 4 * z.r, C:L] = k.wdn_in[0].astype(F32)
    k.bufC[w_me] = k.fst[0 : z.rC].astype(BF16)
    k.vst[...] = jnp.zeros_like(k.vst)
    for j, ref in enumerate((k.bq, k.bv, k.bo, k.g1, k.s1, k.bd, k.g2, k.s2)):
        k.vst[j : j + 1, 0 : z.r] = ref[...].astype(F32)
    k.vst[V_BU : V_BU + 1, 0 : 4 * z.r] = k.bu[...].astype(F32)
    k.bufV[w_me] = k.vst[...].astype(BF16)

    pos = b * R + lax.broadcasted_iota(jnp.int32, (16, R), 1)
    row16 = lax.broadcasted_iota(jnp.int32, (16, R), 0)
    for m in range(MB):
        doc = jnp.zeros((16, R), jnp.int32)
        end = k.lens[m, 0, 0]
        for j in range(z.ND):
            if j > 0:
                end = end + k.lens[m, 0, j]
            doc = doc + (pos >= end).astype(jnp.int32)
        onehot = jnp.where(row16 == doc, 1.0, 0.0).astype(BF16)
        k.xs[m, 0:C] = k.tok[m].T
        k.xs[m, C : z.XR] = onehot
        k.cs[m] = k.cot[m].T

    pl.semaphore_wait(bar, W - 1 + nh - 1)

    def member(m, s):
        return (m * nd + d) * z.tb + s // nd, s % nd

    def x_send(m, s):
        bt, dt = member(m, s)
        return rcopy(k.xs.at[m], k.xb.at[b], k.x_ss.at[m * S + s], k.x_rs.at[b], (bt, dt, h))

    def not_me(pos):
        return jnp.logical_or(pos[0] != b, pos[1] != d)

    def is_me(pos):
        return jnp.logical_and(pos[0] == b, pos[1] == d)

    def start_x(i):
        m, s = i // S, i % S

        @pl.when(not_me(member(m, s)))
        def _():
            x_send(m, s).start()

        @pl.when(is_me(member(m, s)))
        def _():
            k.xb[b] = k.xs[m]

    loop(MB * S, start_x)

    bufs = (k.bufA, k.bufV, k.bufB, k.bufC)

    def g1(q, i):
        bt = lax.rem(b + i, nb)
        return rcopy(bufs[q].at[w_me], bufs[q].at[w_me], k.g1_ss.at[q, i], k.g1_rs.at[q, i], (bt, d, h))

    def g1_wait(q, i):
        src = lax.rem(b + nb - i, nb) * nd + d
        rcopy(bufs[q].at[src], bufs[q].at[src], k.g1_ss.at[q, i], k.g1_rs.at[q, i], (b, d, h)).wait_recv()

    def g2(q, e, i):
        src = lax.rem(b + nb - i, nb) * nd + d
        dt = lax.rem(d + e, nd)
        return rcopy(
            bufs[q].at[src], bufs[q].at[src], k.g2_ss.at[q, e - 1, i], k.g2_rs.at[q, e - 1, i], (b, dt, h)
        )

    def g2_wait(q, e, i):
        src = lax.rem(b + nb - i, nb) * nd + lax.rem(d + nd - e, nd)
        rcopy(
            bufs[q].at[src], bufs[q].at[src], k.g2_ss.at[q, e - 1, i], k.g2_rs.at[q, e - 1, i], (b, d, h)
        ).wait_recv()

    def gather_start(q):
        for e in range(1, nd):
            g2(q, e, 0).start()
        loop(nb - 1, lambda i: g1(q, i + 1).start())

    def gather_forward(q):
        def one(i):
            g1_wait(q, i + 1)
            for e in range(1, nd):
                g2(q, e, i + 1).start()

        loop(nb - 1, one)

    def gather_wait(q):
        for e in range(1, nd):
            loop(nb, lambda i: g2_wait(q, e, i))

    def gather_drain(q):
        loop(nb - 1, lambda i: g1(q, i + 1).wait_send())
        for e in range(1, nd):
            loop(nb, lambda i: g2(q, e, i).wait_send())

    gather_start(0)
    gather_start(1)

    own_s = b // MB

    def c_send(m):
        return rcopy(
            k.cs.at[m], k.cb.at[b % MB], k.c_ss.at[m], k.c_rs.at[b % MB], (*member(m, own_s), h)
        )

    for m in range(MB):

        @pl.when(not_me(member(m, own_s)))
        def _():
            c_send(m).start()

        @pl.when(is_me(member(m, own_s)))
        def _():
            k.cb[b % MB] = k.cs[m]

    gather_start(2)
    gather_start(3)
    gather_forward(0)
    gather_forward(1)
    gather_wait(0)
    gather_wait(1)

    for w in range(W):
        slab = k.bufA[w].astype(F32)
        k.fkv[w * z.r : w * z.r + z.rs] = slab[0 : z.rs]
        k.fq[w * z.r : w * z.r + z.rs] = slab[z.rs : 2 * z.rs]
    k.wkv[...] = k.fkv[0:C].astype(BF16)
    k.wkvt[...] = k.fkv[0:C].T.astype(BF16)
    k.wq[...] = k.fq[0:C, 0:C].astype(BF16)
    k.wqt[...] = k.fq[0:C, 0:C].T.astype(BF16)
    eye = (
        lax.broadcasted_iota(jnp.int32, (128, 128), 0) == lax.broadcasted_iota(jnp.int32, (128, 128), 1)
    ).astype(F32).astype(BF16)
    for w in range(W):
        col = mm_nt(eye, k.bufV[w])
        k.vcol[w * z.r : w * z.r + z.rs] = col[0 : z.rs]
        k.ucol[w * 4 * z.r : w * 4 * z.r + z.rC] = col[0 : z.rC]

    def vec(j):
        return k.vcol[0:C, j : j + 1]

    x_src_self = d == d_t
    feat_row = lax.broadcasted_iota(jnp.int32, (16, R), 0)

    def x_wait(j):
        @pl.when(jnp.logical_not(jnp.logical_and(x_src_self, j == b)))
        def _():
            rcopy(k.xb.at[j], k.xb.at[j], k.x_ss.at[0], k.x_rs.at[j], (b, d, h)).wait_recv()

    one_rows = jnp.where(feat_row < 2, 1.0, 0.0).astype(BF16)

    def kv_block(j):
        x_wait(j)
        kv = mm(k.wkvt[...], k.xb[j, 0:C])
        kb = kv[0:C].astype(BF16)
        vb = (kv[C:L] + vec(V_BV)).astype(BF16)
        hot = k.xb[j, C : z.XR].astype(F32)
        kf = jnp.where(feat_row < z.ND, (hot - 1.0) * BIG, 0.0).astype(BF16)
        pad = jnp.zeros((48, R), BF16)
        for a in range(H):
            kh, vh = kb[a * HEAD_DIM : (a + 1) * HEAD_DIM], vb[a * HEAD_DIM : (a + 1) * HEAD_DIM]
            k.kx[j, a] = kh
            k.vx[j, a, 0:HEAD_DIM] = vh
            k.vx[j, a, HEAD_DIM:] = one_rows
            k.kt[j, a] = jnp.concatenate([kh, kf, pad], axis=0).T
            k.vt[j, a] = jnp.concatenate([vh, one_rows, pad], axis=0).T

    loop(nb, kv_block)

    for i in range(MB):
        xi = k.xb[s_me * MB + i]
        k.xq[:, i * R : (i + 1) * R] = xi[0:C]
        qi = ((mm(k.wqt[...], xi[0:C]) + vec(V_BQ)).astype(BF16).astype(F32) * HEAD_DIM**-0.5).astype(BF16)
        pad = jnp.zeros((48, R), BF16)
        for a in range(H):
            full = jnp.concatenate([qi[a * HEAD_DIM : (a + 1) * HEAD_DIM], xi[C : z.XR], pad], axis=0)
            k.qx[a, :, i * R : (i + 1) * R] = full
            k.qt[a, i * R : (i + 1) * R, :] = full.T

    def o_send(i, a):
        part = pl.ds(a * HEAD_DIM, HEAD_DIM)
        return rcopy(
            k.oall.at[h, part], k.oall.at[h, part], k.o_ss.at[i, a], k.o_rs.at[i, a], (b, d, hpeer[i])
        )

    def o_wait(i, a):
        part = pl.ds(a * HEAD_DIM, HEAD_DIM)
        rcopy(
            k.oall.at[hsrc[i], part], k.oall.at[hsrc[i], part], k.o_ss.at[i, a], k.o_rs.at[i, a], (b, d, h)
        ).wait_recv()

    def scores(a, j):
        return mm(k.kt[j, a], k.qx[a])

    def prob(a, j):
        if z.keep:
            return k.pbuf[a, j]
        return jnp.exp(scores(a, j) - k.mrow[a, 0:1]).astype(BF16)

    for a in range(H):
        k.mrow[a] = jnp.full((8, Q), -3e38, F32)

        def top(j):
            s = scores(a, j)
            if z.keep:
                k.sbuf[j] = s
            k.mrow[a, 0:1] = jnp.maximum(k.mrow[a, 0:1], jnp.max(s, axis=0, keepdims=True))

        loop(nb, top)
        acc_ref = k.dqacc
        k.mrow[a, 1:2] = jnp.zeros((1, Q), F32)
        acc_ref[a] = jnp.zeros((HEAD_DIM, Q), F32)

        def weigh(j):
            if z.keep:
                k.pbuf[a, j] = jnp.exp(k.sbuf[j] - k.mrow[a, 0:1]).astype(BF16)
            o = mm(k.vx[j, a], prob(a, j))
            acc_ref[a] += o[0:HEAD_DIM]
            k.mrow[a, 1:2] += o[HEAD_DIM : HEAD_DIM + 1]

        loop(nb, weigh)
        inv = 1.0 / k.mrow[a, 1:2]
        k.mrow[a, 2:3] = inv
        k.oall[h, a * HEAD_DIM : (a + 1) * HEAD_DIM] = (acc_ref[a] * inv).astype(BF16)
        for i in range(1, nh):
            o_send(i, a).start()
        if a == 0:
            gather_forward(2)
        if a == 1:
            gather_forward(3)

    gather_wait(3)
    for w in range(W):
        k.fod[w * 4 * z.r : w * 4 * z.r + z.rC] = k.bufC[w].astype(F32)
    for j in range(nh):
        k.wo[j] = k.fod[j * C : (j + 1) * C, 0:C].astype(BF16)
    k.wot[...] = k.fod[0:F, 0:C].T.astype(BF16)
    k.wdn[...] = k.fod[0:F, C:L].astype(BF16)
    k.wdnt[...] = k.fod[0:F, C:L].T.astype(BF16)

    def w_send(i):
        return rcopy(k.wo.at[hpeer[i]], k.wor.at[h], k.w_ss.at[i], k.w_rs.at[i], (b, d, hpeer[i]))

    for i in range(1, nh):
        w_send(i).start()
    k.wor[h] = k.wo[h]
    gather_wait(2)
    for w in range(W):
        slab = k.bufB[w].astype(F32)
        k.fup[w * z.r : w * z.r + z.rs, 0:L] = slab[0 : z.rs]
        k.fup[w * z.r : w * z.r + z.rs, L:F] = slab[z.rs : 2 * z.rs]
    k.wup[...] = k.fup[0:C].astype(BF16)
    k.wupt[...] = k.fup[0:C].T.astype(BF16)

    for i in range(1, nh):
        for a in range(H):
            o_wait(i, a)
    o_full = k.oall[...].reshape(D, Q)
    h1 = k.xq[...].astype(F32) + mm(k.wot[...], o_full) + vec(V_BO)

    def st_send(e, i):
        return rcopy(
            k.stats.at[e, h], k.stats.at[e, h], k.st_ss.at[e, i], k.st_rs.at[e, i], (b, d, hpeer[i])
        )

    def reduce_start(e, rows):
        k.stats[e, h] = jnp.zeros((8, Q), F32)
        for j, v in enumerate(rows):
            k.stats[e, h, j : j + 1] = jnp.sum(v, axis=0, keepdims=True)
        for i in range(1, nh):
            st_send(e, i).start()

    def reduce_end(e):
        for i in range(1, nh):
            src = hsrc[i]
            rcopy(
                k.stats.at[e, src], k.stats.at[e, src], k.st_ss.at[e, i], k.st_rs.at[e, i], (b, d, h)
            ).wait_recv()
        total = k.stats[e, 0]
        for j in range(1, nh):
            total = total + k.stats[e, j]
        return total / D

    reduce_start(0, (h1, h1 * h1))
    tot = reduce_end(0)
    mu1 = tot[0:1]
    r1 = lax.rsqrt(tot[1:2] - mu1 * mu1 + EPS)
    n1 = (h1 - mu1) * r1
    y1 = n1 * vec(V_G1) + vec(V_S1)
    y1b = y1.astype(BF16)

    ub = k.ucol[0:F, V_BU : V_BU + 1]
    u = mm(k.wupt[...], y1b) + ub
    k.u[...] = u
    act = (0.5 * u * (1.0 + lax.erf(u * (0.5**0.5)))).astype(BF16)
    k.act[...] = act
    h2 = y1 + mm(k.wdnt[...], act) + vec(V_BD)

    for i in range(MB):

        @pl.when(jnp.logical_not(jnp.logical_and(x_src_self, s_me * MB + i == b)))
        def _():
            rcopy(k.cb.at[i], k.cb.at[i], k.c_ss.at[i], k.c_rs.at[i], (b, d, h)).wait_recv()

    g = jnp.concatenate([k.cb[i] for i in range(MB)], axis=1).astype(F32)
    dn2 = g * vec(V_G2)
    reduce_start(1, (h2, h2 * h2, dn2, dn2 * h2))
    uu = k.u[...]
    k.u[...] = 0.5 * (1.0 + lax.erf(uu * (0.5**0.5))) + uu * jnp.exp(-0.5 * uu * uu) * ((2 * jnp.pi) ** -0.5)
    tot = reduce_end(1)
    mu2 = tot[0:1]
    r2 = lax.rsqrt(tot[1:2] - mu2 * mu2 + EPS)
    n2 = (h2 - mu2) * r2
    out = (n2 * vec(V_G2) + vec(V_S2)).astype(BF16)
    for i in range(MB):
        k.mo[i] = out[:, i * R : (i + 1) * R]

    def mo_dst(i):
        return s_me * MB + i, d_t

    def mo_send(i):
        return rcopy(k.mo.at[i], k.o_mo.at[m_t], k.mo_ss.at[i], k.mo_rs.at[m_t], (*mo_dst(i), h))

    for i in range(MB):

        @pl.when(not_me(mo_dst(i)))
        def _():
            mo_send(i).start()

        @pl.when(is_me(mo_dst(i)))
        def _():
            k.o_mo[m_t] = k.mo[i]

    dh2 = r2 * (dn2 - tot[2:3] - n2 * (r2 * (tot[3:4] - mu2 * tot[2:3])))
    dz = dh2.astype(BF16)
    ones = jnp.ones((16, Q), BF16)

    def vec_grad(j, x):
        k.vg[j : j + 1] = mm_nt(ones, x)[0:1]

    k.vg[...] = jnp.zeros_like(k.vg)
    k.vgu[...] = jnp.zeros_like(k.vgu)
    vec_grad(V_G2, (g * n2).astype(BF16))
    vec_grad(V_S2, g.astype(BF16))
    vec_grad(V_BD, dz)

    du = (mm(k.wdn[...], dz) * k.u[...]).astype(BF16)
    k.du[...] = du
    dy1 = dh2 + mm(k.wup[...], du)
    dn1 = dy1 * vec(V_G1)
    reduce_start(2, (dn1, dn1 * n1))
    k.god[0:F, C:L] = mm_nt(k.act[...], dz)
    k.gup[0:C] = mm_nt(y1b, k.du[...])
    k.vgu[V_BU : V_BU + 1] = mm_nt(ones, k.du[...])[0:1]
    vec_grad(V_G1, (dy1 * n1).astype(BF16))
    vec_grad(V_S1, dy1.astype(BF16))
    tot = reduce_end(2)
    dh1 = r1 * (dn1 - tot[0:1] - n1 * tot[1:2])
    dp = dh1.astype(BF16)
    k.pall[h] = dp

    def p_send(i):
        return rcopy(k.pall.at[h], k.pall.at[h], k.p_ss.at[i], k.p_rs.at[i], (b, d, hpeer[i]))

    for i in range(1, nh):
        p_send(i).start()

    k.god[0:F, 0:C] = mm_nt(o_full, dp)
    vec_grad(V_BO, dp)
    for w in range(W):
        k.pB[w] = jnp.concatenate(
            [k.gup[w * z.r : w * z.r + z.rs, 0:L], k.gup[w * z.r : w * z.r + z.rs, L:F]]
            + ([jnp.zeros((z.rA - 2 * z.rs, L), F32)] if z.rA > 2 * z.rs else []),
            axis=0,
        ).astype(BF16)
        k.pC[w] = k.god[w * 4 * z.r : w * 4 * z.r + z.rC].astype(BF16)

    packs = (k.pA, k.pV, k.pB, k.pC)
    firsts = (k.r1A, k.r1V, k.r1B, k.r1C)
    seconds = (k.s2A, k.s2V, k.s2B, k.s2C)
    lasts = (k.r2A, k.r2V, k.r2B, k.r2C)
    sums = (k.o_A, k.o_V, k.o_B, k.o_C)

    def s1_send(q, e, i):
        dt = lax.rem(d + e, nd)
        return rcopy(
            packs[q].at[i * nd + dt], firsts[q].at[e - 1, i], k.s1_ss.at[q, e - 1, i], k.s1_rs.at[q, e - 1, i],
            (b, dt, h),
        )

    def s2_send(q, i):
        bt = lax.rem(b + i, nb)
        return rcopy(
            seconds[q].at[bt], lasts[q].at[b], k.s2_ss.at[q, i], k.s2_rs.at[q, i], (bt, d, h)
        )

    def scatter_start(q):
        for e in range(1, nd):
            loop(nb, lambda i: s1_send(q, e, i).start())

    def scatter_forward(q):
        def one(i):
            bt = lax.rem(b + i, nb)
            part = packs[q][bt * nd + d].astype(F32)
            for e in range(1, nd):
                rcopy(
                    firsts[q].at[e - 1, bt], firsts[q].at[e - 1, bt], k.s1_ss.at[q, e - 1, bt],
                    k.s1_rs.at[q, e - 1, bt], (b, d, h),
                ).wait_recv()
                part = part + firsts[q][e - 1, bt].astype(F32)
            return bt, part

        def send(i):
            bt, part = one(i)
            seconds[q][bt] = part.astype(BF16)
            s2_send(q, i).start()

        loop(nb - 1, lambda i: send(i + 1))
        sums[q][...] = one(0)[1]

    def scatter_end(q):
        def one(i):
            src = lax.rem(b + nb - i, nb)
            rcopy(
                lasts[q].at[src], lasts[q].at[src], k.s2_ss.at[q, i], k.s2_rs.at[q, i], (b, d, h)
            ).wait_recv()
            sums[q][...] += lasts[q][src].astype(F32)

        loop(nb - 1, lambda i: one(i + 1))
        loop(nb - 1, lambda i: s2_send(q, i + 1).wait_send())
        for e in range(1, nd):
            loop(nb, lambda i: s1_send(q, e, i).wait_send())

    scatter_start(2)
    scatter_start(3)

    for i in range(1, nh):
        src = hsrc[i]
        rcopy(k.wor.at[src], k.wor.at[src], k.w_ss.at[i], k.w_rs.at[i], (b, d, h)).wait_recv()
        rcopy(k.pall.at[src], k.pall.at[src], k.p_ss.at[i], k.p_rs.at[i], (b, d, h)).wait_recv()
    do = mm(k.wor[0], k.pall[0])
    for j in range(1, nh):
        do = do + mm(k.wor[j], k.pall[j])
    do = do.astype(BF16).astype(F32)
    row16q = lax.broadcasted_iota(jnp.int32, (16, Q), 0)
    for a in range(H):
        part = do[a * HEAD_DIM : (a + 1) * HEAD_DIM] * k.mrow[a, 2:3]
        own = k.oall[h, a * HEAD_DIM : (a + 1) * HEAD_DIM].astype(F32)
        delta = jnp.sum(part * own, axis=0, keepdims=True)
        hi = delta.astype(BF16).astype(F32)
        tail = jnp.where(row16q == 0, -hi, jnp.where(row16q == 1, hi - delta, 0.0))
        full = jnp.concatenate([part.astype(BF16), tail.astype(BF16), jnp.zeros((48, Q), BF16)], axis=0)
        k.dox[a] = full
        k.dot[a] = full.T
        k.dqacc[a] = jnp.zeros((HEAD_DIM, Q), F32)

    k.gkv[...] = jnp.zeros_like(k.gkv)
    k.gq[...] = jnp.zeros_like(k.gq)

    def back_block(j):
        for a in range(H):
            p = prob(a, j)
            ds = (p.astype(F32) * mm(k.vt[j, a], k.dox[a])).astype(BF16)
            k.dqacc[a] += mm(k.kx[j, a], ds)
            dk = mm(ds, k.qt[a])
            dv = mm(p, k.dot[a])
            k.dkv[a * HEAD_DIM : (a + 1) * HEAD_DIM] = dk.T[0:HEAD_DIM].astype(BF16)
            k.dkv[C + a * HEAD_DIM : C + (a + 1) * HEAD_DIM] = dv.T[0:HEAD_DIM].astype(BF16)
        dkv = k.dkv[...]
        k.gkv[0:C] += mm_nt(k.xb[j, 0:C], dkv)
        k.tgs[j] = mm(k.wkv[...], dkv).astype(BF16)
        k.vg[V_BV : V_BV + 1] += mm_nt(ones[:, 0:R], dkv[C:L])[0:1]

    loop(nb, back_block)
    scatter_forward(2)
    scatter_forward(3)

    for a in range(H):
        k.dq[a * HEAD_DIM : (a + 1) * HEAD_DIM] = (k.dqacc[a] * HEAD_DIM**-0.5).astype(BF16)
    dq = k.dq[...]
    k.gq[0:C, 0:C] = mm_nt(k.xq[...], dq)
    vec_grad(V_BQ, dq)
    own = dh1 + mm(k.wq[...], dq)
    for i in range(MB):
        j = s_me * MB + i
        k.tgs[j] = (k.tgs[j].astype(F32) + own[:, i * R : (i + 1) * R]).astype(BF16)

    def t_send(j):
        return rcopy(
            k.tgs.at[j], k.o_tg.at[m_t * S + s_me], k.t_ss.at[j], k.t_rs.at[m_t * S + s_me], (j, d_t, h)
        )

    def t_start(j):
        @pl.when(not_me((j, d_t)))
        def _():
            t_send(j).start()

        @pl.when(is_me((j, d_t)))
        def _():
            k.o_tg[m_t * S + s_me] = k.tgs[j]

    loop(nb, t_start)

    for w in range(W):
        k.pA[w] = jnp.concatenate(
            [k.gkv[w * z.r : w * z.r + z.rs], k.gq[w * z.r : w * z.r + z.rs]]
            + ([jnp.zeros((z.rA - 2 * z.rs, L), F32)] if z.rA > 2 * z.rs else []),
            axis=0,
        ).astype(BF16)
    vgb, vgub = k.vg[...].astype(BF16), k.vgu[...].astype(BF16)

    def pack_v(w):
        def pick(n, per):
            i = lax.broadcasted_iota(jnp.int32, (n, 128), 0)
            j = lax.broadcasted_iota(jnp.int32, (n, 128), 1)
            return jnp.where(jnp.logical_and(i == w * per + j, j < per), 1.0, 0.0).astype(BF16)

        k.pV[w] = (mm(vgb, pick(C, z.r)) + mm(vgub, pick(F, 4 * z.r))).astype(BF16)

    loop(W, pack_v)
    scatter_start(0)
    scatter_start(1)
    scatter_forward(0)
    scatter_forward(1)

    for q in (2, 3, 0, 1):
        scatter_end(q)

    def t_wait(i):
        m, s = i // S, i % S

        @pl.when(not_me(member(m, s)))
        def _():
            rcopy(k.o_tg.at[i], k.o_tg.at[i], k.t_ss.at[0], k.t_rs.at[i], (b, d, h)).wait_recv()

    loop(MB * S, t_wait)

    def t_drain(j):
        @pl.when(not_me((j, d_t)))
        def _():
            t_send(j).wait_send()

    loop(nb, t_drain)
    for m in range(MB):

        @pl.when(not_me(member(m, own_s)))
        def _():
            rcopy(k.o_mo.at[m], k.o_mo.at[m], k.mo_ss.at[m], k.mo_rs.at[m], (b, d, h)).wait_recv()
            c_send(m).wait_send()

    for i in range(MB):

        @pl.when(not_me(mo_dst(i)))
        def _():
            mo_send(i).wait_send()

    def x_drain(i):
        m, s = i // S, i % S

        @pl.when(not_me(member(m, s)))
        def _():
            x_send(m, s).wait_send()

    loop(MB * S, x_drain)
    for q in range(4):
        gather_drain(q)
    for i in range(1, nh):
        for a in range(H):
            o_send(i, a).wait_send()
        w_send(i).wait_send()
        p_send(i).wait_send()
        for e in range(3):
            st_send(e, i).wait_send()


def finish_kernel(z, mo, tg, gA, gB, gC, gV, *outs):
    (mixed, dtok, dwq, dbq, dwk, dwv, dbv, dwo, dbo, dg1, ds1, dwup, dbu, dwdn, dbd, dg2, ds2) = outs
    r, rs, C, L, S = z.r, z.rs, z.C, z.L, z.S
    for m in range(z.MB):
        mixed[m] = mo[m].T
        total = tg[m * S].astype(F32)
        for s in range(1, S):
            total = total + tg[m * S + s].astype(F32)
        dtok[m] = total.T
    dwk[0] = gA[0:r, 0:C]
    dwv[0] = gA[0:r, C:L]
    dwq[0] = gA[rs : rs + r, 0:C]
    dwup[0, :, 0:L] = gB[0:r]
    dwup[0, :, L : 2 * L] = gB[rs : rs + r]
    dwo[...] = gC[0 : 4 * r, 0:C]
    dwdn[0] = gC[0 : 4 * r, C:L]
    for j, ref in enumerate((dbq, dbv, dbo, dg1, ds1, dbd, dg2, ds2)):
        ref[...] = gV[j : j + 1, 0:r]
    dbu[...] = gV[V_BU : V_BU + 1, 0 : 4 * r]


def solution(mesh):
    vec_spec = P("head", ("blk", "dp"))
    mat_spec = P("head", ("blk", "dp"), None)
    tok_spec = P(None, "dp", "head", "blk")
    out_spec = P(("blk", "dp"), "head")

    def body(
        tokens, doc_lengths, cotangent, query_weight, query_bias, key_weight, value_weight, value_bias,
        out_weight, out_bias, first_gain, first_shift, up_weight, up_bias, down_weight, down_bias,
        second_gain, second_shift,
    ):
        z = Sizes(mesh, tokens, query_weight, up_weight, doc_lengths)
        scratch = main_scratch(z)
        vmem = pl.BlockSpec(memory_space=pltpu.VMEM)
        smem = pl.BlockSpec(memory_space=pltpu.SMEM)
        names = INPUTS + OUTPUTS + list(scratch)
        sds = jax.ShapeDtypeStruct
        parts = pl.pallas_call(
            lambda *refs: main_kernel(z, names, *refs),
            out_shape=[
                sds((z.MB, z.C, z.R), BF16),
                sds((z.MB * z.S, z.C, z.R), BF16),
                sds((z.rA, z.L), F32),
                sds((z.rA, z.L), F32),
                sds((z.rC, z.L), F32),
                sds((VROWS, 128), F32),
            ],
            in_specs=[smem] + [vmem] * (len(INPUTS) - 1),
            out_specs=[vmem] * len(OUTPUTS),
            scratch_shapes=list(scratch.values()),
            compiler_params=pltpu.CompilerParams(
                collective_id=0, has_side_effects=True, vmem_limit_bytes=63 << 20
            ),
            name="layer",
        )(
            doc_lengths, tokens.reshape(z.MB, z.R, z.C), cotangent.reshape(z.MB, z.R, z.C), query_weight,
            query_bias, key_weight, value_weight, value_bias, out_weight, out_bias, first_gain, first_shift,
            up_weight, up_bias, down_weight, down_bias, second_gain, second_shift,
        )
        mat, vec = sds((1, z.r, z.C), F32), sds((1, z.r), F32)
        outs = pl.pallas_call(
            lambda *refs: finish_kernel(z, *refs),
            out_shape=[
                sds((z.MB, z.R, z.C), BF16), sds((z.MB, z.R, z.C), F32), mat, vec, mat, mat, vec,
                sds((4 * z.r, z.C), F32), vec, vec, vec, sds((1, z.r, z.F), F32), sds((1, 4 * z.r), F32),
                sds((1, 4 * z.r, z.C), F32), vec, vec, vec,
            ],
            in_specs=[vmem] * len(OUTPUTS),
            out_specs=[vmem] * 17,
            name="finish",
        )(*parts)
        shape = tokens.shape
        return (outs[0].reshape(shape), outs[1].reshape(shape), *outs[2:])

    return jax.shard_map(
        body,
        mesh=mesh,
        in_specs=(
            tok_spec, P(None, "dp", None), tok_spec, mat_spec, vec_spec, mat_spec, mat_spec, vec_spec,
            out_spec, vec_spec, vec_spec, vec_spec, mat_spec, vec_spec, mat_spec, vec_spec, vec_spec, vec_spec,
        ),
        out_specs=(
            tok_spec, tok_spec, mat_spec, vec_spec, mat_spec, mat_spec, vec_spec, out_spec, vec_spec, vec_spec,
            vec_spec, mat_spec, vec_spec, mat_spec, vec_spec, vec_spec, vec_spec,
        ),
        check_vma=False,
    )
```

time: 1610 us -> 105 us (0.07)
  the two profiles are of different devices: /device:TPU:0 before, /device:TPU:1 now
where the time goes in v1:
time: 105 us
  Pallas kernels  97 us (92%)
  local copies, waits for them, and re-layouts  7.15 us (7%)
    pallas_call x1, Pallas kernels, body(): pl.pallas_call(lambda *refs: main_kernel(z, names, *refs), out_shape=[sds...  94.6 us
    reshape x2, local copies, waits for them, and re-layouts, body(): return (outs[0].reshape(shape), outs[1].reshape(shape), *outs[2:])  4.23 us
    pallas_call x1, Pallas kernels, body(): pl.pallas_call(lambda *refs: finish_kernel(z, *refs), out_shape=[sds((z.M...  2.46 us

profile of v1, /device:TPU:1, one launch (start us, length us, event | category | flops | bytes accessed | tf_op | source)
XLA Modules:
  0.0 104.8 jit_solution(16482320737906003349)
XLA Ops:
  0.7 0.0 copy-start
  0.7 2.0 %reshape.46.refs_1_ = bf16[2,256,192]{2,1,0:T(8,128)(2,1)} reshape(bf16[2,1,1,49152]{3,0,2,1:T(2,128)(2,1)} %param.18) | data formatting | bytes 393216 | tf_op jit(solution)/shard_map/reshape | solution.py:841
  2.6 0.0 copy-done
  2.6 1.0 reshape.47.refs_2_
  3.6 94.6 %layer.1 = (bf16[2,192,256]{2,1,0:T(8,128)(2,1)}, bf16[4,192,256]{2,1,0:T(8,128)(2,1)}, f32[48,384]{1,0:T(8,128)}, f32[48,384]{1,0:T(8,128)}, f32[96,384]{1,0:T(8,128)}, /*index=5*/f32[16,128]{1,0:T(8,128)}) custom-call(s32[2,1,4]{2,1,0:T(1,128)} %refs_0_.1, bf16[2,256,192]{2,1,0:T(8,128)(2,1)} %reshape.46.refs_1_, bf16[2,256,192]{2,1,0:T(8,128)(2,1)} %reshape.47.refs_2_, ...), custom_call_target="tpu_custom_call" | custom-call | tf_op jit(solution)/shard_map/layer/pallas_call | solution.py:823
  98.1 2.5 %finish.1 = (bf16[2,256,192]{2,1,0:T(8,128)(2,1)}, f32[2,256,192]{2,1,0:T(8,128)}, f32[1,24,192]{2,1,0:T(8,128)}, f32[1,24]{1,0:T(1,128)}, f32[1,24,192]{2,1,0:T...) custom-call(bf16[2,192,256]{2,1,0:T(8,128)(2,1)} %get-tuple-element., ...), custom_call_target="tpu_custom_call" | custom-call | tf_op jit(solution)/shard_map/finish/pallas_call | solution.py:846
  100.6 2.0 %reshape.48 = bf16[2,1,1,49152]{3,0,2,1:T(2,128)(2,1)} reshape(bf16[2,256,192]{2,1,0:T(8,128)(2,1)} %get-tuple-element.46) | data formatting | bytes 393216 | tf_op jit(solution)/shard_map/reshape | solution.py:858
  102.6 2.3 %reshape.50 = f32[2,1,1,49152]{3,2,1,0:T(1,128)} reshape(f32[2,256,192]{2,1,0:T(8,128)} %get-tuple-element.47) | data formatting | bytes 786432 | tf_op jit(solution)/shard_map/reshape | solution.py:858
Async XLA Ops:
  0.7 2.0 %copy-start = (bf16[2,1,1,49152]{3,0,2,1:T(2,128)(2,1)S(1)}, bf16[2,1,1,49152]{3,0,2,1:T(2,128)(2,1)}, u32[]{:S(2)}) copy-start(bf16[2,1,1,49152]{3,0,2,1:T(2,128)(2,1)} %param.20) | copy-start | bytes 589828

commit v2 on v1

--- a/solution.py
+++ b/solution.py
@@ -110,7 +110,7 @@
         mrow=v((H, 8, Q), F32),
         oall=v((z.nh, C, Q), BF16),
         pall=v((z.nh, C, Q), BF16),
-        stats=v((3, z.nh, 8, Q), F32),
+        stats=v((3, z.nh, 4 * Q // 128, 128), F32),
         u=v((F, Q), F32),
         act=v((F, Q), BF16),
         du=v((F, Q), BF16),
@@ -121,6 +121,9 @@
         dkv=v((L, R), BF16),
         dq=v((C, Q), BF16),
         tgs=v((nb, C, R), BF16),
+        tgo=v((z.MB, C, R), F32),
+        tgr=v((z.MB, z.S, C, R), BF16),
+        tgx=v((z.MB, C, R), BF16),
         gkv=v((C + 8, L), F32),
         gq=v((C + 8, L), F32),
         gup=v((C + 8, F), F32),
@@ -143,7 +146,8 @@
         r2B=v((nb, z.rA, L), BF16),
         r2C=v((nb, z.rC, L), BF16),
         r2V=v((nb, VROWS, 128), BF16),
-        x_ss=dma((z.MB * z.S,)),
+        x_ss=dma((z.MB,)),
+        xf_ss=dma((z.MB, z.S)),
         x_rs=dma((nb,)),
         c_ss=dma((z.MB,)),
         c_rs=dma((z.MB,)),
@@ -157,12 +161,14 @@
         w_rs=dma((z.nh,)),
         st_ss=dma((3, z.nh)),
         st_rs=dma((3, z.nh)),
-        p_ss=dma((z.nh,)),
-        p_rs=dma((z.nh,)),
+        p_ss=dma((z.nh, H)),
+        p_rs=dma((z.nh, H)),
         mo_ss=dma((z.MB,)),
         mo_rs=dma((z.MB,)),
-        t_ss=dma((nb,)),
-        t_rs=dma((z.MB * z.S,)),
+        tp_ss=dma((nb,)),
+        tp_rs=dma((z.MB, z.S)),
+        t_ss=dma((z.MB,)),
+        t_rs=dma((z.MB,)),
         s1_ss=dma((4, dd, nb)),
         s1_rs=dma((4, dd, nb)),
         s2_ss=dma((4, nb)),
@@ -234,9 +240,8 @@
     def member(m, s):
         return (m * nd + d) * z.tb + s // nd, s % nd
 
-    def x_send(m, s):
-        bt, dt = member(m, s)
-        return rcopy(k.xs.at[m], k.xb.at[b], k.x_ss.at[m * S + s], k.x_rs.at[b], (bt, dt, h))
+    def mate(s):
+        return team * z.tb + s // nd, s % nd
 
     def not_me(pos):
         return jnp.logical_or(pos[0] != b, pos[1] != d)
@@ -244,18 +249,31 @@
     def is_me(pos):
         return jnp.logical_and(pos[0] == b, pos[1] == d)
 
-    def start_x(i):
-        m, s = i // S, i % S
-
-        @pl.when(not_me(member(m, s)))
+    own_s, own_i = b % S, b // S
+    mine = [i * S + s_me for i in range(MB)]
+
+    def x_send(m):
+        return rcopy(k.xs.at[m], k.xb.at[b], k.x_ss.at[m], k.x_rs.at[b], (*member(m, own_s), h))
+
+    def x_pass(i, e):
+        to = mate(lax.rem(s_me + e, S))
+        return rcopy(k.xb.at[mine[i]], k.xb.at[mine[i]], k.xf_ss.at[i, e], k.x_rs.at[mine[i]], (*to, h))
+
+    def x_wait(j):
+        rcopy(k.xb.at[j], k.xb.at[j], k.x_ss.at[0], k.x_rs.at[j], (b, d, h)).wait_recv()
+
+    def from_me(i):
+        return jnp.logical_and(d == d_t, mine[i] == b)
+
+    for m in range(MB):
+
+        @pl.when(not_me(member(m, own_s)))
         def _():
-            x_send(m, s).start()
-
-        @pl.when(is_me(member(m, s)))
+            x_send(m).start()
+
+        @pl.when(is_me(member(m, own_s)))
         def _():
             k.xb[b] = k.xs[m]
-
-    loop(MB * S, start_x)
 
     bufs = (k.bufA, k.bufV, k.bufB, k.bufC)
 
@@ -305,27 +323,18 @@
     gather_start(0)
     gather_start(1)
 
-    own_s = b // MB
-
-    def c_send(m):
-        return rcopy(
-            k.cs.at[m], k.cb.at[b % MB], k.c_ss.at[m], k.c_rs.at[b % MB], (*member(m, own_s), h)
-        )
-
-    for m in range(MB):
-
-        @pl.when(not_me(member(m, own_s)))
+    for i in range(MB):
+
+        @pl.when(jnp.logical_not(from_me(i)))
         def _():
-            c_send(m).start()
-
-        @pl.when(is_me(member(m, own_s)))
-        def _():
-            k.cb[b % MB] = k.cs[m]
-
-    gather_start(2)
-    gather_start(3)
+            x_wait(mine[i])
+
+        loop(S - 1, lambda e: x_pass(i, e + 1).start())
+
     gather_forward(0)
     gather_forward(1)
+    gather_start(3)
+
     gather_wait(0)
     gather_wait(1)
 
@@ -348,18 +357,10 @@
     def vec(j):
         return k.vcol[0:C, j : j + 1]
 
-    x_src_self = d == d_t
     feat_row = lax.broadcasted_iota(jnp.int32, (16, R), 0)
-
-    def x_wait(j):
-        @pl.when(jnp.logical_not(jnp.logical_and(x_src_self, j == b)))
-        def _():
-            rcopy(k.xb.at[j], k.xb.at[j], k.x_ss.at[0], k.x_rs.at[j], (b, d, h)).wait_recv()
-
     one_rows = jnp.where(feat_row < 2, 1.0, 0.0).astype(BF16)
 
     def kv_block(j):
-        x_wait(j)
         kv = mm(k.wkvt[...], k.xb[j, 0:C])
         kb = kv[0:C].astype(BF16)
         vb = (kv[C:L] + vec(V_BV)).astype(BF16)
@@ -374,10 +375,17 @@
             k.kt[j, a] = jnp.concatenate([kh, kf, pad], axis=0).T
             k.vt[j, a] = jnp.concatenate([vh, one_rows, pad], axis=0).T
 
-    loop(nb, kv_block)
+    def kv_other(n):
+        j = lax.rem(s_me + 1 + n // MB, S) + (n % MB) * S
+        x_wait(j)
+        kv_block(j)
 
     for i in range(MB):
-        xi = k.xb[s_me * MB + i]
+        kv_block(mine[i])
+    loop(nb - MB, kv_other)
+
+    for i in range(MB):
+        xi = k.xb[mine[i]]
         k.xq[:, i * R : (i + 1) * R] = xi[0:C]
         qi = ((mm(k.wqt[...], xi[0:C]) + vec(V_BQ)).astype(BF16).astype(F32) * HEAD_DIM**-0.5).astype(BF16)
         pad = jnp.zeros((48, R), BF16)
@@ -386,17 +394,50 @@
             k.qx[a, :, i * R : (i + 1) * R] = full
             k.qt[a, i * R : (i + 1) * R, :] = full.T
 
-    def o_send(i, a):
+    def c_send(m):
+        return rcopy(k.cs.at[m], k.cb.at[own_i], k.c_ss.at[m], k.c_rs.at[own_i], (*member(m, own_s), h))
+
+    def c_start():
+        for m in range(MB):
+
+            @pl.when(not_me(member(m, own_s)))
+            def _():
+                c_send(m).start()
+
+            @pl.when(is_me(member(m, own_s)))
+            def _():
+                k.cb[own_i] = k.cs[m]
+
+    half = nh // 2
+
+    def xor(i):
+        return lax.bitwise_xor(h, i)
+
+    def head_send(buf, ss, rs, i, a):
         part = pl.ds(a * HEAD_DIM, HEAD_DIM)
-        return rcopy(
-            k.oall.at[h, part], k.oall.at[h, part], k.o_ss.at[i, a], k.o_rs.at[i, a], (b, d, hpeer[i])
-        )
-
-    def o_wait(i, a):
+        src, to = (h, xor(i)) if i <= half else (xor(half), xor(i - half))
+        return rcopy(buf.at[src, part], buf.at[src, part], ss.at[i, a], rs.at[i, a], (b, d, to))
+
+    def head_wait(buf, ss, rs, i, a):
         part = pl.ds(a * HEAD_DIM, HEAD_DIM)
-        rcopy(
-            k.oall.at[hsrc[i], part], k.oall.at[hsrc[i], part], k.o_ss.at[i, a], k.o_rs.at[i, a], (b, d, h)
-        ).wait_recv()
+        rcopy(buf.at[xor(i), part], buf.at[xor(i), part], ss.at[i, a], rs.at[i, a], (b, d, h)).wait_recv()
+
+    def head_start(buf, ss, rs, a):
+        for i in range(half, 0, -1):
+            head_send(buf, ss, rs, i, a).start()
+
+    def head_pass(buf, ss, rs, a):
+        head_wait(buf, ss, rs, half, a)
+        for i in range(half + 1, nh):
+            head_send(buf, ss, rs, i, a).start()
+
+    def head_end(buf, ss, rs, a):
+        for i in range(1, nh):
+            if i != half:
+                head_wait(buf, ss, rs, i, a)
+
+    o_net = (k.oall, k.o_ss, k.o_rs)
+    p_net = (k.pall, k.p_ss, k.p_rs)
 
     def scores(a, j):
         return mm(k.kt[j, a], k.qx[a])
@@ -431,12 +472,14 @@
         inv = 1.0 / k.mrow[a, 1:2]
         k.mrow[a, 2:3] = inv
         k.oall[h, a * HEAD_DIM : (a + 1) * HEAD_DIM] = (acc_ref[a] * inv).astype(BF16)
-        for i in range(1, nh):
-            o_send(i, a).start()
+        head_start(*o_net, a)
         if a == 0:
-            gather_forward(2)
-        if a == 1:
-            gather_forward(3)
+            gather_start(2)
+
+    gather_forward(3)
+    for a in range(H):
+        head_pass(*o_net, a)
+    c_start()
 
     gather_wait(3)
     for w in range(W):
@@ -450,9 +493,42 @@
     def w_send(i):
         return rcopy(k.wo.at[hpeer[i]], k.wor.at[h], k.w_ss.at[i], k.w_rs.at[i], (b, d, hpeer[i]))
 
-    for i in range(1, nh):
-        w_send(i).start()
-    k.wor[h] = k.wo[h]
+    for a in range(H):
+        head_end(*o_net, a)
+    o_full = k.oall[...].reshape(D, Q)
+    h1 = k.xq[...].astype(F32) + mm(k.wot[...], o_full) + vec(V_BO)
+
+    lane_rows = Q // 128
+    stat_rows = [pl.ds(0, n * lane_rows) for n in (2, 4, 2)]
+
+    def st_send(e, i):
+        mine_ = k.stats.at[e, h, stat_rows[e]]
+        return rcopy(mine_, mine_, k.st_ss.at[e, i], k.st_rs.at[e, i], (b, d, hpeer[i]))
+
+    def reduce_start(e, rows):
+        for j, v in enumerate(rows):
+            row = jnp.sum(v, axis=0, keepdims=True)
+            for c in range(lane_rows):
+                k.stats[e, h, pl.ds(j * lane_rows + c, 1)] = row[:, c * 128 : (c + 1) * 128]
+        for i in range(1, nh):
+            st_send(e, i).start()
+
+    def reduce_end(e):
+        for i in range(1, nh):
+            src = k.stats.at[e, hsrc[i], stat_rows[e]]
+            rcopy(src, src, k.st_ss.at[e, i], k.st_rs.at[e, i], (b, d, h)).wait_recv()
+        total = k.stats[e, 0, stat_rows[e]]
+        for j in range(1, nh):
+            total = total + k.stats[e, j, stat_rows[e]]
+        total = total / D
+        return [
+            jnp.concatenate([total[j * lane_rows + c :][0:1] for c in range(lane_rows)], axis=1)
+            for j in range(stat_rows[e].size // lane_rows)
+        ]
+
+    reduce_start(0, (h1, h1 * h1))
+
+    gather_forward(2)
     gather_wait(2)
     for w in range(W):
         slab = k.bufB[w].astype(F32)
@@ -461,39 +537,12 @@
     k.wup[...] = k.fup[0:C].astype(BF16)
     k.wupt[...] = k.fup[0:C].T.astype(BF16)
 
+    tot = reduce_end(0)
     for i in range(1, nh):
-        for a in range(H):
-            o_wait(i, a)
-    o_full = k.oall[...].reshape(D, Q)
-    h1 = k.xq[...].astype(F32) + mm(k.wot[...], o_full) + vec(V_BO)
-
-    def st_send(e, i):
-        return rcopy(
-            k.stats.at[e, h], k.stats.at[e, h], k.st_ss.at[e, i], k.st_rs.at[e, i], (b, d, hpeer[i])
-        )
-
-    def reduce_start(e, rows):
-        k.stats[e, h] = jnp.zeros((8, Q), F32)
-        for j, v in enumerate(rows):
-            k.stats[e, h, j : j + 1] = jnp.sum(v, axis=0, keepdims=True)
-        for i in range(1, nh):
-            st_send(e, i).start()
-
-    def reduce_end(e):
-        for i in range(1, nh):
-            src = hsrc[i]
-            rcopy(
-                k.stats.at[e, src], k.stats.at[e, src], k.st_ss.at[e, i], k.st_rs.at[e, i], (b, d, h)
-            ).wait_recv()
-        total = k.stats[e, 0]
-        for j in range(1, nh):
-            total = total + k.stats[e, j]
-        return total / D
-
-    reduce_start(0, (h1, h1 * h1))
-    tot = reduce_end(0)
-    mu1 = tot[0:1]
-    r1 = lax.rsqrt(tot[1:2] - mu1 * mu1 + EPS)
+        w_send(i).start()
+    k.wor[h] = k.wo[h]
+    mu1 = tot[0]
+    r1 = lax.rsqrt(tot[1] - mu1 * mu1 + EPS)
     n1 = (h1 - mu1) * r1
     y1 = n1 * vec(V_G1) + vec(V_S1)
     y1b = y1.astype(BF16)
@@ -507,7 +556,7 @@
 
     for i in range(MB):
 
-        @pl.when(jnp.logical_not(jnp.logical_and(x_src_self, s_me * MB + i == b)))
+        @pl.when(jnp.logical_not(from_me(i)))
         def _():
             rcopy(k.cb.at[i], k.cb.at[i], k.c_ss.at[i], k.c_rs.at[i], (b, d, h)).wait_recv()
 
@@ -517,15 +566,15 @@
     uu = k.u[...]
     k.u[...] = 0.5 * (1.0 + lax.erf(uu * (0.5**0.5))) + uu * jnp.exp(-0.5 * uu * uu) * ((2 * jnp.pi) ** -0.5)
     tot = reduce_end(1)
-    mu2 = tot[0:1]
-    r2 = lax.rsqrt(tot[1:2] - mu2 * mu2 + EPS)
+    mu2 = tot[0]
+    r2 = lax.rsqrt(tot[1] - mu2 * mu2 + EPS)
     n2 = (h2 - mu2) * r2
     out = (n2 * vec(V_G2) + vec(V_S2)).astype(BF16)
     for i in range(MB):
         k.mo[i] = out[:, i * R : (i + 1) * R]
 
     def mo_dst(i):
-        return s_me * MB + i, d_t
+        return mine[i], d_t
 
     def mo_send(i):
         return rcopy(k.mo.at[i], k.o_mo.at[m_t], k.mo_ss.at[i], k.mo_rs.at[m_t], (*mo_dst(i), h))
@@ -540,7 +589,7 @@
         def _():
             k.o_mo[m_t] = k.mo[i]
 
-    dh2 = r2 * (dn2 - tot[2:3] - n2 * (r2 * (tot[3:4] - mu2 * tot[2:3])))
+    dh2 = r2 * (dn2 - tot[2] - n2 * (r2 * (tot[3] - mu2 * tot[2])))
     dz = dh2.astype(BF16)
     ones = jnp.ones((16, Q), BF16)
 
@@ -552,37 +601,6 @@
     vec_grad(V_G2, (g * n2).astype(BF16))
     vec_grad(V_S2, g.astype(BF16))
     vec_grad(V_BD, dz)
-
-    du = (mm(k.wdn[...], dz) * k.u[...]).astype(BF16)
-    k.du[...] = du
-    dy1 = dh2 + mm(k.wup[...], du)
-    dn1 = dy1 * vec(V_G1)
-    reduce_start(2, (dn1, dn1 * n1))
-    k.god[0:F, C:L] = mm_nt(k.act[...], dz)
-    k.gup[0:C] = mm_nt(y1b, k.du[...])
-    k.vgu[V_BU : V_BU + 1] = mm_nt(ones, k.du[...])[0:1]
-    vec_grad(V_G1, (dy1 * n1).astype(BF16))
-    vec_grad(V_S1, dy1.astype(BF16))
-    tot = reduce_end(2)
-    dh1 = r1 * (dn1 - tot[0:1] - n1 * tot[1:2])
-    dp = dh1.astype(BF16)
-    k.pall[h] = dp
-
-    def p_send(i):
-        return rcopy(k.pall.at[h], k.pall.at[h], k.p_ss.at[i], k.p_rs.at[i], (b, d, hpeer[i]))
-
-    for i in range(1, nh):
-        p_send(i).start()
-
-    k.god[0:F, 0:C] = mm_nt(o_full, dp)
-    vec_grad(V_BO, dp)
-    for w in range(W):
-        k.pB[w] = jnp.concatenate(
-            [k.gup[w * z.r : w * z.r + z.rs, 0:L], k.gup[w * z.r : w * z.r + z.rs, L:F]]
-            + ([jnp.zeros((z.rA - 2 * z.rs, L), F32)] if z.rA > 2 * z.rs else []),
-            axis=0,
-        ).astype(BF16)
-        k.pC[w] = k.god[w * 4 * z.r : w * 4 * z.r + z.rC].astype(BF16)
 
     packs = (k.pA, k.pV, k.pB, k.pC)
     firsts = (k.r1A, k.r1V, k.r1B, k.r1C)
@@ -607,25 +625,27 @@
         for e in range(1, nd):
             loop(nb, lambda i: s1_send(q, e, i).start())
 
+    def scatter_sum(q, bt):
+        part = packs[q][bt * nd + d].astype(F32)
+        for e in range(1, nd):
+            rcopy(
+                firsts[q].at[e - 1, bt], firsts[q].at[e - 1, bt], k.s1_ss.at[q, e - 1, bt],
+                k.s1_rs.at[q, e - 1, bt], (b, d, h),
+            ).wait_recv()
+            part = part + firsts[q][e - 1, bt].astype(F32)
+        return part
+
+    def scatter_pass(q, i):
+        bt = lax.rem(b + i, nb)
+        seconds[q][bt] = scatter_sum(q, bt).astype(BF16)
+        s2_send(q, i).start()
+
+    def scatter_own(q):
+        sums[q][...] = scatter_sum(q, b)
+
     def scatter_forward(q):
-        def one(i):
-            bt = lax.rem(b + i, nb)
-            part = packs[q][bt * nd + d].astype(F32)
-            for e in range(1, nd):
-                rcopy(
-                    firsts[q].at[e - 1, bt], firsts[q].at[e - 1, bt], k.s1_ss.at[q, e - 1, bt],
-                    k.s1_rs.at[q, e - 1, bt], (b, d, h),
-                ).wait_recv()
-                part = part + firsts[q][e - 1, bt].astype(F32)
-            return bt, part
-
-        def send(i):
-            bt, part = one(i)
-            seconds[q][bt] = part.astype(BF16)
-            s2_send(q, i).start()
-
-        loop(nb - 1, lambda i: send(i + 1))
-        sums[q][...] = one(0)[1]
+        loop(nb - 1, lambda i: scatter_pass(q, i + 1))
+        scatter_own(q)
 
     def scatter_end(q):
         def one(i):
@@ -640,13 +660,45 @@
         for e in range(1, nd):
             loop(nb, lambda i: s1_send(q, e, i).wait_send())
 
+    du = (mm(k.wdn[...], dz) * k.u[...]).astype(BF16)
+    k.du[...] = du
+    dy1 = dh2 + mm(k.wup[...], du)
+    dn1 = dy1 * vec(V_G1)
+    reduce_start(2, (dn1, dn1 * n1))
+    k.gup[0:C] = mm_nt(y1b, k.du[...])
+    for w in range(W):
+        k.pB[w] = jnp.concatenate(
+            [k.gup[w * z.r : w * z.r + z.rs, 0:L], k.gup[w * z.r : w * z.r + z.rs, L:F]]
+            + ([jnp.zeros((z.rA - 2 * z.rs, L), F32)] if z.rA > 2 * z.rs else []),
+            axis=0,
+        ).astype(BF16)
     scatter_start(2)
+    k.god[0:F, C:L] = mm_nt(k.act[...], dz)
+    k.vgu[V_BU : V_BU + 1] = mm_nt(ones, k.du[...])[0:1]
+    vec_grad(V_G1, (dy1 * n1).astype(BF16))
+    vec_grad(V_S1, dy1.astype(BF16))
+    tot = reduce_end(2)
+    dh1 = r1 * (dn1 - tot[0] - n1 * tot[1])
+    dp = dh1.astype(BF16)
+    k.pall[h] = dp
+
+    for a in range(H):
+        head_start(*p_net, a)
+
+    k.god[0:F, 0:C] = mm_nt(o_full, dp)
+    vec_grad(V_BO, dp)
+    for w in range(W):
+        k.pC[w] = k.god[w * 4 * z.r : w * 4 * z.r + z.rC].astype(BF16)
     scatter_start(3)
-
+    for a in range(H):
+        head_pass(*p_net, a)
+    scatter_forward(2)
+
+    for a in range(H):
+        head_end(*p_net, a)
     for i in range(1, nh):
         src = hsrc[i]
         rcopy(k.wor.at[src], k.wor.at[src], k.w_ss.at[i], k.w_rs.at[i], (b, d, h)).wait_recv()
-        rcopy(k.pall.at[src], k.pall.at[src], k.p_ss.at[i], k.p_rs.at[i], (b, d, h)).wait_recv()
     do = mm(k.wor[0], k.pall[0])
     for j in range(1, nh):
         do = do + mm(k.wor[j], k.pall[j])
@@ -666,6 +718,11 @@
     k.gkv[...] = jnp.zeros_like(k.gkv)
     k.gq[...] = jnp.zeros_like(k.gq)
 
+    def tp_send(j):
+        to = j % S
+        dst = k.tgr.at[j // S, s_me]
+        return rcopy(k.tgs.at[j], dst, k.tp_ss.at[j], k.tp_rs.at[j // S, s_me], (*mate(to), h))
+
     def back_block(j):
         for a in range(H):
             p = prob(a, j)
@@ -677,38 +734,24 @@
             k.dkv[C + a * HEAD_DIM : C + (a + 1) * HEAD_DIM] = dv.T[0:HEAD_DIM].astype(BF16)
         dkv = k.dkv[...]
         k.gkv[0:C] += mm_nt(k.xb[j, 0:C], dkv)
-        k.tgs[j] = mm(k.wkv[...], dkv).astype(BF16)
         k.vg[V_BV : V_BV + 1] += mm_nt(ones[:, 0:R], dkv[C:L])[0:1]
-
-    loop(nb, back_block)
-    scatter_forward(2)
+        return mm(k.wkv[...], dkv)
+
+    def back_other(n):
+        j = lax.rem(s_me + 1 + n // MB, S) + (n % MB) * S
+        k.tgs[j] = back_block(j).astype(BF16)
+        tp_send(j).start()
+
+    loop(nb - MB, back_other)
     scatter_forward(3)
+    for i in range(MB):
+        k.tgo[i] = back_block(mine[i])
 
     for a in range(H):
         k.dq[a * HEAD_DIM : (a + 1) * HEAD_DIM] = (k.dqacc[a] * HEAD_DIM**-0.5).astype(BF16)
     dq = k.dq[...]
     k.gq[0:C, 0:C] = mm_nt(k.xq[...], dq)
     vec_grad(V_BQ, dq)
-    own = dh1 + mm(k.wq[...], dq)
-    for i in range(MB):
-        j = s_me * MB + i
-        k.tgs[j] = (k.tgs[j].astype(F32) + own[:, i * R : (i + 1) * R]).astype(BF16)
-
-    def t_send(j):
-        return rcopy(
-            k.tgs.at[j], k.o_tg.at[m_t * S + s_me], k.t_ss.at[j], k.t_rs.at[m_t * S + s_me], (j, d_t, h)
-        )
-
-    def t_start(j):
-        @pl.when(not_me((j, d_t)))
-        def _():
-            t_send(j).start()
-
-        @pl.when(is_me((j, d_t)))
-        def _():
-            k.o_tg[m_t * S + s_me] = k.tgs[j]
-
-    loop(nb, t_start)
 
     for w in range(W):
         k.pA[w] = jnp.concatenate(
@@ -729,68 +772,75 @@
     loop(W, pack_v)
     scatter_start(0)
     scatter_start(1)
+
+    def t_send(i):
+        return rcopy(k.tgx.at[i], k.o_tg.at[m_t], k.t_ss.at[i], k.t_rs.at[m_t], (*mo_dst(i), h))
+
+    own = dh1 + mm(k.wq[...], dq)
+    for i in range(MB):
+        k.tgo[i] += own[:, i * R : (i + 1) * R]
+
+        def add(e):
+            s = lax.rem(s_me + e + 1, S)
+            rcopy(k.tgr.at[i, s], k.tgr.at[i, s], k.tp_ss.at[0], k.tp_rs.at[i, s], (b, d, h)).wait_recv()
+            k.tgo[i] += k.tgr[i, s].astype(F32)
+
+        loop(S - 1, add)
+        k.tgx[i] = k.tgo[i].astype(BF16)
+
+        @pl.when(not_me(mo_dst(i)))
+        def _():
+            t_send(i).start()
+
+        @pl.when(is_me(mo_dst(i)))
+        def _():
+            k.o_tg[m_t] = k.tgx[i]
+
     scatter_forward(0)
     scatter_forward(1)
 
     for q in (2, 3, 0, 1):
         scatter_end(q)
 
-    def t_wait(i):
-        m, s = i // S, i % S
-
-        @pl.when(not_me(member(m, s)))
-        def _():
-            rcopy(k.o_tg.at[i], k.o_tg.at[i], k.t_ss.at[0], k.t_rs.at[i], (b, d, h)).wait_recv()
-
-    loop(MB * S, t_wait)
-
-    def t_drain(j):
-        @pl.when(not_me((j, d_t)))
-        def _():
-            t_send(j).wait_send()
-
-    loop(nb, t_drain)
     for m in range(MB):
 
         @pl.when(not_me(member(m, own_s)))
         def _():
+            rcopy(k.o_tg.at[m], k.o_tg.at[m], k.t_ss.at[m], k.t_rs.at[m], (b, d, h)).wait_recv()
             rcopy(k.o_mo.at[m], k.o_mo.at[m], k.mo_ss.at[m], k.mo_rs.at[m], (b, d, h)).wait_recv()
             c_send(m).wait_send()
+            x_send(m).wait_send()
 
     for i in range(MB):
 
         @pl.when(not_me(mo_dst(i)))
         def _():
             mo_send(i).wait_send()
-
-    def x_drain(i):
-        m, s = i // S, i % S
-
-        @pl.when(not_me(member(m, s)))
-        def _():
-            x_send(m, s).wait_send()
-
-    loop(MB * S, x_drain)
+            t_send(i).wait_send()
+
+        loop(S - 1, lambda e: x_pass(i, e + 1).wait_send())
+
+    def tp_drain(n):
+        tp_send(lax.rem(s_me + 1 + n // MB, S) + (n % MB) * S).wait_send()
+
+    loop(nb - MB, tp_drain)
     for q in range(4):
         gather_drain(q)
     for i in range(1, nh):
         for a in range(H):
-            o_send(i, a).wait_send()
+            head_send(*o_net, i, a).wait_send()
+            head_send(*p_net, i, a).wait_send()
         w_send(i).wait_send()
-        p_send(i).wait_send()
         for e in range(3):
             st_send(e, i).wait_send()
 
 
 def finish_kernel(z, mo, tg, gA, gB, gC, gV, *outs):
     (mixed, dtok, dwq, dbq, dwk, dwv, dbv, dwo, dbo, dg1, ds1, dwup, dbu, dwdn, dbd, dg2, ds2) = outs
-    r, rs, C, L, S = z.r, z.rs, z.C, z.L, z.S
+    r, rs, C, L = z.r, z.rs, z.C, z.L
     for m in range(z.MB):
         mixed[m] = mo[m].T
-        total = tg[m * S].astype(F32)
-        for s in range(1, S):
-            total = total + tg[m * S + s].astype(F32)
-        dtok[m] = total.T
+        dtok[m] = tg[m].astype(F32).T
     dwk[0] = gA[0:r, 0:C]
     dwv[0] = gA[0:r, C:L]
     dwq[0] = gA[rs : rs + r, 0:C]
@@ -824,7 +874,7 @@
             lambda *refs: main_kernel(z, names, *refs),
             out_shape=[
                 sds((z.MB, z.C, z.R), BF16),
-                sds((z.MB * z.S, z.C, z.R), BF16),
+                sds((z.MB, z.C, z.R), BF16),
                 sds((z.rA, z.L), F32),
                 sds((z.rA, z.L), F32),
                 sds((z.rC, z.L), F32),

time: 105 us -> 92.2 us (0.88)
  the two profiles are of different devices: /device:TPU:1 before, /device:TPU:0 now
where the time goes in v2:
time: 92.2 us; the launch traced here: 92 us
  Pallas kernels  84.2 us (91%)
  local copies, waits for them, and re-layouts  7.15 us (8%)
    pallas_call x1, Pallas kernels, body(): pl.pallas_call(lambda *refs: main_kernel(z, names, *refs), out_shape=[sds...  81.8 us
    reshape x2, local copies, waits for them, and re-layouts, body(): return (outs[0].reshape(shape), outs[1].reshape(shape), *outs[2:])  4.23 us
    pallas_call x1, Pallas kernels, body(): pl.pallas_call(lambda *refs: finish_kernel(z, *refs), out_shape=[sds((z.M...  2.4 us
    reshape x1, local copies, waits for them, and re-layouts, body(): tokens.reshape(z.MB, z.R, z.C)  1.95 us

profile of v2, /device:TPU:0, one launch (start us, length us, event | category | flops | bytes accessed | tf_op | source)
XLA Modules:
  0.0 92.0 jit_solution(710004645046559357)
XLA Ops:
  0.7 0.0 copy-start
  0.7 2.0 %reshape.46.refs_1_ = bf16[2,256,192]{2,1,0:T(8,128)(2,1)} reshape(bf16[2,1,1,49152]{3,0,2,1:T(2,128)(2,1)} %param.18) | data formatting | bytes 393216 | tf_op jit(solution)/shard_map/reshape | solution.py:891
  2.6 0.0 copy-done
  2.6 1.0 %reshape.47.refs_2_ = bf16[2,256,192]{2,1,0:T(8,128)(2,1)} reshape(bf16[2,1,1,49152]{3,0,2,1:T(2,128)(2,1)S(1)} %copy-done) | data formatting | bytes 393216 | tf_op jit(solution)/shard_map/reshape | solution.py:891
  3.6 81.8 %layer.1 = (bf16[2,192,256]{2,1,0:T(8,128)(2,1)}, bf16[2,192,256]{2,1,0:T(8,128)(2,1)}, f32[48,384]{1,0:T(8,128)}, f32[48,384]{1,0:T(8,128)}, f32[96,384]{1,0:T(8,128)}, /*index=5*/f32[16,128]{1,0:T(8,128)}) custom-call(s32[2,1,4]{2,1,0:T(1,128)} %refs_0_.1, bf16[2,256,192]{2,1,0:T(8,128)(2,1)} %reshape.46.refs_1_, bf16[2,256,192]{2,1,0:T(8,128)(2,1)} %reshape.47.refs_2_, ...), custom_call_target="tpu_custom_call" | custom-call | tf_op jit(solution)/shard_map/layer/pallas_call | solution.py:873
  85.3 2.4 %finish.1 = (bf16[2,256,192]{2,1,0:T(8,128)(2,1)}, f32[2,256,192]{2,1,0:T(8,128)}, f32[1,24,192]{2,1,0:T(8,128)}, f32[1,24]{1,0:T(1,128)}, f32[1,24,192]{2,1,0:T...) custom-call(bf16[2,192,256]{2,1,0:T(8,128)(2,1)} %get-tuple-element., ...), custom_call_target="tpu_custom_call" | custom-call | tf_op jit(solution)/shard_map/finish/pallas_call | solution.py:896
  87.7 2.0 %reshape.48 = bf16[2,1,1,49152]{3,0,2,1:T(2,128)(2,1)} reshape(bf16[2,256,192]{2,1,0:T(8,128)(2,1)} %get-tuple-element.46) | data formatting | bytes 393216 | tf_op jit(solution)/shard_map/reshape | solution.py:908
  89.7 2.3 %reshape.50 = f32[2,1,1,49152]{3,2,1,0:T(1,128)} reshape(f32[2,256,192]{2,1,0:T(8,128)} %get-tuple-element.47) | data formatting | bytes 786432 | tf_op jit(solution)/shard_map/reshape | solution.py:908
Async XLA Ops:
  0.7 2.0 %copy-start = (bf16[2,1,1,49152]{3,0,2,1:T(2,128)(2,1)S(1)}, bf16[2,1,1,49152]{3,0,2,1:T(2,128)(2,1)}, u32[]{:S(2)}) copy-start(bf16[2,1,1,49152]{3,0,2,1:T(2,128)(2,1)} %param.20) | copy-start | bytes 589828

commit v3 on v2

v3 whole, which is shorter than its diff:
```python
import types

import jax
import jax.numpy as jnp
from jax import lax
from jax.experimental import pallas as pl
from jax.experimental.pallas import tpu as pltpu
from jax.sharding import PartitionSpec as P

HEAD_DIM = 64
EPS = 1e-05
BIG = 1e30
MESH = pl.DeviceIdType.MESH
F32 = jnp.float32
BF16 = jnp.bfloat16
V_BQ, V_BV, V_BO, V_G1, V_S1, V_BD, V_G2, V_S2 = range(8)
VECS = 16
M_QKV, M_OUT, M_UP, M_DOWN = range(4)


def up_to(n, m):
    return (n + m - 1) // m * m


def mm(a, b):
    return lax.dot_general(a, b, (((1,), (0,)), ((), ())), preferred_element_type=F32)


def mm_nt(a, b):
    return lax.dot_general(a, b, (((1,), (1,)), ((), ())), preferred_element_type=F32)


def loop(n, fn):
    if n <= 8:
        for i in range(n):
            fn(i)
    else:
        lax.fori_loop(0, n, lambda i, c: (fn(i), c)[1], 0)


def rcopy(src, dst, ss, rs, dev):
    return pltpu.make_async_remote_copy(
        src_ref=src, dst_ref=dst, send_sem=ss, recv_sem=rs, device_id=dev, device_id_type=MESH
    )


class Sizes:
    def __init__(self, mesh, tokens, query_weight, up_weight, doc_lengths):
        self.nb, self.nd, self.nh = mesh.shape["blk"], mesh.shape["dp"], mesh.shape["head"]
        self.W = self.nb * self.nd
        self.C, self.F = query_weight.shape[2], up_weight.shape[2]
        self.MB = tokens.shape[0]
        self.R = tokens.shape[3] // self.C
        self.S = self.nb // self.MB
        self.Q = self.MB * self.R
        self.H = self.C // HEAD_DIM
        self.ND = doc_lengths.shape[2]
        self.r = query_weight.shape[1]
        self.rs = up_to(self.r, 8)
        self.r2 = up_to(2 * self.r, 8)
        self.rA = up_to(2 * self.rs, 16)
        self.L = 2 * self.C
        self.keep = self.nb * self.R * self.Q * self.H * 2 <= (8 << 20)
        assert self.F == 4 * self.C and self.F == self.nh * self.C and self.W % self.nh == 0


def main_scratch(z):
    dma = pltpu.SemaphoreType.DMA
    v = pltpu.VMEM
    nb, W, L, R, C, F, Q, H, MB, rA, nh = z.nb, z.W, z.L, z.R, z.C, z.F, z.Q, z.H, z.MB, z.rA, z.nh
    dd = max(z.nd - 1, 1)
    return dict(
        xs=v((MB, C, R), BF16),
        xb=v((nb, C, R), BF16),
        cs=v((MB, C, R), BF16),
        cb=v((MB, C, R), BF16),
        buf=v((4, W, rA, L), BF16),
        wob=v((nh, W // nh, rA, L), BF16),
        fst=v((rA, L), F32),
        vst=v((VECS, 128), F32),
        fkv=v((C + 8, L), F32),
        fq=v((C + 8, L), F32),
        fup=v((C + 16, F), F32),
        fod=v((F + 16, C), F32),
        wkv=v((C, L), BF16),
        wkvt=v((L, C), BF16),
        wq=v((C, C), BF16),
        wqt=v((C, C), BF16),
        wup=v((C, F), BF16),
        wupt=v((F, C + 16), BF16),
        wor=v((C, F), BF16),
        wot=v((C, F), BF16),
        wdn=v((F, C), BF16),
        wdnt=v((C, F), BF16),
        xq=v((C, Q), BF16),
        qx=v((MB, H, 128, R), BF16),
        kx=v((nb, H, HEAD_DIM, R), BF16),
        vx=v((nb, H, HEAD_DIM + 16, R), BF16),
        kt=v((nb, H, R, 128), BF16),
        vt=v((nb, H, R, 128), BF16),
        pbuf=v((MB, H, nb, R, R) if z.keep else (1, 1, 1, 16, 128), BF16),
        mrow=v((MB, H, 8, R), F32),
        oall=v((MB, nh, C, R), BF16),
        pall=v((MB, nh, C, R), BF16),
        stats=v((3, MB, nh, 8, 128), F32),
        n1=v((MB, C, R), F32),
        y1=v((MB, C, R), F32),
        h2=v((MB, C, R), F32),
        gel=v((MB, F, R), F32),
        dh1=v((MB, C, R), F32),
        y1b=v((C, Q), BF16),
        act=v((F, Q), BF16),
        dz=v((C, Q), BF16),
        du=v((F, Q), BF16),
        mo=v((MB, C, R), BF16),
        dox=v((MB, H, 128, R), BF16),
        dqacc=v((MB, H, HEAD_DIM, R), F32),
        dkacc=v((nb - MB if z.keep else 1, L, R), F32),
        dkv=v((L, R), F32),
        dq=v((C, Q), BF16),
        tgs=v((nb, C, R), BF16),
        tgo=v((MB, C, R), F32),
        tgr=v((MB, z.S, C, R), BF16),
        tgx=v((MB, C, R), BF16),
        gkv=v((C + 8, L), F32),
        gq=v((C + 8, L), F32),
        gup=v((C + 8, F), F32),
        gout=v((F + 16, C), F32),
        gdn=v((F + 16, C), F32),
        vg=v((VECS, C), F32),
        ug=v((8, F), F32),
        pk=v((4, W, rA, L), BF16),
        got1=v((4, dd, nb, rA, L), BF16),
        sent2=v((4, nb, rA, L), BF16),
        got2=v((4, nb, rA, L), BF16),
        x_ss=dma((MB,)),
        xf_ss=dma((MB, z.S)),
        x_rs=dma((nb,)),
        c_ss=dma((MB,)),
        c_rs=dma((MB,)),
        g1_ss=dma((4, nb)),
        g1_rs=dma((4, nb)),
        g2_ss=dma((4, dd, nb)),
        g2_rs=dma((4, dd, nb)),
        o_ss=dma((MB, nh)),
        o_rs=dma((MB, nh)),
        p_ss=dma((MB, nh)),
        p_rs=dma((MB, nh)),
        w_ss=dma((nh,)),
        w_rs=dma((nh,)),
        st_ss=dma((3, MB, nh)),
        st_rs=dma((3, MB, nh)),
        mo_ss=dma((MB,)),
        mo_rs=dma((MB,)),
        tp_ss=dma((nb,)),
        tp_rs=dma((MB, z.S)),
        t_ss=dma((MB,)),
        t_rs=dma((MB,)),
        s1_ss=dma((4, dd, nb)),
        s1_rs=dma((4, dd, nb)),
        s2_ss=dma((4, nb)),
        s2_rs=dma((4, nb)),
    )


INPUTS = [
    "lens", "tok", "cot", "wq_in", "bq", "wk_in", "wv_in", "bv", "wo_in", "bo", "g1", "s1", "wup_in", "bu",
    "wdn_in", "bd", "g2", "s2",
]
OUTPUTS = ["o_mo", "o_tg", "o_G"]


def main_kernel(z, names, *refs):
    k = types.SimpleNamespace(**dict(zip(names, refs)))
    nb, nd, nh, W, MB, R, C, F, H, L, S, r, rs, rA = (
        z.nb, z.nd, z.nh, z.W, z.MB, z.R, z.C, z.F, z.H, z.L, z.S, z.r, z.rs, z.rA,
    )
    b, d, h = lax.axis_index("blk"), lax.axis_index("dp"), lax.axis_index("head")
    w_me = b * nd + d
    m_t, s_me = b // S, b % S
    mine = [i * S + s_me for i in range(MB)]
    D = nh * C
    half = nh // 2

    def xor(i):
        return lax.bitwise_xor(h, i)

    def later(e):
        return lax.rem(m_t + e, MB)

    def mate(e):
        return lax.rem(s_me + e, S)

    bar = pltpu.get_barrier_semaphore()
    peers = [(lax.rem(b + i, nb), d, h) for i in range(1, nb)]
    peers += [(b, lax.rem(d + i, nd), h) for i in range(1, nd)]
    peers += [(b, d, xor(i)) for i in range(1, nh)]
    for peer in peers:
        pl.semaphore_signal(bar, inc=1, device_id=peer, device_id_type=MESH)

    def pack(q):
        k.buf[q, w_me] = k.fst[...].astype(BF16)

    k.vst[...] = jnp.zeros_like(k.vst)
    for j, ref in enumerate((k.bq, k.bv, k.bo, k.g1, k.s1, k.bd, k.g2, k.s2)):
        k.vst[j : j + 1, 0:r] = ref[...].astype(F32)
    k.fst[...] = jnp.zeros_like(k.fst)
    k.fst[0:r, 0:C] = k.wk_in[0].astype(F32)
    k.fst[0:r, C:L] = k.wv_in[0].astype(F32)
    k.fst[rs : rs + r, 0:C] = k.wq_in[0].astype(F32)
    k.fst[rs : rs + r, C : C + VECS] = k.vst[...].T[0:r]
    k.fst[rs : rs + 1, C + VECS : C + VECS + 4 * r] = k.bu[...].astype(F32)
    pack(M_QKV)
    for q, src in ((M_OUT, k.wo_in[...]), (M_DOWN, k.wdn_in[0])):
        src = src.astype(F32)
        k.fst[0 : 2 * r, 0:C] = src[0 : 2 * r]
        k.fst[0 : 2 * r, C:L] = src[2 * r : 4 * r]
        pack(q)
    k.fst[0:r] = k.wup_in[0, :, 0:L].astype(F32)
    k.fst[rs : rs + r] = k.wup_in[0, :, L : 2 * L].astype(F32)
    pack(M_UP)

    for m in range(MB):
        k.xs[m] = k.tok[m].T
        k.cs[m] = k.cot[m].T
    k.xb[b] = k.xs[m_t]
    k.cb[m_t] = k.cs[m_t]

    pl.semaphore_wait(bar, len(peers))

    def g1(q, i):
        own = k.buf.at[q, w_me]
        return rcopy(own, own, k.g1_ss.at[q, i], k.g1_rs.at[q, i], (lax.rem(b + i, nb), d, h))

    def g1_wait(q, i):
        src = k.buf.at[q, lax.rem(b + nb - i, nb) * nd + d]
        rcopy(src, src, k.g1_ss.at[q, i], k.g1_rs.at[q, i], (b, d, h)).wait_recv()

    def g2(q, e, i):
        src = k.buf.at[q, lax.rem(b + nb - i, nb) * nd + d]
        return rcopy(src, src, k.g2_ss.at[q, e - 1, i], k.g2_rs.at[q, e - 1, i], (b, lax.rem(d + e, nd), h))

    def g2_wait(q, e, i):
        src = k.buf.at[q, lax.rem(b + nb - i, nb) * nd + lax.rem(d + nd - e, nd)]
        rcopy(src, src, k.g2_ss.at[q, e - 1, i], k.g2_rs.at[q, e - 1, i], (b, d, h)).wait_recv()

    def gather_start(q):
        for e in range(1, nd):
            g2(q, e, 0).start()
        loop(nb - 1, lambda i: g1(q, i + 1).start())

    def gather_forward(q):
        def one(i):
            g1_wait(q, i + 1)
            for e in range(1, nd):
                g2(q, e, i + 1).start()

        loop(nb - 1, one)

    def gather_wait(q):
        for e in range(1, nd):
            loop(nb, lambda i: g2_wait(q, e, i))

    def gather_drain(q):
        loop(nb - 1, lambda i: g1(q, i + 1).wait_send())
        for e in range(1, nd):
            loop(nb, lambda i: g2(q, e, i).wait_send())

    gather_start(M_QKV)

    def x_send(e):
        m = later(e)
        return rcopy(k.xs.at[m], k.xb.at[b], k.x_ss.at[e], k.x_rs.at[b], (m * S + s_me, d, h))

    def x_pass(e, f):
        src = k.xb.at[later(e) * S + s_me]
        return rcopy(src, src, k.xf_ss.at[e, f], k.x_rs.at[later(e) * S + s_me], (m_t * S + mate(f), d, h))

    def x_wait(j):
        rcopy(k.xb.at[j], k.xb.at[j], k.x_ss.at[0], k.x_rs.at[j], (b, d, h)).wait_recv()

    for e in range(1, MB):
        x_send(e).start()
    loop(S - 1, lambda f: x_pass(0, f + 1).start())

    gather_forward(M_QKV)

    for e in range(1, MB):
        x_wait(later(e) * S + s_me)
        loop(S - 1, lambda f: x_pass(e, f + 1).start())
    gather_start(M_OUT)

    gather_wait(M_QKV)

    for w in range(W):
        slab = k.buf[M_QKV, w].astype(F32)
        k.fkv[w * r : w * r + rs] = slab[0:rs]
        k.fq[w * r : w * r + rs] = slab[rs : 2 * rs]
    k.wkv[...] = k.fkv[0:C].astype(BF16)
    k.wkvt[...] = k.fkv[0:C].T.astype(BF16)
    k.wq[...] = k.fq[0:C, 0:C].astype(BF16)
    k.wqt[...] = k.fq[0:C, 0:C].T.astype(BF16)

    def vec(j):
        return k.fq[0:C, C + j : C + j + 1]

    row16 = lax.broadcasted_iota(jnp.int32, (16, R), 0)
    lane = lax.broadcasted_iota(jnp.int32, (16, R), 1)
    pad = jnp.zeros((48, R), BF16)
    one_rows = jnp.where(row16 < 2, 1.0, 0.0).astype(BF16)

    def in_doc(j):
        doc = jnp.zeros((16, R), jnp.int32)
        end = jnp.int32(0)
        for n in range(z.ND):
            end = end + k.lens[m_t, 0, n]
            doc = doc + (j * R + lane >= end).astype(jnp.int32)
        return row16 == doc

    def kv_block(j):
        kv = mm(k.wkvt[...], k.xb[j])
        kb = kv[0:C].astype(BF16)
        vb = (kv[C:L] + vec(V_BV)).astype(BF16)
        barred = jnp.logical_and(row16 < z.ND, jnp.logical_not(in_doc(j)))
        kf = jnp.where(barred, -BIG, 0.0).astype(BF16)
        for a in range(H):
            kh, vh = kb[a * HEAD_DIM : (a + 1) * HEAD_DIM], vb[a * HEAD_DIM : (a + 1) * HEAD_DIM]
            k.kx[j, a] = kh
            k.vx[j, a, 0:HEAD_DIM] = vh
            k.vx[j, a, HEAD_DIM:] = one_rows
            k.kt[j, a] = jnp.concatenate([kh, kf, pad], axis=0).T
            k.vt[j, a] = jnp.concatenate([vh, one_rows, pad], axis=0).T

    def other(n):
        return lax.rem(s_me + 1 + n // MB, S) + lax.rem(m_t + n, MB) * S

    def kv_other(n):
        x_wait(other(n))
        kv_block(other(n))

    for i in range(MB):
        kv_block(mine[i])

    for i in range(MB):
        xi = k.xb[mine[i]]
        k.xq[:, i * R : (i + 1) * R] = xi
        qi = ((mm(k.wqt[...], xi) + vec(V_BQ)).astype(BF16).astype(F32) * HEAD_DIM**-0.5).astype(BF16)
        hot = jnp.where(in_doc(mine[i]), 1.0, 0.0).astype(BF16)
        for a in range(H):
            full = jnp.concatenate([qi[a * HEAD_DIM : (a + 1) * HEAD_DIM], hot, pad], axis=0)
            k.qx[i, a] = full

    loop(nb - MB, kv_other)
    gather_start(M_UP)

    def head_send(net, i, p):
        buf, ss, rs_ = net
        src, to = (h, xor(p)) if p <= half else (xor(half), xor(p - half))
        return rcopy(buf.at[i, src], buf.at[i, src], ss.at[i, p], rs_.at[i, p], (b, d, to))

    def head_wait(net, i, p):
        buf, ss, rs_ = net
        rcopy(buf.at[i, xor(p)], buf.at[i, xor(p)], ss.at[i, p], rs_.at[i, p], (b, d, h)).wait_recv()

    def head_start(net, i):
        for p in range(half, 0, -1):
            head_send(net, i, p).start()

    def head_pass(net, i):
        head_wait(net, i, half)
        for p in range(half + 1, nh):
            head_send(net, i, p).start()

    def head_end(net, i):
        for p in range(1, nh):
            if p != half:
                head_wait(net, i, p)

    o_net = (k.oall, k.o_ss, k.o_rs)
    p_net = (k.pall, k.p_ss, k.p_rs)

    def scores(i, a, j):
        return mm(k.kt[j, a], k.qx[i, a])

    def prob(i, a, j):
        if z.keep:
            return k.pbuf[i, a, j]
        return jnp.exp(scores(i, a, j) - k.mrow[i, a, 0:1]).astype(BF16)

    def attend(i, a):
        if z.keep:
            s = [scores(i, a, j) for j in range(nb)]
            top = jnp.max(s[0], axis=0, keepdims=True)
            for j in range(1, nb):
                top = jnp.maximum(top, jnp.max(s[j], axis=0, keepdims=True))
            o = None
            for j in range(nb):
                e = jnp.exp(s[j] - top).astype(BF16)
                k.pbuf[i, a, j] = e
                o = mm(k.vx[j, a], e) if o is None else o + mm(k.vx[j, a], e)
        else:
            k.mrow[i, a, 0:1] = jnp.full((1, R), -3e38, F32)

            def see(j):
                best = jnp.max(scores(i, a, j), axis=0, keepdims=True)
                k.mrow[i, a, 0:1] = jnp.maximum(k.mrow[i, a, 0:1], best)

            loop(nb, see)
            acc = k.tgo.at[0, 0 : HEAD_DIM + 16]
            acc[...] = jnp.zeros((HEAD_DIM + 16, R), F32)

            def add(j):
                acc[...] += mm(k.vx[j, a], prob(i, a, j))

            loop(nb, add)
            o = acc[...]
        inv = 1.0 / o[HEAD_DIM : HEAD_DIM + 1]
        k.mrow[i, a, 2:3] = inv
        k.oall[i, h, a * HEAD_DIM : (a + 1) * HEAD_DIM] = (o[0:HEAD_DIM] * inv).astype(BF16)

    for i in range(MB):
        for a in range(H):
            attend(i, a)
        head_start(o_net, i)
    gather_start(M_DOWN)

    def c_send(e):
        m = later(e)
        return rcopy(k.cs.at[m], k.cb.at[m_t], k.c_ss.at[e], k.c_rs.at[m_t], (m * S + s_me, d, h))

    for e in range(1, MB):
        c_send(e).start()

    gather_forward(M_OUT)
    gather_forward(M_UP)
    for i in range(MB):
        head_pass(o_net, i)
    gather_wait(M_OUT)

    per = W // nh

    def w_send(p):
        src = k.buf.at[M_OUT, pl.ds(xor(p) * per, per)]
        return rcopy(src, k.wob.at[h], k.w_ss.at[p], k.w_rs.at[p], (b, d, xor(p)))

    for p in range(1, nh):
        w_send(p).start()

    def spread(dst, slab, row):
        slab = slab.astype(F32)
        dst[row : row + z.r2] = slab[0 : z.r2, 0:C]
        dst[row + 2 * r : row + 2 * r + z.r2] = slab[0 : z.r2, C:L]

    for w in range(W):
        spread(k.fod, k.buf[M_OUT, w], 4 * r * w)
    k.wot[...] = k.fod[0:F].T.astype(BF16)

    gather_forward(M_DOWN)

    lane_rows = R // 128

    def st_send(e, i, p):
        own = k.stats.at[e, i, h]
        return rcopy(own, own, k.st_ss.at[e, i, p], k.st_rs.at[e, i, p], (b, d, xor(p)))

    def reduce_start(e, i, rows):
        for j, v in enumerate(rows):
            row = jnp.sum(v, axis=0, keepdims=True)
            for c in range(lane_rows):
                k.stats[e, i, h, pl.ds(j * lane_rows + c, 1)] = row[:, c * 128 : (c + 1) * 128]
        if len(rows) * lane_rows < 8:
            rest = 8 - len(rows) * lane_rows
            k.stats[e, i, h, pl.ds(8 - rest, rest)] = jnp.zeros((rest, 128), F32)
        for p in range(nh - 1, 0, -1):
            st_send(e, i, p).start()

    def reduce_end(e, i, n):
        for p in range(1, nh):
            src = k.stats.at[e, i, xor(p)]
            rcopy(src, src, k.st_ss.at[e, i, p], k.st_rs.at[e, i, p], (b, d, h)).wait_recv()
        total = k.stats[e, i, 0]
        for j in range(1, nh):
            total = total + k.stats[e, i, j]
        total = total / D
        return [
            jnp.concatenate([total[j * lane_rows + c :][0:1] for c in range(lane_rows)], axis=1)
            for j in range(n)
        ]

    def cols(ref, i):
        return ref[:, i * R : (i + 1) * R]

    for i in range(MB):
        head_end(o_net, i)
        h1 = cols(k.xq, i).astype(F32) + mm(k.wot[...], k.oall[i].reshape(D, R)) + vec(V_BO)
        k.n1[i] = h1
        reduce_start(0, i, (h1, h1 * h1))

    gather_wait(M_UP)
    for w in range(W):
        slab = k.buf[M_UP, w].astype(F32)
        k.fup[w * r : w * r + rs, 0:L] = slab[0:rs]
        k.fup[w * r : w * r + rs, L:F] = slab[rs : 2 * rs]
    k.fup[C : C + 16] = jnp.zeros((16, F), F32)
    for w in range(W):
        row = k.buf[M_QKV, w].astype(F32)[rs : rs + 1, C + VECS : C + VECS + 4 * r]
        k.fup[C : C + 1, 4 * r * w : 4 * r * (w + 1)] = row
    k.wup[...] = k.fup[0:C].astype(BF16)
    k.wupt[...] = k.fup[...].T.astype(BF16)
    gather_wait(M_DOWN)
    for w in range(W):
        spread(k.fod, k.buf[M_DOWN, w], 4 * r * w)
    k.wdn[...] = k.fod[0:F].astype(BF16)
    k.wdnt[...] = k.fod[0:F].T.astype(BF16)

    first_one = jnp.where(row16 < 1, 1.0, 0.0).astype(BF16)
    r1 = [None] * MB
    gdn = [None] * MB
    for i in range(MB):
        mean, square = reduce_end(0, i, 2)
        r1[i] = lax.rsqrt(square - mean * mean + EPS)
        n1 = (k.n1[i] - mean) * r1[i]
        k.n1[i] = n1
        y1 = n1 * vec(V_G1) + vec(V_S1)
        k.y1[i] = y1
        y1b = y1.astype(BF16)
        k.y1b[:, i * R : (i + 1) * R] = y1b
        u = mm(k.wupt[...], jnp.concatenate([y1b, first_one], axis=0))
        cdf = 0.5 * (1.0 + lax.erf(u * (0.5**0.5)))
        act = (u * cdf).astype(BF16)
        k.act[:, i * R : (i + 1) * R] = act
        h2 = y1 + mm(k.wdnt[...], act) + vec(V_BD)
        k.h2[i] = h2

        @pl.when(m_t != i)
        def _():
            rcopy(k.cb.at[i], k.cb.at[i], k.c_ss.at[0], k.c_rs.at[i], (b, d, h)).wait_recv()

        dn2 = k.cb[i].astype(F32) * vec(V_G2)
        reduce_start(1, i, (h2, h2 * h2, dn2, dn2 * h2))
        k.gel[i] = cdf + u * jnp.exp(-0.5 * u * u) * ((2 * jnp.pi) ** -0.5)
    k.vg[...] = jnp.zeros_like(k.vg)
    ones = jnp.ones((16, R), BF16)

    def vec_grad(j, x):
        k.vg[j : j + 1] += mm_nt(ones, x)[0:1]

    def mo_send(i):
        return rcopy(k.mo.at[i], k.o_mo.at[m_t], k.mo_ss.at[i], k.mo_rs.at[m_t], (mine[i], d, h))

    for i in range(MB):
        mean, square, dmean, dsquare = reduce_end(1, i, 4)
        r2 = lax.rsqrt(square - mean * mean + EPS)
        g = k.cb[i].astype(F32)
        dn2 = g * vec(V_G2)
        n2 = (k.h2[i] - mean) * r2
        dh2 = r2 * (dn2 - dmean - n2 * (r2 * (dsquare - mean * dmean)))
        dz = dh2.astype(BF16)
        k.dz[:, i * R : (i + 1) * R] = dz
        du = (mm(k.wdn[...], dz) * k.gel[i]).astype(BF16)
        k.du[:, i * R : (i + 1) * R] = du
        dy1 = dh2 + mm(k.wup[...], du)
        dn1 = dy1 * vec(V_G1)
        k.dh1[i] = dn1
        n1 = k.n1[i]
        reduce_start(2, i, (dn1, dn1 * n1))
        k.mo[i] = (n2 * vec(V_G2) + vec(V_S2)).astype(BF16)

        @pl.when(m_t != i)
        def _():
            mo_send(i).start()

        @pl.when(m_t == i)
        def _():
            k.o_mo[m_t] = k.mo[i]

        vec_grad(V_G2, (g * n2).astype(BF16))
        vec_grad(V_S2, k.cb[i])
        vec_grad(V_BD, dz)
        vec_grad(V_G1, (dy1 * n1).astype(BF16))
        vec_grad(V_S1, dy1.astype(BF16))

    def s1_send(q, e, i):
        dt = lax.rem(d + e, nd)
        return rcopy(
            k.pk.at[q, i * nd + dt], k.got1.at[q, e - 1, i], k.s1_ss.at[q, e - 1, i], k.s1_rs.at[q, e - 1, i],
            (b, dt, h),
        )

    def s2_send(q, i):
        bt = lax.rem(b + i, nb)
        return rcopy(k.sent2.at[q, bt], k.got2.at[q, b], k.s2_ss.at[q, i], k.s2_rs.at[q, i], (bt, d, h))

    def scatter_start(q):
        for e in range(1, nd):
            loop(nb, lambda i: s1_send(q, e, i).start())

    def scatter_sum(q, bt):
        part = k.pk[q, bt * nd + d].astype(F32)
        for e in range(1, nd):
            src = k.got1.at[q, e - 1, bt]
            rcopy(src, src, k.s1_ss.at[q, e - 1, bt], k.s1_rs.at[q, e - 1, bt], (b, d, h)).wait_recv()
            part = part + src[...].astype(F32)
        return part

    def scatter_forward(q):
        def one(i):
            bt = lax.rem(b + i + 1, nb)
            k.sent2[q, bt] = scatter_sum(q, bt).astype(BF16)
            s2_send(q, i + 1).start()

        loop(nb - 1, one)
        k.o_G[q] = scatter_sum(q, b)

    def scatter_end(q):
        def one(i):
            src = k.got2.at[q, lax.rem(b + nb - i - 1, nb)]
            rcopy(src, src, k.s2_ss.at[q, i + 1], k.s2_rs.at[q, i + 1], (b, d, h)).wait_recv()
            k.o_G[q] += src[...].astype(F32)

        loop(nb - 1, one)
        loop(nb - 1, lambda i: s2_send(q, i + 1).wait_send())
        for e in range(1, nd):
            loop(nb, lambda i: s1_send(q, e, i).wait_send())

    def rows_of(parts):
        rows = jnp.concatenate(parts, axis=0)
        if rows.shape[0] < rA:
            rows = jnp.concatenate([rows, jnp.zeros((rA - rows.shape[0], L), F32)], axis=0)
        return rows.astype(BF16)

    def pack_halves(q, g):
        for w in range(W):
            at = 4 * r * w
            pair = jnp.concatenate([g[at : at + z.r2], g[at + 2 * r : at + 2 * r + z.r2]], axis=1)
            k.pk[q, w] = rows_of([pair])
        scatter_start(q)

    k.gdn[0:F] = mm_nt(k.act[...], k.dz[...])
    pack_halves(M_DOWN, k.gdn)
    k.gup[0:C] = mm_nt(k.y1b[...], k.du[...])
    for w in range(W):
        k.pk[M_UP, w] = rows_of([k.gup[w * r : w * r + rs, 0:L], k.gup[w * r : w * r + rs, L:F]])
    scatter_start(M_UP)

    for i in range(MB):
        dmean, dsquare = reduce_end(2, i, 2)
        dh1 = r1[i] * (k.dh1[i] - dmean - k.n1[i] * dsquare)
        k.dh1[i] = dh1
        dp = dh1.astype(BF16)
        k.pall[i, h] = dp
        head_start(p_net, i)

    g = None
    for i in range(MB):
        dp = k.pall[i, h]
        part = mm_nt(k.oall[i].reshape(D, R), dp)
        g = part if g is None else g + part
        vec_grad(V_BO, dp)
    k.gout[0:F] = g
    pack_halves(M_OUT, k.gout)
    ug = mm_nt(jnp.ones((16, z.Q), BF16), k.du[...])
    k.gq[...] = jnp.zeros_like(k.gq)
    for w in range(W):
        k.gq[w * r : w * r + 1, C + VECS : C + VECS + 4 * r] = ug[0:1, 4 * r * w : 4 * r * (w + 1)]
    k.gkv[...] = jnp.zeros_like(k.gkv)

    for p in range(1, nh):
        src = k.wob.at[xor(p)]
        rcopy(src, src, k.w_ss.at[p], k.w_rs.at[p], (b, d, h)).wait_recv()
    k.wob[h] = k.buf[M_OUT, pl.ds(h * per, per)]
    for j in range(nh):
        for n in range(per):
            spread(k.fod, k.wob[j, n], j * C + 4 * r * n)
    for j in range(nh):
        k.wor[:, j * C : (j + 1) * C] = k.fod[j * C : (j + 1) * C].astype(BF16)

    head_pass(p_net, 0)
    scatter_forward(M_DOWN)
    for i in range(1, MB):
        head_pass(p_net, i)

    def grad_in(i):
        head_end(p_net, i)
        do = mm(k.wor[...], k.pall[i].reshape(D, R)).astype(BF16).astype(F32)
        for a in range(H):
            part = do[a * HEAD_DIM : (a + 1) * HEAD_DIM] * k.mrow[i, a, 2:3]
            own = k.oall[i, h, a * HEAD_DIM : (a + 1) * HEAD_DIM].astype(F32)
            delta = jnp.sum(part * own, axis=0, keepdims=True)
            hi = delta.astype(BF16).astype(F32)
            rest = jnp.where(row16 == 0, -hi, jnp.where(row16 == 1, hi - delta, 0.0))
            full = jnp.concatenate([part.astype(BF16), rest.astype(BF16), pad], axis=0)
            k.dox[i, a] = full
            k.dqacc[i, a] = jnp.zeros((HEAD_DIM, R), F32)

    def back(j, queries, into):
        for a in range(H):
            dk = dv = None
            for i in queries:
                p = prob(i, a, j)
                ds = (p.astype(F32) * mm(k.vt[j, a], k.dox[i, a])).astype(BF16)
                k.dqacc[i, a] += mm(k.kx[j, a], ds)
                dk_i, dv_i = mm_nt(k.qx[i, a, 0:HEAD_DIM], ds), mm_nt(k.dox[i, a, 0:HEAD_DIM], p)
                dk = dk_i if dk is None else dk + dk_i
                dv = dv_i if dv is None else dv + dv_i
            into(slice(a * HEAD_DIM, (a + 1) * HEAD_DIM), dk)
            into(slice(C + a * HEAD_DIM, C + (a + 1) * HEAD_DIM), dv)

    def tokens_part(j, dkv):
        k.gkv[0:C] += mm_nt(k.xb[j], dkv)
        vec_grad(V_BV, dkv[C:L])
        return mm(k.wkv[...], dkv)

    def tp_send(n):
        j = other(n)
        slot = j // S
        return rcopy(k.tgs.at[j], k.tgr.at[slot, s_me], k.tp_ss.at[j], k.tp_rs.at[slot, s_me], (m_t * S + j % S, d, h))

    def back_other(n, queries):
        slot = n if z.keep else 0

        def into(rows, v):
            if queries[0] == 0:
                k.dkacc[slot, rows] = v
            else:
                k.dkacc[slot, rows] += v

        back(other(n), queries, into)
        if queries[-1] == MB - 1:
            k.tgs[other(n)] = tokens_part(other(n), k.dkacc[slot].astype(BF16)).astype(BF16)
            tp_send(n).start()

    for i in range(MB):
        grad_in(i)
        if z.keep:
            loop(nb - MB, lambda n: back_other(n, [i]))
        if i == 0:
            scatter_forward(M_UP)
    if not z.keep:
        loop(nb - MB, lambda n: back_other(n, list(range(MB))))

    for i in range(MB):

        def into(rows, v):
            k.dkv[rows] = v

        back(mine[i], range(MB), into)
        k.tgo[i] = tokens_part(mine[i], k.dkv[...].astype(BF16))
        if i == 0:
            scatter_forward(M_OUT)

    for i in range(MB):
        for a in range(H):
            rows = slice(a * HEAD_DIM, (a + 1) * HEAD_DIM)
            k.dq[rows, i * R : (i + 1) * R] = (k.dqacc[i, a] * HEAD_DIM**-0.5).astype(BF16)
        vec_grad(V_BQ, cols(k.dq, i))
    k.gq[0:C, 0:C] = mm_nt(k.xq[...], k.dq[...])
    k.gq[0:C, C : C + VECS] = k.vg[...].T

    for w in range(W):
        k.pk[M_QKV, w] = rows_of([k.gkv[w * r : w * r + rs], k.gq[w * r : w * r + rs]])
    scatter_start(M_QKV)

    def t_send(i):
        return rcopy(k.tgx.at[i], k.o_tg.at[m_t], k.t_ss.at[i], k.t_rs.at[m_t], (mine[i], d, h))

    for i in range(MB):
        k.tgo[i] += k.dh1[i] + mm(k.wq[...], cols(k.dq, i))

        def add(f):
            src = k.tgr.at[i, mate(f + 1)]
            rcopy(src, src, k.tp_ss.at[0], k.tp_rs.at[i, mate(f + 1)], (b, d, h)).wait_recv()
            k.tgo[i] += src[...].astype(F32)

        loop(S - 1, add)
        k.tgx[i] = k.tgo[i].astype(BF16)

        @pl.when(m_t != i)
        def _():
            t_send(i).start()

        @pl.when(m_t == i)
        def _():
            k.o_tg[m_t] = k.tgx[i]

    scatter_forward(M_QKV)

    for q in (M_DOWN, M_UP, M_OUT, M_QKV):
        scatter_end(q)
    for e in range(1, MB):
        m = later(e)
        for out, ss, rs_ in ((k.o_tg, k.t_ss, k.t_rs), (k.o_mo, k.mo_ss, k.mo_rs)):
            rcopy(out.at[m], out.at[m], ss.at[m], rs_.at[m], (b, d, h)).wait_recv()
        c_send(e).wait_send()
        x_send(e).wait_send()
        mo_send_e = rcopy(k.mo.at[m], k.o_mo.at[m_t], k.mo_ss.at[m], k.mo_rs.at[m_t], (b, d, h))
        mo_send_e.wait_send()
        t_send_e = rcopy(k.tgx.at[m], k.o_tg.at[m_t], k.t_ss.at[m], k.t_rs.at[m_t], (b, d, h))
        t_send_e.wait_send()
    for e in range(MB):
        loop(S - 1, lambda f: x_pass(e, f + 1).wait_send())
    loop(nb - MB, lambda n: tp_send(n).wait_send())
    for q in range(4):
        gather_drain(q)
    for p in range(1, nh):
        w_send(p).wait_send()
        for i in range(MB):
            head_send(o_net, i, p).wait_send()
            head_send(p_net, i, p).wait_send()
            for e in range(3):
                st_send(e, i, p).wait_send()


def finish_kernel(z, mo, tg, G, *outs):
    (mixed, dtok, dwq, dbq, dwk, dwv, dbv, dwo, dbo, dg1, ds1, dwup, dbu, dwdn, dbd, dg2, ds2) = outs
    r, rs, C, L = z.r, z.rs, z.C, z.L
    for m in range(z.MB):
        mixed[m] = mo[m].T
        dtok[m] = tg[m].astype(F32).T
    dwk[0] = G[M_QKV, 0:r, 0:C]
    dwv[0] = G[M_QKV, 0:r, C:L]
    dwq[0] = G[M_QKV, rs : rs + r, 0:C]
    dwup[0, :, 0:L] = G[M_UP, 0:r]
    dwup[0, :, L : 2 * L] = G[M_UP, rs : rs + r]
    for q, ref in ((M_OUT, dwo), (M_DOWN, dwdn.at[0])):
        ref[0 : 2 * r] = G[q, 0 : 2 * r, 0:C]
        ref[2 * r : 4 * r] = G[q, 0 : 2 * r, C:L]
    vecs = G[M_QKV, rs : 2 * rs, C : C + VECS].T
    for j, ref in enumerate((dbq, dbv, dbo, dg1, ds1, dbd, dg2, ds2)):
        ref[...] = vecs[j : j + 1, 0:r]
    dbu[...] = G[M_QKV, rs : rs + 1, C + VECS : C + VECS + 4 * r]


def solution(mesh):
    vec_spec = P("head", ("blk", "dp"))
    mat_spec = P("head", ("blk", "dp"), None)
    tok_spec = P(None, "dp", "head", "blk")
    out_spec = P(("blk", "dp"), "head")

    def body(
        tokens, doc_lengths, cotangent, query_weight, query_bias, key_weight, value_weight, value_bias,
        out_weight, out_bias, first_gain, first_shift, up_weight, up_bias, down_weight, down_bias,
        second_gain, second_shift,
    ):
        z = Sizes(mesh, tokens, query_weight, up_weight, doc_lengths)
        scratch = main_scratch(z)
        vmem = pl.BlockSpec(memory_space=pltpu.VMEM)
        smem = pl.BlockSpec(memory_space=pltpu.SMEM)
        names = INPUTS + OUTPUTS + list(scratch)
        sds = jax.ShapeDtypeStruct
        parts = pl.pallas_call(
            lambda *refs: main_kernel(z, names, *refs),
            out_shape=[
                sds((z.MB, z.C, z.R), BF16),
                sds((z.MB, z.C, z.R), BF16),
                sds((4, z.rA, z.L), F32),
            ],
            in_specs=[smem] + [vmem] * (len(INPUTS) - 1),
            out_specs=[vmem] * len(OUTPUTS),
            scratch_shapes=list(scratch.values()),
            compiler_params=pltpu.CompilerParams(
                collective_id=0, has_side_effects=True, vmem_limit_bytes=63 << 20
            ),
            name="layer",
        )(
            doc_lengths, tokens.reshape(z.MB, z.R, z.C), cotangent.reshape(z.MB, z.R, z.C), query_weight,
            query_bias, key_weight, value_weight, value_bias, out_weight, out_bias, first_gain, first_shift,
            up_weight, up_bias, down_weight, down_bias, second_gain, second_shift,
        )
        mat, vec = sds((1, z.r, z.C), F32), sds((1, z.r), F32)
        outs = pl.pallas_call(
            lambda *refs: finish_kernel(z, *refs),
            out_shape=[
                sds((z.MB, z.R, z.C), BF16), sds((z.MB, z.R, z.C), F32), mat, vec, mat, mat, vec,
                sds((4 * z.r, z.C), F32), vec, vec, vec, sds((1, z.r, z.F), F32), sds((1, 4 * z.r), F32),
                sds((1, 4 * z.r, z.C), F32), vec, vec, vec,
            ],
            in_specs=[vmem] * len(OUTPUTS),
            out_specs=[vmem] * 17,
            name="finish",
        )(*parts)
        shape = tokens.shape
        return (outs[0].reshape(shape), outs[1].reshape(shape), *outs[2:])

    return jax.shard_map(
        body,
        mesh=mesh,
        in_specs=(
            tok_spec, P(None, "dp", None), tok_spec, mat_spec, vec_spec, mat_spec, mat_spec, vec_spec,
            out_spec, vec_spec, vec_spec, vec_spec, mat_spec, vec_spec, mat_spec, vec_spec, vec_spec, vec_spec,
        ),
        out_specs=(
            tok_spec, tok_spec, mat_spec, vec_spec, mat_spec, mat_spec, vec_spec, out_spec, vec_spec, vec_spec,
            vec_spec, mat_spec, vec_spec, mat_spec, vec_spec, vec_spec, vec_spec,
        ),
        check_vma=False,
    )
```

time: 92.2 us -> 81.1 us (0.88)
  Pallas kernels: 84.2 us -> 73 us
    pallas_call x1, Pallas kernels: 81.8 us -> 70.6 us  [body(): pl.pallas_call(lambda *refs: main_kernel(z, names, *refs), out_shape=[sds...]
where the time goes in v3:
time: 81.1 us; the launch traced here: 80.8 us
  Pallas kernels  73 us (90%)
  local copies, waits for them, and re-layouts  7.15 us (9%)
    pallas_call x1, Pallas kernels, body(): pl.pallas_call(lambda *refs: main_kernel(z, names, *refs), out_shape=[sds...  70.6 us
    reshape x2, local copies, waits for them, and re-layouts, body(): return (outs[0].reshape(shape), outs[1].reshape(shape), *outs[2:])  4.23 us
    pallas_call x1, Pallas kernels, body(): pl.pallas_call(lambda *refs: finish_kernel(z, *refs), out_shape=[sds((z.M...  2.38 us
    reshape x1, local copies, waits for them, and re-layouts, body(): tokens.reshape(z.MB, z.R, z.C)  1.95 us

profile of v3, /device:TPU:0, one launch (start us, length us, event | category | flops | bytes accessed | tf_op | source)
XLA Modules:
  0.0 80.8 jit_solution(15806959313942037967)
XLA Ops:
  0.7 0.0 copy-start
  0.7 2.0 %reshape.46.refs_1_ = bf16[2,256,192]{2,1,0:T(8,128)(2,1)} reshape(bf16[2,1,1,49152]{3,0,2,1:T(2,128)(2,1)} %param.18) | data formatting | bytes 393216 | tf_op jit(solution)/shard_map/reshape | solution.py:866
  2.6 0.0 copy-done
  2.6 1.0 %reshape.47.refs_2_ = bf16[2,256,192]{2,1,0:T(8,128)(2,1)} reshape(bf16[2,1,1,49152]{3,0,2,1:T(2,128)(2,1)S(1)} %copy-done) | data formatting | bytes 393216 | tf_op jit(solution)/shard_map/reshape | solution.py:866
  3.6 70.6 %layer.1 = (bf16[2,192,256]{2,1,0:T(8,128)(2,1)}, bf16[2,192,256]{2,1,0:T(8,128)(2,1)}, f32[4,48,384]{2,1,0:T(8,128)}) custom-call(s32[2,1,4]{2,1,0:T(1,128)} %refs_0_.1, bf16[2,256,192]{2,1,0:T(8,128)(2,1)} %reshape.46.refs_1_, bf16[2,256,192]{2,1,0:T(8,128)(2,1)} %reshape.47.refs_2_, bf16[1,24,192]{2,1,0:T(8,128)(2,1)} %refs_3_.1, bf16[1,24]{1,0:T(2,128)(2,1)} %refs_4_.1, ...), custom_call_target="tpu_custom_call" | custom-call | tf_op jit(solution)/shard_map/layer/pallas_call | solution.py:851
  74.2 2.4 %finish.1 = (bf16[2,256,192]{2,1,0:T(8,128)(2,1)}, f32[2,256,192]{2,1,0:T(8,128)}, f32[1,24,192]{2,1,0:T(8,128)}, f32[1,24]{1,0:T(1,128)}, f32[1,24,192]{2,1,0:T...) custom-call(bf16[2,192,256]{2,1,0:T(8,128)(2,1)} %get-tuple-element., ...), custom_call_target="tpu_custom_call" | custom-call | tf_op jit(solution)/shard_map/finish/pallas_call | solution.py:871
  76.6 2.0 %reshape.48 = bf16[2,1,1,49152]{3,0,2,1:T(2,128)(2,1)} reshape(bf16[2,256,192]{2,1,0:T(8,128)(2,1)} %get-tuple-element.40) | data formatting | bytes 393216 | tf_op jit(solution)/shard_map/reshape | solution.py:883
  78.5 2.3 %reshape.50 = f32[2,1,1,49152]{3,2,1,0:T(1,128)} reshape(f32[2,256,192]{2,1,0:T(8,128)} %get-tuple-element.41) | data formatting | bytes 786432 | tf_op jit(solution)/shard_map/reshape | solution.py:883
Async XLA Ops:
  0.7 2.0 %copy-start = (bf16[2,1,1,49152]{3,0,2,1:T(2,128)(2,1)S(1)}, bf16[2,1,1,49152]{3,0,2,1:T(2,128)(2,1)}, u32[]{:S(2)}) copy-start(bf16[2,1,1,49152]{3,0,2,1:T(2,128)(2,1)} %param.20) | copy-start | bytes 589828

commit v4 on v3

--- a/solution.py
+++ b/solution.py
@@ -1,3 +1,4 @@
+import math
 import types
 
 import jax
@@ -44,6 +45,36 @@
     )
 
 
+def pieces(c, u):
+    at, end = u * c, (u + 1) * c
+    found = []
+    while at < end:
+        size = min(128 - at % 128, end - at)
+        found.append((at // 128, at % 128, size))
+        at += size
+    return found
+
+
+def columns_of(z, flat):
+    rows = [flat[pl.ds(i, z.R // z.per, stride=z.span)].T for i in range(z.span)]
+    tokens = []
+    for u in range(z.per):
+        tokens.append(jnp.concatenate([rows[i][at : at + n] for i, at, n in pieces(z.C, u)], axis=0))
+    return jnp.concatenate(tokens, axis=1)
+
+
+def put_rows(z, value, put):
+    n = z.R // z.per
+    parts = [[] for _ in range(z.span)]
+    for u in range(z.per):
+        c = 0
+        for i, _, size in pieces(z.C, u):
+            parts[i].append(value[c : c + size, u * n : (u + 1) * n])
+            c += size
+    for i in range(z.span):
+        put(i, jnp.concatenate(parts[i], axis=0).T)
+
+
 class Sizes:
     def __init__(self, mesh, tokens, query_weight, up_weight, doc_lengths):
         self.nb, self.nd, self.nh = mesh.shape["blk"], mesh.shape["dp"], mesh.shape["head"]
@@ -53,6 +84,9 @@
         self.R = tokens.shape[3] // self.C
         self.S = self.nb // self.MB
         self.Q = self.MB * self.R
+        self.N = self.R * self.C // 128
+        self.per = 128 // math.gcd(self.C, 128)
+        self.span = self.per * self.C // 128
         self.H = self.C // HEAD_DIM
         self.ND = doc_lengths.shape[2]
         self.r = query_weight.shape[1]
@@ -70,6 +104,7 @@
     nb, W, L, R, C, F, Q, H, MB, rA, nh = z.nb, z.W, z.L, z.R, z.C, z.F, z.Q, z.H, z.MB, z.rA, z.nh
     dd = max(z.nd - 1, 1)
     return dict(
+        flat=v((2 * MB, z.N, 128), F32),
         xs=v((MB, C, R), BF16),
         xb=v((nb, C, R), BF16),
         cs=v((MB, C, R), BF16),
@@ -220,9 +255,11 @@
     k.fst[rs : rs + r] = k.wup_in[0, :, L : 2 * L].astype(F32)
     pack(M_UP)
 
-    for m in range(MB):
-        k.xs[m] = k.tok[m].T
-        k.cs[m] = k.cot[m].T
+    for n, (src, dst) in enumerate(((k.tok, k.xs), (k.cot, k.cs))):
+        both = src[...].astype(F32)
+        for m in range(MB):
+            k.flat[n * MB + m] = both[:, m]
+            dst[m] = columns_of(z, k.flat.at[n * MB + m]).astype(BF16)
     k.xb[b] = k.xs[m_t]
     k.cb[m_t] = k.cs[m_t]
 
@@ -305,7 +342,9 @@
         return k.fq[0:C, C + j : C + j + 1]
 
     row16 = lax.broadcasted_iota(jnp.int32, (16, R), 0)
-    lane = lax.broadcasted_iota(jnp.int32, (16, R), 1)
+    column = lax.broadcasted_iota(jnp.int32, (16, R), 1)
+    step = R // z.per
+    token = z.per * (column % step) + column // step
     pad = jnp.zeros((48, R), BF16)
     one_rows = jnp.where(row16 < 2, 1.0, 0.0).astype(BF16)
 
@@ -314,7 +353,7 @@
         end = jnp.int32(0)
         for n in range(z.ND):
             end = end + k.lens[m_t, 0, n]
-            doc = doc + (j * R + lane >= end).astype(jnp.int32)
+            doc = doc + (j * R + token >= end).astype(jnp.int32)
         return row16 == doc
 
     def kv_block(j):
@@ -812,11 +851,20 @@
 
 
 def finish_kernel(z, mo, tg, G, *outs):
-    (mixed, dtok, dwq, dbq, dwk, dwv, dbv, dwo, dbo, dg1, ds1, dwup, dbu, dwdn, dbd, dg2, ds2) = outs
+    (mixed, dtok, dwq, dbq, dwk, dwv, dbv, dwo, dbo, dg1, ds1, dwup, dbu, dwdn, dbd, dg2, ds2, both) = outs
     r, rs, C, L = z.r, z.rs, z.C, z.L
     for m in range(z.MB):
-        mixed[m] = mo[m].T
-        dtok[m] = tg[m].astype(F32).T
+
+
+        def put_mixed(i, rows):
+            both[pl.ds(i, z.R // z.per, stride=z.span), m] = rows
+
+        def put_grad(i, rows):
+            dtok[m, pl.ds(i, z.R // z.per, stride=z.span)] = rows
+
+        put_rows(z, mo[m].astype(F32), put_mixed)
+        put_rows(z, tg[m].astype(F32), put_grad)
+    mixed[...] = both[...].astype(BF16)
     dwk[0] = G[M_QKV, 0:r, 0:C]
     dwv[0] = G[M_QKV, 0:r, C:L]
     dwq[0] = G[M_QKV, rs : rs + r, 0:C]
@@ -843,6 +891,10 @@
         second_gain, second_shift,
     ):
         z = Sizes(mesh, tokens, query_weight, up_weight, doc_lengths)
+
+        def as_rows(a):
+            return a.reshape(z.MB, z.N, 128).transpose(1, 0, 2)
+
         scratch = main_scratch(z)
         vmem = pl.BlockSpec(memory_space=pltpu.VMEM)
         smem = pl.BlockSpec(memory_space=pltpu.SMEM)
@@ -863,7 +915,7 @@
             ),
             name="layer",
         )(
-            doc_lengths, tokens.reshape(z.MB, z.R, z.C), cotangent.reshape(z.MB, z.R, z.C), query_weight,
+            doc_lengths, as_rows(tokens), as_rows(cotangent), query_weight,
             query_bias, key_weight, value_weight, value_bias, out_weight, out_bias, first_gain, first_shift,
             up_weight, up_bias, down_weight, down_bias, second_gain, second_shift,
         )
@@ -871,16 +923,17 @@
         outs = pl.pallas_call(
             lambda *refs: finish_kernel(z, *refs),
             out_shape=[
-                sds((z.MB, z.R, z.C), BF16), sds((z.MB, z.R, z.C), F32), mat, vec, mat, mat, vec,
+                sds((z.N, z.MB, 128), BF16), sds((z.MB, z.N, 128), F32), mat, vec, mat, mat, vec,
                 sds((4 * z.r, z.C), F32), vec, vec, vec, sds((1, z.r, z.F), F32), sds((1, 4 * z.r), F32),
                 sds((1, 4 * z.r, z.C), F32), vec, vec, vec,
             ],
             in_specs=[vmem] * len(OUTPUTS),
             out_specs=[vmem] * 17,
+            scratch_shapes=[pltpu.VMEM((z.N, z.MB, 128), F32)],
             name="finish",
         )(*parts)
         shape = tokens.shape
-        return (outs[0].reshape(shape), outs[1].reshape(shape), *outs[2:])
+        return (outs[0].transpose(1, 0, 2).reshape(shape), outs[1].reshape(shape), *outs[2:])
 
     return jax.shard_map(
         body,

time: 81.1 us -> 74.2 us (0.915)
  local copies, waits for them, and re-layouts: 7.15 us -> 0 us
    reshape x4 -> x0, local copies, waits for them, and re-layouts: 7.15 us -> none  [the longest x2 4.23 us: body(): return (outs[0].reshape(shape), outs[1].reshape(shape), *outs[2:])]
where the time goes in v4:
time: 74.2 us; the launch traced here: 74 us
  Pallas kernels  73.2 us (99%)
  between operations  0.83 us (1%)
    pallas_call x1, Pallas kernels, body(): pl.pallas_call(lambda *refs: main_kernel(z, names, *refs), out_shape=[sds...  70.6 us
    pallas_call x1, Pallas kernels, body(): pl.pallas_call(lambda *refs: finish_kernel(z, *refs), out_shape=[sds((z.N...  2.58 us

profile of v4, /device:TPU:0, one launch (start us, length us, event | category | flops | bytes accessed | tf_op | source)
XLA Modules:
  0.0 74.0 jit_solution(5141363397022218906)
XLA Ops:
  0.7 70.6 %layer.1 = (bf16[2,192,256]{2,1,0:T(8,128)(2,1)}, bf16[2,192,256]{2,1,0:T(8,128)(2,1)}, f32[4,48,384]{2,1,0:T(8,128)}) custom-call(s32[2,1,4]{2,1,0:T(1,128)} %refs_0_.1, bf16[384,2,128]{2,1,0:T(2,128)(2,1)} %bitcast.10, bf16[384,2,128]{2,1,0:T(2,128)(2,1)} %bitcast.11, bf16[1,24,192]{2,1,0:T(8,128)(2,1)} %refs_3_.1, bf16[1,24]{1,0:T(2,128)(2,1)} %refs_4_.1, ...), custom_call_target="tpu_custom_call" | custom-call | tf_op jit(solution)/shard_map/layer/pallas_call | solution.py:903
  71.3 2.6 %finish.1 = (bf16[384,2,128]{2,1,0:T(2,128)(2,1)}, f32[2,384,128]{2,1,0:T(8,128)}, f32[1,24,192]{2,1,0:T(8,128)}, f32[1,24]{1,0:T(1,128)}, f32[1,24,192]{2,1,0:T...) custom-call(bf16[2,192,256]{2,1,0:T(8,128)(2,1)} %get-tuple-element., ...), custom_call_target="tpu_custom_call" | custom-call | tf_op jit(solution)/shard_map/finish/pallas_call | solution.py:923

commit v5 on v4

--- a/solution.py
+++ b/solution.py
@@ -98,12 +98,20 @@
         assert self.F == 4 * self.C and self.F == self.nh * self.C and self.W % self.nh == 0
 
 
-def main_scratch(z):
+INPUTS = [
+    "lens", "tok", "cot", "wq_in", "bq", "wk_in", "wv_in", "bv", "wo_in", "bo", "g1", "s1", "wup_in", "bu",
+    "wdn_in", "bd", "g2", "s2",
+]
+OUTPUTS = ["o_mo", "o_tg", "o_G"]
+
+
+def main_scratch(z, inputs):
     dma = pltpu.SemaphoreType.DMA
     v = pltpu.VMEM
     nb, W, L, R, C, F, Q, H, MB, rA, nh = z.nb, z.W, z.L, z.R, z.C, z.F, z.Q, z.H, z.MB, z.rA, z.nh
     dd = max(z.nd - 1, 1)
     return dict(
+        in_sem=dma((len(INPUTS) - 1,)),
         flat=v((2 * MB, z.N, 128), F32),
         xs=v((MB, C, R), BF16),
         xb=v((nb, C, R), BF16),
@@ -133,8 +141,10 @@
         vx=v((nb, H, HEAD_DIM + 16, R), BF16),
         kt=v((nb, H, R, 128), BF16),
         vt=v((nb, H, R, 128), BF16),
-        pbuf=v((MB, H, nb, R, R) if z.keep else (1, 1, 1, 16, 128), BF16),
-        mrow=v((MB, H, 8, R), F32),
+        pbuf=v((nb, MB, H, R, R) if z.keep else (1, 1, 1, 16, 128), BF16),
+        tops=v((MB, H, up_to(nb, 8), R), F32),
+        top=v((MB, H, 8, R), F32),
+        osum=v((MB, H, HEAD_DIM + 16, R), F32),
         oall=v((MB, nh, C, R), BF16),
         pall=v((MB, nh, C, R), BF16),
         stats=v((3, MB, nh, 8, 128), F32),
@@ -148,7 +158,9 @@
         dz=v((C, Q), BF16),
         du=v((F, Q), BF16),
         mo=v((MB, C, R), BF16),
-        dox=v((MB, H, 128, R), BF16),
+        dox=v((nb if z.keep else 1, MB, H, 128, R), BF16),
+        part=v((MB, H, HEAD_DIM, R), F32),
+        delta=v((MB, H, 8, R), F32),
         dqacc=v((MB, H, HEAD_DIM, R), F32),
         dkacc=v((nb - MB if z.keep else 1, L, R), F32),
         dkv=v((L, R), F32),
@@ -195,14 +207,8 @@
         s1_rs=dma((4, dd, nb)),
         s2_ss=dma((4, nb)),
         s2_rs=dma((4, nb)),
+        **{"v_" + name: v(a.shape, a.dtype) for name, a in zip(INPUTS[1:], inputs)},
     )
-
-
-INPUTS = [
-    "lens", "tok", "cot", "wq_in", "bq", "wk_in", "wv_in", "bv", "wo_in", "bo", "g1", "s1", "wup_in", "bu",
-    "wdn_in", "bd", "g2", "s2",
-]
-OUTPUTS = ["o_mo", "o_tg", "o_G"]
 
 
 def main_kernel(z, names, *refs):
@@ -213,7 +219,6 @@
     b, d, h = lax.axis_index("blk"), lax.axis_index("dp"), lax.axis_index("head")
     w_me = b * nd + d
     m_t, s_me = b // S, b % S
-    mine = [i * S + s_me for i in range(MB)]
     D = nh * C
     half = nh // 2
 
@@ -223,8 +228,21 @@
     def later(e):
         return lax.rem(m_t + e, MB)
 
+    def home(e):
+        return later(e) * S + s_me
+
     def mate(e):
         return lax.rem(s_me + e, S)
+
+    def other(n):
+        return lax.rem(s_me + 1 + n // MB, S) + lax.rem(m_t + n, MB) * S
+
+    fetch = [
+        pltpu.make_async_copy(getattr(k, name), getattr(k, "v_" + name), k.in_sem.at[n])
+        for n, name in enumerate(INPUTS[1:])
+    ]
+    for copy in fetch:
+        copy.start()
 
     bar = pltpu.get_barrier_semaphore()
     peers = [(lax.rem(b + i, nb), d, h) for i in range(1, nb)]
@@ -233,35 +251,38 @@
     for peer in peers:
         pl.semaphore_signal(bar, inc=1, device_id=peer, device_id_type=MESH)
 
+    for copy in fetch:
+        copy.wait()
+
     def pack(q):
         k.buf[q, w_me] = k.fst[...].astype(BF16)
 
     k.vst[...] = jnp.zeros_like(k.vst)
-    for j, ref in enumerate((k.bq, k.bv, k.bo, k.g1, k.s1, k.bd, k.g2, k.s2)):
+    for j, ref in enumerate((k.v_bq, k.v_bv, k.v_bo, k.v_g1, k.v_s1, k.v_bd, k.v_g2, k.v_s2)):
         k.vst[j : j + 1, 0:r] = ref[...].astype(F32)
     k.fst[...] = jnp.zeros_like(k.fst)
-    k.fst[0:r, 0:C] = k.wk_in[0].astype(F32)
-    k.fst[0:r, C:L] = k.wv_in[0].astype(F32)
-    k.fst[rs : rs + r, 0:C] = k.wq_in[0].astype(F32)
+    k.fst[0:r, 0:C] = k.v_wk_in[0].astype(F32)
+    k.fst[0:r, C:L] = k.v_wv_in[0].astype(F32)
+    k.fst[rs : rs + r, 0:C] = k.v_wq_in[0].astype(F32)
     k.fst[rs : rs + r, C : C + VECS] = k.vst[...].T[0:r]
-    k.fst[rs : rs + 1, C + VECS : C + VECS + 4 * r] = k.bu[...].astype(F32)
+    k.fst[rs : rs + 1, C + VECS : C + VECS + 4 * r] = k.v_bu[...].astype(F32)
     pack(M_QKV)
-    for q, src in ((M_OUT, k.wo_in[...]), (M_DOWN, k.wdn_in[0])):
+    for q, src in ((M_OUT, k.v_wo_in[...]), (M_DOWN, k.v_wdn_in[0])):
         src = src.astype(F32)
         k.fst[0 : 2 * r, 0:C] = src[0 : 2 * r]
         k.fst[0 : 2 * r, C:L] = src[2 * r : 4 * r]
         pack(q)
-    k.fst[0:r] = k.wup_in[0, :, 0:L].astype(F32)
-    k.fst[rs : rs + r] = k.wup_in[0, :, L : 2 * L].astype(F32)
+    k.fst[0:r] = k.v_wup_in[0, :, 0:L].astype(F32)
+    k.fst[rs : rs + r] = k.v_wup_in[0, :, L : 2 * L].astype(F32)
     pack(M_UP)
 
-    for n, (src, dst) in enumerate(((k.tok, k.xs), (k.cot, k.cs))):
+    for n, (src, dst) in enumerate(((k.v_tok, k.xs), (k.v_cot, k.cs))):
         both = src[...].astype(F32)
         for m in range(MB):
             k.flat[n * MB + m] = both[:, m]
             dst[m] = columns_of(z, k.flat.at[n * MB + m]).astype(BF16)
     k.xb[b] = k.xs[m_t]
-    k.cb[m_t] = k.cs[m_t]
+    k.cb[0] = k.cs[m_t]
 
     pl.semaphore_wait(bar, len(peers))
 
@@ -310,8 +331,8 @@
         return rcopy(k.xs.at[m], k.xb.at[b], k.x_ss.at[e], k.x_rs.at[b], (m * S + s_me, d, h))
 
     def x_pass(e, f):
-        src = k.xb.at[later(e) * S + s_me]
-        return rcopy(src, src, k.xf_ss.at[e, f], k.x_rs.at[later(e) * S + s_me], (m_t * S + mate(f), d, h))
+        src = k.xb.at[home(e)]
+        return rcopy(src, src, k.xf_ss.at[e, f], k.x_rs.at[home(e)], (m_t * S + mate(f), d, h))
 
     def x_wait(j):
         rcopy(k.xb.at[j], k.xb.at[j], k.x_ss.at[0], k.x_rs.at[j], (b, d, h)).wait_recv()
@@ -321,11 +342,6 @@
     loop(S - 1, lambda f: x_pass(0, f + 1).start())
 
     gather_forward(M_QKV)
-
-    for e in range(1, MB):
-        x_wait(later(e) * S + s_me)
-        loop(S - 1, lambda f: x_pass(e, f + 1).start())
-    gather_start(M_OUT)
 
     gather_wait(M_QKV)
 
@@ -356,7 +372,33 @@
             doc = doc + (j * R + token >= end).astype(jnp.int32)
         return row16 == doc
 
-    def kv_block(j):
+    def head_send(net, i, p):
+        buf, ss, rs_ = net
+        src, to = (h, xor(p)) if p <= half else (xor(half), xor(p - half))
+        return rcopy(buf.at[i, src], buf.at[i, src], ss.at[i, p], rs_.at[i, p], (b, d, to))
+
+    def head_wait(net, i, p):
+        buf, ss, rs_ = net
+        rcopy(buf.at[i, xor(p)], buf.at[i, xor(p)], ss.at[i, p], rs_.at[i, p], (b, d, h)).wait_recv()
+
+    def head_start(net, i):
+        for p in range(half, 0, -1):
+            head_send(net, i, p).start()
+
+    def head_pass(net, i):
+        head_wait(net, i, half)
+        for p in range(half + 1, nh):
+            head_send(net, i, p).start()
+
+    def head_end(net, i):
+        for p in range(1, nh):
+            if p != half:
+                head_wait(net, i, p)
+
+    o_net = (k.oall, k.o_ss, k.o_rs)
+    p_net = (k.pall, k.p_ss, k.p_rs)
+
+    def kv_block(t, j):
         kv = mm(k.wkvt[...], k.xb[j])
         kb = kv[0:C].astype(BF16)
         vb = (kv[C:L] + vec(V_BV)).astype(BF16)
@@ -364,116 +406,88 @@
         kf = jnp.where(barred, -BIG, 0.0).astype(BF16)
         for a in range(H):
             kh, vh = kb[a * HEAD_DIM : (a + 1) * HEAD_DIM], vb[a * HEAD_DIM : (a + 1) * HEAD_DIM]
-            k.kx[j, a] = kh
-            k.vx[j, a, 0:HEAD_DIM] = vh
-            k.vx[j, a, HEAD_DIM:] = one_rows
-            k.kt[j, a] = jnp.concatenate([kh, kf, pad], axis=0).T
-            k.vt[j, a] = jnp.concatenate([vh, one_rows, pad], axis=0).T
-
-    def other(n):
-        return lax.rem(s_me + 1 + n // MB, S) + lax.rem(m_t + n, MB) * S
-
-    def kv_other(n):
+            k.kx[t, a] = kh
+            k.vx[t, a, 0:HEAD_DIM] = vh
+            k.vx[t, a, HEAD_DIM:] = one_rows
+            k.kt[t, a] = jnp.concatenate([kh, kf, pad], axis=0).T
+            k.vt[t, a] = jnp.concatenate([vh, one_rows, pad], axis=0).T
+
+    def query_block(e):
+        xi = k.xb[home(e)]
+        k.xq[:, e * R : (e + 1) * R] = xi
+        qi = ((mm(k.wqt[...], xi) + vec(V_BQ)).astype(BF16).astype(F32) * HEAD_DIM**-0.5).astype(BF16)
+        hot = jnp.where(in_doc(home(e)), 1.0, 0.0).astype(BF16)
+        for a in range(H):
+            k.qx[e, a] = jnp.concatenate([qi[a * HEAD_DIM : (a + 1) * HEAD_DIM], hot, pad], axis=0)
+
+    def scores(e, a, t):
+        return mm(k.kt[t, a], k.qx[e, a])
+
+    def prob(e, a, t):
+        if z.keep:
+            return k.pbuf[t, e, a]
+        return jnp.exp(scores(e, a, t) - k.tops[e, a, pl.ds(t, 1)]).astype(BF16)
+
+    def attend(pairs):
+        units = [(e, a, t) for e, t in pairs for a in range(H)]
+        s = [scores(*u) for u in units]
+        top = [jnp.max(x, axis=0, keepdims=True) for x in s]
+        p = [jnp.exp(x - y).astype(BF16) for x, y in zip(s, top)]
+        o = [mm(k.vx[t, a], x) for (e, a, t), x in zip(units, p)]
+        for i, (e, a, t) in enumerate(units):
+            if z.keep:
+                k.pbuf[t, e, a] = p[i]
+            k.tops[e, a, pl.ds(t, 1)] = top[i]
+        for i, (e, a, t) in enumerate(units):
+            if isinstance(t, int) and t == 0:
+                k.top[e, a, 0:1] = top[i]
+                k.osum[e, a] = o[i]
+            else:
+                old = k.top[e, a, 0:1]
+                new = jnp.maximum(old, top[i])
+                k.top[e, a, 0:1] = new
+                k.osum[e, a] = k.osum[e, a] * jnp.exp(old - new) + o[i] * jnp.exp(top[i] - new)
+
+    def factor(e, a, t):
+        return jnp.exp(k.tops[e, a, pl.ds(t, 1)] - k.top[e, a, 0:1]) * k.top[e, a, 1:2]
+
+    for e in range(1, MB):
+        x_wait(home(e))
+        loop(S - 1, lambda f: x_pass(e, f + 1).start())
+    gather_start(M_OUT)
+    for e in range(MB):
+        kv_block(e, home(e))
+        query_block(e)
+    for t in range(MB):
+        attend([(e, t) for e in range(MB)])
+
+    def attend_other(n):
         x_wait(other(n))
-        kv_block(other(n))
-
-    for i in range(MB):
-        kv_block(mine[i])
-
-    for i in range(MB):
-        xi = k.xb[mine[i]]
-        k.xq[:, i * R : (i + 1) * R] = xi
-        qi = ((mm(k.wqt[...], xi) + vec(V_BQ)).astype(BF16).astype(F32) * HEAD_DIM**-0.5).astype(BF16)
-        hot = jnp.where(in_doc(mine[i]), 1.0, 0.0).astype(BF16)
+        kv_block(MB + n, other(n))
+        attend([(e, MB + n) for e in range(MB)])
+
+    def heads_done(e):
         for a in range(H):
-            full = jnp.concatenate([qi[a * HEAD_DIM : (a + 1) * HEAD_DIM], hot, pad], axis=0)
-            k.qx[i, a] = full
-
-    loop(nb - MB, kv_other)
+            o = k.osum[e, a]
+            inv = 1.0 / o[HEAD_DIM : HEAD_DIM + 1]
+            k.top[e, a, 1:2] = inv
+            k.oall[e, h, a * HEAD_DIM : (a + 1) * HEAD_DIM] = (o[0:HEAD_DIM] * inv).astype(BF16)
+        head_start(o_net, e)
+
+    last = nb - MB - 1
+    loop(last, attend_other)
+    x_wait(other(last))
     gather_start(M_UP)
-
-    def head_send(net, i, p):
-        buf, ss, rs_ = net
-        src, to = (h, xor(p)) if p <= half else (xor(half), xor(p - half))
-        return rcopy(buf.at[i, src], buf.at[i, src], ss.at[i, p], rs_.at[i, p], (b, d, to))
-
-    def head_wait(net, i, p):
-        buf, ss, rs_ = net
-        rcopy(buf.at[i, xor(p)], buf.at[i, xor(p)], ss.at[i, p], rs_.at[i, p], (b, d, h)).wait_recv()
-
-    def head_start(net, i):
-        for p in range(half, 0, -1):
-            head_send(net, i, p).start()
-
-    def head_pass(net, i):
-        head_wait(net, i, half)
-        for p in range(half + 1, nh):
-            head_send(net, i, p).start()
-
-    def head_end(net, i):
-        for p in range(1, nh):
-            if p != half:
-                head_wait(net, i, p)
-
-    o_net = (k.oall, k.o_ss, k.o_rs)
-    p_net = (k.pall, k.p_ss, k.p_rs)
-
-    def scores(i, a, j):
-        return mm(k.kt[j, a], k.qx[i, a])
-
-    def prob(i, a, j):
-        if z.keep:
-            return k.pbuf[i, a, j]
-        return jnp.exp(scores(i, a, j) - k.mrow[i, a, 0:1]).astype(BF16)
-
-    def attend(i, a):
-        if z.keep:
-            s = [scores(i, a, j) for j in range(nb)]
-            top = jnp.max(s[0], axis=0, keepdims=True)
-            for j in range(1, nb):
-                top = jnp.maximum(top, jnp.max(s[j], axis=0, keepdims=True))
-            o = None
-            for j in range(nb):
-                e = jnp.exp(s[j] - top).astype(BF16)
-                k.pbuf[i, a, j] = e
-                o = mm(k.vx[j, a], e) if o is None else o + mm(k.vx[j, a], e)
-        else:
-            k.mrow[i, a, 0:1] = jnp.full((1, R), -3e38, F32)
-
-            def see(j):
-                best = jnp.max(scores(i, a, j), axis=0, keepdims=True)
-                k.mrow[i, a, 0:1] = jnp.maximum(k.mrow[i, a, 0:1], best)
-
-            loop(nb, see)
-            acc = k.tgo.at[0, 0 : HEAD_DIM + 16]
-            acc[...] = jnp.zeros((HEAD_DIM + 16, R), F32)
-
-            def add(j):
-                acc[...] += mm(k.vx[j, a], prob(i, a, j))
-
-            loop(nb, add)
-            o = acc[...]
-        inv = 1.0 / o[HEAD_DIM : HEAD_DIM + 1]
-        k.mrow[i, a, 2:3] = inv
-        k.oall[i, h, a * HEAD_DIM : (a + 1) * HEAD_DIM] = (o[0:HEAD_DIM] * inv).astype(BF16)
-
-    for i in range(MB):
-        for a in range(H):
-            attend(i, a)
-        head_start(o_net, i)
+    kv_block(MB + last, other(last))
+    for e in range(MB):
+        attend([(e, MB + last)])
+        heads_done(e)
     gather_start(M_DOWN)
-
-    def c_send(e):
-        m = later(e)
-        return rcopy(k.cs.at[m], k.cb.at[m_t], k.c_ss.at[e], k.c_rs.at[m_t], (m * S + s_me, d, h))
-
-    for e in range(1, MB):
-        c_send(e).start()
 
     gather_forward(M_OUT)
     gather_forward(M_UP)
-    for i in range(MB):
-        head_pass(o_net, i)
+    for e in range(MB):
+        head_pass(o_net, e)
     gather_wait(M_OUT)
 
     per = W // nh
@@ -495,6 +509,14 @@
     k.wot[...] = k.fod[0:F].T.astype(BF16)
 
     gather_forward(M_DOWN)
+
+    def c_send(e):
+        m = later(e)
+        slot = lax.rem(m_t + MB - m, MB)
+        return rcopy(k.cs.at[m], k.cb.at[slot], k.c_ss.at[e], k.c_rs.at[slot], (m * S + s_me, d, h))
+
+    for e in range(1, MB):
+        c_send(e).start()
 
     lane_rows = R // 128
 
@@ -571,10 +593,8 @@
         h2 = y1 + mm(k.wdnt[...], act) + vec(V_BD)
         k.h2[i] = h2
 
-        @pl.when(m_t != i)
-        def _():
+        if i > 0:
             rcopy(k.cb.at[i], k.cb.at[i], k.c_ss.at[0], k.c_rs.at[i], (b, d, h)).wait_recv()
-
         dn2 = k.cb[i].astype(F32) * vec(V_G2)
         reduce_start(1, i, (h2, h2 * h2, dn2, dn2 * h2))
         k.gel[i] = cdf + u * jnp.exp(-0.5 * u * u) * ((2 * jnp.pi) ** -0.5)
@@ -585,7 +605,7 @@
         k.vg[j : j + 1] += mm_nt(ones, x)[0:1]
 
     def mo_send(i):
-        return rcopy(k.mo.at[i], k.o_mo.at[m_t], k.mo_ss.at[i], k.mo_rs.at[m_t], (mine[i], d, h))
+        return rcopy(k.mo.at[i], k.o_mo.at[m_t], k.mo_ss.at[i], k.mo_rs.at[m_t], (home(i), d, h))
 
     for i in range(MB):
         mean, square, dmean, dsquare = reduce_end(1, i, 4)
@@ -603,16 +623,12 @@
         k.dh1[i] = dn1
         n1 = k.n1[i]
         reduce_start(2, i, (dn1, dn1 * n1))
-        k.mo[i] = (n2 * vec(V_G2) + vec(V_S2)).astype(BF16)
-
-        @pl.when(m_t != i)
-        def _():
+        out = (n2 * vec(V_G2) + vec(V_S2)).astype(BF16)
+        if i > 0:
+            k.mo[i] = out
             mo_send(i).start()
-
-        @pl.when(m_t == i)
-        def _():
-            k.o_mo[m_t] = k.mo[i]
-
+        else:
+            k.o_mo[m_t] = out
         vec_grad(V_G2, (g * n2).astype(BF16))
         vec_grad(V_S2, k.cb[i])
         vec_grad(V_BD, dz)
@@ -719,29 +735,36 @@
     for i in range(1, MB):
         head_pass(p_net, i)
 
-    def grad_in(i):
-        head_end(p_net, i)
-        do = mm(k.wor[...], k.pall[i].reshape(D, R)).astype(BF16).astype(F32)
+    def grad_in(e):
+        head_end(p_net, e)
+        do = mm(k.wor[...], k.pall[e].reshape(D, R)).astype(BF16).astype(F32)
         for a in range(H):
-            part = do[a * HEAD_DIM : (a + 1) * HEAD_DIM] * k.mrow[i, a, 2:3]
-            own = k.oall[i, h, a * HEAD_DIM : (a + 1) * HEAD_DIM].astype(F32)
-            delta = jnp.sum(part * own, axis=0, keepdims=True)
-            hi = delta.astype(BF16).astype(F32)
-            rest = jnp.where(row16 == 0, -hi, jnp.where(row16 == 1, hi - delta, 0.0))
-            full = jnp.concatenate([part.astype(BF16), rest.astype(BF16), pad], axis=0)
-            k.dox[i, a] = full
-            k.dqacc[i, a] = jnp.zeros((HEAD_DIM, R), F32)
-
-    def back(j, queries, into):
+            part = do[a * HEAD_DIM : (a + 1) * HEAD_DIM]
+            own = k.oall[e, h, a * HEAD_DIM : (a + 1) * HEAD_DIM].astype(F32)
+            k.part[e, a] = part
+            k.delta[e, a, 0:1] = jnp.sum(part * own, axis=0, keepdims=True)
+            k.dqacc[e, a] = jnp.zeros((HEAD_DIM, R), F32)
+
+    def scaled(e, a, t):
+        f = factor(e, a, t)
+        delta = k.delta[e, a, 0:1] * f
+        hi = delta.astype(BF16).astype(F32)
+        rest = jnp.where(row16 == 0, -hi, jnp.where(row16 == 1, hi - delta, 0.0))
+        return jnp.concatenate([(k.part[e, a] * f).astype(BF16), rest.astype(BF16), pad], axis=0)
+
+    def back(t, queries, into):
         for a in range(H):
             dk = dv = None
-            for i in queries:
-                p = prob(i, a, j)
-                ds = (p.astype(F32) * mm(k.vt[j, a], k.dox[i, a])).astype(BF16)
-                k.dqacc[i, a] += mm(k.kx[j, a], ds)
-                dk_i, dv_i = mm_nt(k.qx[i, a, 0:HEAD_DIM], ds), mm_nt(k.dox[i, a, 0:HEAD_DIM], p)
-                dk = dk_i if dk is None else dk + dk_i
-                dv = dv_i if dv is None else dv + dv_i
+            for e in queries:
+                slot = t if z.keep else 0
+                k.dox[slot, e, a] = scaled(e, a, t)
+                p = prob(e, a, t)
+                ds = (p.astype(F32) * mm(k.vt[t, a], k.dox[slot, e, a])).astype(BF16)
+                k.dqacc[e, a] += mm(k.kx[t, a], ds)
+                dk_e = mm_nt(k.qx[e, a, 0:HEAD_DIM], ds)
+                dv_e = mm_nt(k.dox[slot, e, a, 0:HEAD_DIM], p)
+                dk = dk_e if dk is None else dk + dk_e
+                dv = dv_e if dv is None else dv + dv_e
             into(slice(a * HEAD_DIM, (a + 1) * HEAD_DIM), dk)
             into(slice(C + a * HEAD_DIM, C + (a + 1) * HEAD_DIM), dv)
 
@@ -751,9 +774,9 @@
         return mm(k.wkv[...], dkv)
 
     def tp_send(n):
-        j = other(n)
-        slot = j // S
-        return rcopy(k.tgs.at[j], k.tgr.at[slot, s_me], k.tp_ss.at[j], k.tp_rs.at[slot, s_me], (m_t * S + j % S, d, h))
+        dst = k.tgr.at[n % MB, s_me]
+        to = lax.rem(s_me + 1 + n // MB, S)
+        return rcopy(k.tgs.at[n], dst, k.tp_ss.at[n], k.tp_rs.at[n % MB, s_me], (m_t * S + to, d, h))
 
     def back_other(n, queries):
         slot = n if z.keep else 0
@@ -764,28 +787,28 @@
             else:
                 k.dkacc[slot, rows] += v
 
-        back(other(n), queries, into)
+        back(MB + n, queries, into)
         if queries[-1] == MB - 1:
-            k.tgs[other(n)] = tokens_part(other(n), k.dkacc[slot].astype(BF16)).astype(BF16)
+            k.tgs[n] = tokens_part(other(n), k.dkacc[slot].astype(BF16)).astype(BF16)
             tp_send(n).start()
 
-    for i in range(MB):
-        grad_in(i)
+    for e in range(MB):
+        grad_in(e)
         if z.keep:
-            loop(nb - MB, lambda n: back_other(n, [i]))
-        if i == 0:
+            loop(nb - MB, lambda n: back_other(nb - MB - 1 - n, [e]))
+        if e == 0:
             scatter_forward(M_UP)
     if not z.keep:
         loop(nb - MB, lambda n: back_other(n, list(range(MB))))
 
-    for i in range(MB):
+    for e in range(MB - 1, -1, -1):
 
         def into(rows, v):
             k.dkv[rows] = v
 
-        back(mine[i], range(MB), into)
-        k.tgo[i] = tokens_part(mine[i], k.dkv[...].astype(BF16))
-        if i == 0:
+        back(e, range(MB), into)
+        k.tgo[e] = tokens_part(home(e), k.dkv[...].astype(BF16))
+        if e == MB - 1:
             scatter_forward(M_OUT)
 
     for i in range(MB):
@@ -800,42 +823,35 @@
         k.pk[M_QKV, w] = rows_of([k.gkv[w * r : w * r + rs], k.gq[w * r : w * r + rs]])
     scatter_start(M_QKV)
 
-    def t_send(i):
-        return rcopy(k.tgx.at[i], k.o_tg.at[m_t], k.t_ss.at[i], k.t_rs.at[m_t], (mine[i], d, h))
-
-    for i in range(MB):
-        k.tgo[i] += k.dh1[i] + mm(k.wq[...], cols(k.dq, i))
+    def t_send(e):
+        return rcopy(k.tgx.at[e], k.o_tg.at[m_t], k.t_ss.at[e], k.t_rs.at[m_t], (home(e), d, h))
+
+    def tokens_total(e):
+        k.tgo[e] += k.dh1[e] + mm(k.wq[...], cols(k.dq, e))
 
         def add(f):
-            src = k.tgr.at[i, mate(f + 1)]
-            rcopy(src, src, k.tp_ss.at[0], k.tp_rs.at[i, mate(f + 1)], (b, d, h)).wait_recv()
-            k.tgo[i] += src[...].astype(F32)
+            src = k.tgr.at[e, mate(f + 1)]
+            rcopy(src, src, k.tp_ss.at[0], k.tp_rs.at[e, mate(f + 1)], (b, d, h)).wait_recv()
+            k.tgo[e] += src[...].astype(F32)
 
         loop(S - 1, add)
-        k.tgx[i] = k.tgo[i].astype(BF16)
-
-        @pl.when(m_t != i)
-        def _():
-            t_send(i).start()
-
-        @pl.when(m_t == i)
-        def _():
-            k.o_tg[m_t] = k.tgx[i]
+        return k.tgo[e].astype(BF16)
+
+    for e in range(1, MB):
+        k.tgx[e] = tokens_total(e)
+        t_send(e).start()
 
     scatter_forward(M_QKV)
 
+    k.o_tg[m_t] = tokens_total(0)
     for q in (M_DOWN, M_UP, M_OUT, M_QKV):
         scatter_end(q)
     for e in range(1, MB):
         m = later(e)
         for out, ss, rs_ in ((k.o_tg, k.t_ss, k.t_rs), (k.o_mo, k.mo_ss, k.mo_rs)):
-            rcopy(out.at[m], out.at[m], ss.at[m], rs_.at[m], (b, d, h)).wait_recv()
-        c_send(e).wait_send()
-        x_send(e).wait_send()
-        mo_send_e = rcopy(k.mo.at[m], k.o_mo.at[m_t], k.mo_ss.at[m], k.mo_rs.at[m_t], (b, d, h))
-        mo_send_e.wait_send()
-        t_send_e = rcopy(k.tgx.at[m], k.o_tg.at[m_t], k.t_ss.at[m], k.t_rs.at[m_t], (b, d, h))
-        t_send_e.wait_send()
+            rcopy(out.at[m], out.at[m], ss.at[e], rs_.at[m], (b, d, h)).wait_recv()
+        for send in (c_send, x_send, mo_send, t_send):
+            send(e).wait_send()
     for e in range(MB):
         loop(S - 1, lambda f: x_pass(e, f + 1).wait_send())
     loop(nb - MB, lambda n: tp_send(n).wait_send())
@@ -895,9 +911,15 @@
         def as_rows(a):
             return a.reshape(z.MB, z.N, 128).transpose(1, 0, 2)
 
-        scratch = main_scratch(z)
+        operands = (
+            as_rows(tokens), as_rows(cotangent), query_weight, query_bias, key_weight, value_weight, value_bias,
+            out_weight, out_bias, first_gain, first_shift, up_weight, up_bias, down_weight, down_bias, second_gain,
+            second_shift,
+        )
+        scratch = main_scratch(z, operands)
         vmem = pl.BlockSpec(memory_space=pltpu.VMEM)
         smem = pl.BlockSpec(memory_space=pltpu.SMEM)
+        hbm = pl.BlockSpec(memory_space=pltpu.HBM)
         names = INPUTS + OUTPUTS + list(scratch)
         sds = jax.ShapeDtypeStruct
         parts = pl.pallas_call(
@@ -907,18 +929,14 @@
                 sds((z.MB, z.C, z.R), BF16),
                 sds((4, z.rA, z.L), F32),
             ],
-            in_specs=[smem] + [vmem] * (len(INPUTS) - 1),
+            in_specs=[smem] + [hbm] * len(operands),
             out_specs=[vmem] * len(OUTPUTS),
             scratch_shapes=list(scratch.values()),
             compiler_params=pltpu.CompilerParams(
                 collective_id=0, has_side_effects=True, vmem_limit_bytes=63 << 20
             ),
             name="layer",
-        )(
-            doc_lengths, as_rows(tokens), as_rows(cotangent), query_weight,
-            query_bias, key_weight, value_weight, value_bias, out_weight, out_bias, first_gain, first_shift,
-            up_weight, up_bias, down_weight, down_bias, second_gain, second_shift,
-        )
+        )(doc_lengths, *operands)
         mat, vec = sds((1, z.r, z.C), F32), sds((1, z.r), F32)
         outs = pl.pallas_call(
             lambda *refs: finish_kernel(z, *refs),

time: 74.2 us -> 71.6 us (0.965)
  Pallas kernels: 73.2 us -> 70.6 us
    pallas_call x1, Pallas kernels: 70.6 us -> 68 us  [body(): pl.pallas_call(lambda *refs: main_kernel(z, names, *refs), out_shape=[sds...]
where the time goes in v5:
time: 71.6 us; the launch traced here: 71.5 us
  Pallas kernels  70.6 us (99%)
  between operations  0.83 us (1%)
    pallas_call x1, Pallas kernels, body(): pl.pallas_call(lambda *refs: main_kernel(z, names, *refs), out_shape=[sds...  68 us
    pallas_call x1, Pallas kernels, body(): pl.pallas_call(lambda *refs: finish_kernel(z, *refs), out_shape=[sds((z.N...  2.58 us

profile of v5, /device:TPU:0, one launch (start us, length us, event | category | flops | bytes accessed | tf_op | source)
XLA Modules:
  0.0 71.5 jit_solution(4206341380568812181)
XLA Ops:
  0.7 68.0 %layer.1 = (bf16[2,192,256]{2,1,0:T(8,128)(2,1)}, bf16[2,192,256]{2,1,0:T(8,128)(2,1)}, f32[4,48,384]{2,1,0:T(8,128)}) custom-call(s32[2,1,4]{2,1,0:T(1,128)} %refs_0_.1, bf16[384,2,128]{2,1,0:T(2,128)(2,1)} %bitcast.10, bf16[384,2,128]{2,1,0:T(2,128)(2,1)} %bitcast.11, bf16[1,24,192]{2,1,0:T(8,128)(2,1)} %refs_3_.1, bf16[1,24]{1,0:T(2,128)(2,1)} %refs_4_.1, ...), custom_call_target="tpu_custom_call" | custom-call | tf_op jit(solution)/shard_map/layer/pallas_call | solution.py:925
  68.7 2.6 %finish.1 = (bf16[384,2,128]{2,1,0:T(2,128)(2,1)}, f32[2,384,128]{2,1,0:T(8,128)}, f32[1,24,192]{2,1,0:T(8,128)}, f32[1,24]{1,0:T(1,128)}, f32[1,24,192]{2,1,0:T...) custom-call(bf16[2,192,256]{2,1,0:T(8,128)(2,1)} %get-tuple-element., ...), custom_call_target="tpu_custom_call" | custom-call | tf_op jit(solution)/shard_map/finish/pallas_call | solution.py:941

commit v6 on v5

--- a/solution.py
+++ b/solution.py
@@ -152,18 +152,18 @@
         y1=v((MB, C, R), F32),
         h2=v((MB, C, R), F32),
         gel=v((MB, F, R), F32),
+        up=v((MB, F, R), F32),
         dh1=v((MB, C, R), F32),
         y1b=v((C, Q), BF16),
         act=v((F, Q), BF16),
         dz=v((C, Q), BF16),
         du=v((F, Q), BF16),
+        vin=v((3, MB, C, R), BF16),
         mo=v((MB, C, R), BF16),
-        dox=v((nb if z.keep else 1, MB, H, 128, R), BF16),
         part=v((MB, H, HEAD_DIM, R), F32),
         delta=v((MB, H, 8, R), F32),
         dqacc=v((MB, H, HEAD_DIM, R), F32),
         dkacc=v((nb - MB if z.keep else 1, L, R), F32),
-        dkv=v((L, R), F32),
         dq=v((C, Q), BF16),
         tgs=v((nb, C, R), BF16),
         tgo=v((MB, C, R), F32),
@@ -455,6 +455,7 @@
         x_wait(home(e))
         loop(S - 1, lambda f: x_pass(e, f + 1).start())
     gather_start(M_OUT)
+    gather_start(M_UP)
     for e in range(MB):
         kv_block(e, home(e))
         query_block(e)
@@ -477,12 +478,11 @@
     last = nb - MB - 1
     loop(last, attend_other)
     x_wait(other(last))
-    gather_start(M_UP)
+    gather_start(M_DOWN)
     kv_block(MB + last, other(last))
     for e in range(MB):
         attend([(e, MB + last)])
         heads_done(e)
-    gather_start(M_DOWN)
 
     gather_forward(M_OUT)
     gather_forward(M_UP)
@@ -597,7 +597,10 @@
             rcopy(k.cb.at[i], k.cb.at[i], k.c_ss.at[0], k.c_rs.at[i], (b, d, h)).wait_recv()
         dn2 = k.cb[i].astype(F32) * vec(V_G2)
         reduce_start(1, i, (h2, h2 * h2, dn2, dn2 * h2))
-        k.gel[i] = cdf + u * jnp.exp(-0.5 * u * u) * ((2 * jnp.pi) ** -0.5)
+        k.up[i], k.gel[i] = u, cdf
+    for i in range(MB):
+        u = k.up[i]
+        k.gel[i] += u * jnp.exp(-0.5 * u * u) * ((2 * jnp.pi) ** -0.5)
     k.vg[...] = jnp.zeros_like(k.vg)
     ones = jnp.ones((16, R), BF16)
 
@@ -629,11 +632,9 @@
             mo_send(i).start()
         else:
             k.o_mo[m_t] = out
-        vec_grad(V_G2, (g * n2).astype(BF16))
-        vec_grad(V_S2, k.cb[i])
-        vec_grad(V_BD, dz)
-        vec_grad(V_G1, (dy1 * n1).astype(BF16))
-        vec_grad(V_S1, dy1.astype(BF16))
+        k.vin[0, i] = (g * n2).astype(BF16)
+        k.vin[1, i] = (dy1 * n1).astype(BF16)
+        k.vin[2, i] = dy1.astype(BF16)
 
     def s1_send(q, e, i):
         dt = lax.rem(d + e, nd)
@@ -697,6 +698,10 @@
     for w in range(W):
         k.pk[M_UP, w] = rows_of([k.gup[w * r : w * r + rs, 0:L], k.gup[w * r : w * r + rs, L:F]])
     scatter_start(M_UP)
+    for i in range(MB):
+        for j, x in ((V_G2, k.vin[0, i]), (V_G1, k.vin[1, i]), (V_S1, k.vin[2, i]), (V_S2, k.cb[i])):
+            vec_grad(j, x)
+        vec_grad(V_BD, cols(k.dz, i))
 
     for i in range(MB):
         dmean, dsquare = reduce_end(2, i, 2)
@@ -752,21 +757,29 @@
         rest = jnp.where(row16 == 0, -hi, jnp.where(row16 == 1, hi - delta, 0.0))
         return jnp.concatenate([(k.part[e, a] * f).astype(BF16), rest.astype(BF16), pad], axis=0)
 
-    def back(t, queries, into):
-        for a in range(H):
-            dk = dv = None
-            for e in queries:
-                slot = t if z.keep else 0
-                k.dox[slot, e, a] = scaled(e, a, t)
-                p = prob(e, a, t)
-                ds = (p.astype(F32) * mm(k.vt[t, a], k.dox[slot, e, a])).astype(BF16)
-                k.dqacc[e, a] += mm(k.kx[t, a], ds)
-                dk_e = mm_nt(k.qx[e, a, 0:HEAD_DIM], ds)
-                dv_e = mm_nt(k.dox[slot, e, a, 0:HEAD_DIM], p)
-                dk = dk_e if dk is None else dk + dk_e
-                dv = dv_e if dv is None else dv + dv_e
-            into(slice(a * HEAD_DIM, (a + 1) * HEAD_DIM), dk)
-            into(slice(C + a * HEAD_DIM, C + (a + 1) * HEAD_DIM), dv)
+    def back(slots, queries):
+        units = [(e, a, t) for t in slots for a in range(H) for e in queries]
+        dox = [scaled(*u) for u in units]
+        p = [prob(*u) for u in units]
+        dp = [mm(k.vt[t, a], x) for (e, a, t), x in zip(units, dox)]
+        ds = [(x.astype(F32) * y).astype(BF16) for x, y in zip(p, dp)]
+        dq = [mm(k.kx[t, a], x) for (e, a, t), x in zip(units, ds)]
+        dk = [mm_nt(k.qx[e, a, 0:HEAD_DIM], x) for (e, a, t), x in zip(units, ds)]
+        dv = [mm_nt(x[0:HEAD_DIM], y) for x, y in zip(dox, p)]
+        for e in queries:
+            for a in range(H):
+                mine = [x for (e2, a2, t), x in zip(units, dq) if (e2, a2) == (e, a)]
+                k.dqacc[e, a] += sum(mine[1:], mine[0])
+        found = []
+        per_slot = H * len(queries)
+        for n in range(len(slots)):
+            rows = []
+            for x in (dk, dv):
+                for a in range(H):
+                    at = n * per_slot + a * len(queries)
+                    rows.append(sum(x[at + 1 : at + len(queries)], x[at]))
+            found.append(jnp.concatenate(rows, axis=0))
+        return found
 
     def tokens_part(j, dkv):
         k.gkv[0:C] += mm_nt(k.xb[j], dkv)
@@ -778,36 +791,31 @@
         to = lax.rem(s_me + 1 + n // MB, S)
         return rcopy(k.tgs.at[n], dst, k.tp_ss.at[n], k.tp_rs.at[n % MB, s_me], (m_t * S + to, d, h))
 
-    def back_other(n, queries):
-        slot = n if z.keep else 0
-
-        def into(rows, v):
-            if queries[0] == 0:
-                k.dkacc[slot, rows] = v
-            else:
-                k.dkacc[slot, rows] += v
-
-        back(MB + n, queries, into)
-        if queries[-1] == MB - 1:
-            k.tgs[n] = tokens_part(other(n), k.dkacc[slot].astype(BF16)).astype(BF16)
+    def send_part(n, dkv):
+        k.tgs[n] = tokens_part(other(n), dkv.astype(BF16)).astype(BF16)
+        if not z.keep or n % MB:
             tp_send(n).start()
 
+    others = list(range(nb - MB - 1, -1, -1))
     for e in range(MB):
         grad_in(e)
         if z.keep:
-            loop(nb - MB, lambda n: back_other(nb - MB - 1 - n, [e]))
+            found = back([MB + n for n in others], [e])
+            for n, dkv in zip(others, found):
+                if e > 0:
+                    dkv = dkv + k.dkacc[n]
+                if e < MB - 1:
+                    k.dkacc[n] = dkv
+                else:
+                    send_part(n, dkv)
         if e == 0:
             scatter_forward(M_UP)
     if not z.keep:
-        loop(nb - MB, lambda n: back_other(n, list(range(MB))))
+        loop(nb - MB, lambda n: send_part(n, back([MB + n], range(MB))[0]))
 
     for e in range(MB - 1, -1, -1):
-
-        def into(rows, v):
-            k.dkv[rows] = v
-
-        back(e, range(MB), into)
-        k.tgo[e] = tokens_part(home(e), k.dkv[...].astype(BF16))
+        dkv = back([e], range(MB))[0]
+        k.tgo[e] = tokens_part(home(e), dkv.astype(BF16))
         if e == MB - 1:
             scatter_forward(M_OUT)
 
@@ -840,6 +848,9 @@
     for e in range(1, MB):
         k.tgx[e] = tokens_total(e)
         t_send(e).start()
+    if z.keep:
+        for n in range(0, nb - MB, MB):
+            tp_send(n).start()
 
     scatter_forward(M_QKV)
 

time: 71.6 us -> 68.9 us (0.962)
  Pallas kernels: 70.6 us -> 67.9 us
    pallas_call x1, Pallas kernels: 68 us -> 65.3 us  [body(): pl.pallas_call(lambda *refs: main_kernel(z, names, *refs), out_shape=[sds...]
where the time goes in v6:
time: 68.9 us; the launch traced here: 68.7 us
  Pallas kernels  67.9 us (99%)
  between operations  0.83 us (1%)
    pallas_call x1, Pallas kernels, body(): pl.pallas_call(lambda *refs: main_kernel(z, names, *refs), out_shape=[sds...  65.3 us
    pallas_call x1, Pallas kernels, body(): pl.pallas_call(lambda *refs: finish_kernel(z, *refs), out_shape=[sds((z.N...  2.58 us

profile of v6, /device:TPU:0, one launch (start us, length us, event | category | flops | bytes accessed | tf_op | source)
XLA Modules:
  0.0 68.7 jit_solution(5157375235036509916)
XLA Ops:
  0.7 65.3 %layer.1 = (bf16[2,192,256]{2,1,0:T(8,128)(2,1)}, bf16[2,192,256]{2,1,0:T(8,128)(2,1)}, f32[4,48,384]{2,1,0:T(8,128)}) custom-call(s32[2,1,4]{2,1,0:T(1,128)} %refs_0_.1, bf16[384,2,128]{2,1,0:T(2,128)(2,1)} %bitcast.10, bf16[384,2,128]{2,1,0:T(2,128)(2,1)} %bitcast.11, bf16[1,24,192]{2,1,0:T(8,128)(2,1)} %refs_3_.1, bf16[1,24]{1,0:T(2,128)(2,1)} %refs_4_.1, ...), custom_call_target="tpu_custom_call" | custom-call | tf_op jit(solution)/shard_map/layer/pallas_call | solution.py:936
  66.0 2.6 %finish.1 = (bf16[384,2,128]{2,1,0:T(2,128)(2,1)}, f32[2,384,128]{2,1,0:T(8,128)}, f32[1,24,192]{2,1,0:T(8,128)}, f32[1,24]{1,0:T(1,128)}, f32[1,24,192]{2,1,0:T...) custom-call(bf16[2,192,256]{2,1,0:T(8,128)(2,1)} %get-tuple-element., ...), custom_call_target="tpu_custom_call" | custom-call | tf_op jit(solution)/shard_map/finish/pallas_call | solution.py:952

commit v7 on v6

--- a/solution.py
+++ b/solution.py
@@ -15,8 +15,7 @@
 F32 = jnp.float32
 BF16 = jnp.bfloat16
 V_BQ, V_BV, V_BO, V_G1, V_S1, V_BD, V_G2, V_S2 = range(8)
-VECS = 16
-M_QKV, M_OUT, M_UP, M_DOWN = range(4)
+M_OUT, M_UP, M_DOWN, M_QKV = range(4)
 
 
 def up_to(n, m):
@@ -94,6 +93,14 @@
         self.r2 = up_to(2 * self.r, 8)
         self.rA = up_to(2 * self.rs, 16)
         self.L = 2 * self.C
+        self.full, left = divmod(3 * self.C, 128)
+        self.left = self.full * self.rs
+        fold = left == 64 and self.r % 2 == 0
+        self.bits = [(0, 0, self.r // 2), (64, self.r // 2, self.r // 2)] if fold else [(0, 0, self.r)]
+        self.vrow = self.left + up_to(self.bits[0][2], 4)
+        self.vper = min(8, 128 // self.r)
+        self.brow = self.vrow + -(-8 // self.vper)
+        self.rQ = up_to(max(self.brow + 1, self.left + self.rs), 16)
         self.keep = self.nb * self.R * self.Q * self.H * 2 <= (8 << 20)
         assert self.F == 4 * self.C and self.F == self.nh * self.C and self.W % self.nh == 0
 
@@ -102,7 +109,7 @@
     "lens", "tok", "cot", "wq_in", "bq", "wk_in", "wv_in", "bv", "wo_in", "bo", "g1", "s1", "wup_in", "bu",
     "wdn_in", "bd", "g2", "s2",
 ]
-OUTPUTS = ["o_mo", "o_tg", "o_G"]
+OUTPUTS = ["o_mo", "o_tg", "o_G", "o_Q"]
 
 
 def main_scratch(z, inputs):
@@ -117,12 +124,14 @@
         xb=v((nb, C, R), BF16),
         cs=v((MB, C, R), BF16),
         cb=v((MB, C, R), BF16),
-        buf=v((4, W, rA, L), BF16),
+        bufq=v((W, z.rQ, 128), BF16),
+        buf=v((3, W, rA, L), BF16),
         wob=v((nh, W // nh, rA, L), BF16),
         fst=v((rA, L), F32),
-        vst=v((VECS, 128), F32),
-        fkv=v((C + 8, L), F32),
-        fq=v((C + 8, L), F32),
+        fsq=v((z.rQ, 128), F32),
+        fall=v((C + 8, up_to(3 * C, 128)), F32),
+        vrows=v((up_to(W * (z.brow - z.vrow), 8), 128), F32),
+        vcol=v((C + 8, 8), F32),
         fup=v((C + 16, F), F32),
         fod=v((F + 16, C), F32),
         wkv=v((C, L), BF16),
@@ -169,20 +178,24 @@
         tgo=v((MB, C, R), F32),
         tgr=v((MB, z.S, C, R), BF16),
         tgx=v((MB, C, R), BF16),
-        gkv=v((C + 8, L), F32),
-        gq=v((C + 8, L), F32),
+        gall=v((C + 8, up_to(3 * C, 128)), F32),
+        gst=v((W, z.rQ, 128), F32),
         gup=v((C + 8, F), F32),
         gout=v((F + 16, C), F32),
         gdn=v((F + 16, C), F32),
-        vg=v((VECS, C), F32),
-        ug=v((8, F), F32),
-        pk=v((4, W, rA, L), BF16),
-        got1=v((4, dd, nb, rA, L), BF16),
-        sent2=v((4, nb, rA, L), BF16),
-        got2=v((4, nb, rA, L), BF16),
-        x_ss=dma((MB,)),
-        xf_ss=dma((MB, z.S)),
-        x_rs=dma((nb,)),
+        vg=v((8, C), F32),
+        pk=v((3, W, rA, L), BF16),
+        got1=v((3, dd, nb, rA, L), BF16),
+        sent2=v((3, nb, rA, L), BF16),
+        got2=v((3, nb, rA, L), BF16),
+        pkq=v((W, z.rQ, 128), BF16),
+        got1q=v((dd, nb, z.rQ, 128), BF16),
+        sent2q=v((nb, z.rQ, 128), BF16),
+        got2q=v((nb, z.rQ, 128), BF16),
+        sync=pltpu.SemaphoreType.REGULAR((2,)),
+        x_ss=dma((MB, 2)),
+        xf_ss=dma((MB, z.S, 2)),
+        x_rs=dma((nb, 2)),
         c_ss=dma((MB,)),
         c_rs=dma((MB,)),
         g1_ss=dma((4, nb)),
@@ -257,16 +270,35 @@
     def pack(q):
         k.buf[q, w_me] = k.fst[...].astype(BF16)
 
-    k.vst[...] = jnp.zeros_like(k.vst)
-    for j, ref in enumerate((k.v_bq, k.v_bv, k.v_bo, k.v_g1, k.v_s1, k.v_bd, k.v_g2, k.v_s2)):
-        k.vst[j : j + 1, 0:r] = ref[...].astype(F32)
+    def place(n, put):
+        column = 0
+        for block, at, size in pieces(C, n):
+            if block < z.full:
+                put(block * rs, at, r, 0, column, size)
+            else:
+                for where, row, rows in z.bits:
+                    put(z.left, at + where, rows, row, column, size)
+            column += size
+
+    vectors = (k.v_bq, k.v_bv, k.v_bo, k.v_g1, k.v_s1, k.v_bd, k.v_g2, k.v_s2)
+
+    def vec_at(j):
+        return z.vrow + j // z.vper, j % z.vper * r
+
+    k.fsq[...] = jnp.zeros_like(k.fsq)
+    for n, src in enumerate((k.v_wk_in[0], k.v_wv_in[0], k.v_wq_in[0])):
+        src = src.astype(F32)
+
+        def put(row, at, rows, row2, column, size):
+            k.fsq[row : row + rows, at : at + size] = src[row2 : row2 + rows, column : column + size]
+
+        place(n, put)
+    for j, ref in enumerate(vectors):
+        row, at = vec_at(j)
+        k.fsq[row : row + 1, at : at + r] = ref[...].astype(F32)
+    k.fsq[z.brow : z.brow + 1, 0 : 4 * r] = k.v_bu[...].astype(F32)
+    k.bufq[w_me] = k.fsq[...].astype(BF16)
     k.fst[...] = jnp.zeros_like(k.fst)
-    k.fst[0:r, 0:C] = k.v_wk_in[0].astype(F32)
-    k.fst[0:r, C:L] = k.v_wv_in[0].astype(F32)
-    k.fst[rs : rs + r, 0:C] = k.v_wq_in[0].astype(F32)
-    k.fst[rs : rs + r, C : C + VECS] = k.vst[...].T[0:r]
-    k.fst[rs : rs + 1, C + VECS : C + VECS + 4 * r] = k.v_bu[...].astype(F32)
-    pack(M_QKV)
     for q, src in ((M_OUT, k.v_wo_in[...]), (M_DOWN, k.v_wdn_in[0])):
         src = src.astype(F32)
         k.fst[0 : 2 * r, 0:C] = src[0 : 2 * r]
@@ -286,20 +318,23 @@
 
     pl.semaphore_wait(bar, len(peers))
 
+    def shares(q):
+        return k.bufq if q == M_QKV else k.buf.at[q]
+
     def g1(q, i):
-        own = k.buf.at[q, w_me]
+        own = shares(q).at[w_me]
         return rcopy(own, own, k.g1_ss.at[q, i], k.g1_rs.at[q, i], (lax.rem(b + i, nb), d, h))
 
     def g1_wait(q, i):
-        src = k.buf.at[q, lax.rem(b + nb - i, nb) * nd + d]
+        src = shares(q).at[lax.rem(b + nb - i, nb) * nd + d]
         rcopy(src, src, k.g1_ss.at[q, i], k.g1_rs.at[q, i], (b, d, h)).wait_recv()
 
     def g2(q, e, i):
-        src = k.buf.at[q, lax.rem(b + nb - i, nb) * nd + d]
+        src = shares(q).at[lax.rem(b + nb - i, nb) * nd + d]
         return rcopy(src, src, k.g2_ss.at[q, e - 1, i], k.g2_rs.at[q, e - 1, i], (b, lax.rem(d + e, nd), h))
 
     def g2_wait(q, e, i):
-        src = k.buf.at[q, lax.rem(b + nb - i, nb) * nd + lax.rem(d + nd - e, nd)]
+        src = shares(q).at[lax.rem(b + nb - i, nb) * nd + lax.rem(d + nd - e, nd)]
         rcopy(src, src, k.g2_ss.at[q, e - 1, i], k.g2_rs.at[q, e - 1, i], (b, d, h)).wait_recv()
 
     def gather_start(q):
@@ -320,42 +355,68 @@
             loop(nb, lambda i: g2_wait(q, e, i))
 
     def gather_drain(q):
-        loop(nb - 1, lambda i: g1(q, i + 1).wait_send())
+        if q != M_QKV:
+            loop(nb - 1, lambda i: g1(q, i + 1).wait_send())
         for e in range(1, nd):
             loop(nb, lambda i: g2(q, e, i).wait_send())
 
+    def in_step(n):
+        pl.semaphore_signal(k.sync.at[n], inc=1, device_id=(b, d, xor(1)), device_id_type=MESH)
+        pl.semaphore_wait(k.sync.at[n], 1)
+
     gather_start(M_QKV)
 
-    def x_send(e):
+    halves = [pl.ds(0, C // 2), pl.ds(C // 2, C // 2)]
+
+    def x_send(e, c):
         m = later(e)
-        return rcopy(k.xs.at[m], k.xb.at[b], k.x_ss.at[e], k.x_rs.at[b], (m * S + s_me, d, h))
-
-    def x_pass(e, f):
-        src = k.xb.at[home(e)]
-        return rcopy(src, src, k.xf_ss.at[e, f], k.x_rs.at[home(e)], (m_t * S + mate(f), d, h))
-
-    def x_wait(j):
-        rcopy(k.xb.at[j], k.xb.at[j], k.x_ss.at[0], k.x_rs.at[j], (b, d, h)).wait_recv()
-
-    for e in range(1, MB):
-        x_send(e).start()
-    loop(S - 1, lambda f: x_pass(0, f + 1).start())
+        dst = k.xb.at[b, halves[c]]
+        return rcopy(k.xs.at[m, halves[c]], dst, k.x_ss.at[e, c], k.x_rs.at[b, c], (m * S + s_me, d, h))
+
+    def x_pass(e, f, c):
+        src = k.xb.at[home(e), halves[c]]
+        return rcopy(src, src, k.xf_ss.at[e, f, c], k.x_rs.at[home(e), c], (m_t * S + mate(f), d, h))
+
+    def x_wait(j, c):
+        src = k.xb.at[j, halves[c]]
+        rcopy(src, src, k.x_ss.at[0, c], k.x_rs.at[j, c], (b, d, h)).wait_recv()
+
+    loop(nb - 1, lambda i: g1(M_QKV, i + 1).wait_send())
+    in_step(0)
+    for c in range(2):
+        for e in range(1, MB):
+            x_send(e, c).start()
+    for c in range(2):
+        loop(S - 1, lambda f: x_pass(0, f + 1, c).start())
 
     gather_forward(M_QKV)
 
     gather_wait(M_QKV)
 
     for w in range(W):
-        slab = k.buf[M_QKV, w].astype(F32)
-        k.fkv[w * r : w * r + rs] = slab[0:rs]
-        k.fq[w * r : w * r + rs] = slab[rs : 2 * rs]
-    k.wkv[...] = k.fkv[0:C].astype(BF16)
-    k.wkvt[...] = k.fkv[0:C].T.astype(BF16)
-    k.wq[...] = k.fq[0:C, 0:C].astype(BF16)
-    k.wqt[...] = k.fq[0:C, 0:C].T.astype(BF16)
+        slab = k.bufq[w].astype(F32)
+        for block in range(z.full):
+            k.fall[w * r : w * r + rs, block * 128 : (block + 1) * 128] = slab[block * rs : (block + 1) * rs]
+        end = z.full * 128
+        for at, row, rows in z.bits:
+            rows = rows if len(z.bits) > 1 else rs
+            part = slab[z.left : z.left + rows, at : at + 3 * C - end]
+            k.fall[w * r + row : w * r + row + rows, end : 3 * C] = part
+        per = z.brow - z.vrow
+        k.vrows[w * per : (w + 1) * per] = slab[z.vrow : z.brow]
+    k.wkv[...] = k.fall[0:C, 0:L].astype(BF16)
+    k.wkvt[...] = k.fall[0:C, 0:L].T.astype(BF16)
+    k.wq[...] = k.fall[0:C, L : 3 * C].astype(BF16)
+    k.wqt[...] = k.fall[0:C, L : 3 * C].T.astype(BF16)
+    columns = k.vrows[...].T
+    for w in range(W):
+        for j in range(8):
+            row, at = vec_at(j)
+            column = w * (z.brow - z.vrow) + row - z.vrow
+            k.vcol[w * r : (w + 1) * r, j : j + 1] = columns[at : at + r, column : column + 1]
 
     def vec(j):
-        return k.fq[0:C, C + j : C + j + 1]
+        return k.vcol[0:C, j : j + 1]
 
     row16 = lax.broadcasted_iota(jnp.int32, (16, R), 0)
     column = lax.broadcasted_iota(jnp.int32, (16, R), 1)
@@ -451,9 +512,10 @@
     def factor(e, a, t):
         return jnp.exp(k.tops[e, a, pl.ds(t, 1)] - k.top[e, a, 0:1]) * k.top[e, a, 1:2]
 
-    for e in range(1, MB):
-        x_wait(home(e))
-        loop(S - 1, lambda f: x_pass(e, f + 1).start())
+    for c in range(2):
+        for e in range(1, MB):
+            x_wait(home(e), c)
+            loop(S - 1, lambda f: x_pass(e, f + 1, c).start())
     gather_start(M_OUT)
     gather_start(M_UP)
     for e in range(MB):
@@ -463,7 +525,8 @@
         attend([(e, t) for e in range(MB)])
 
     def attend_other(n):
-        x_wait(other(n))
+        for c in range(2):
+            x_wait(other(n), c)
         kv_block(MB + n, other(n))
         attend([(e, MB + n) for e in range(MB)])
 
@@ -477,7 +540,8 @@
 
     last = nb - MB - 1
     loop(last, attend_other)
-    x_wait(other(last))
+    for c in range(2):
+        x_wait(other(last), c)
     gather_start(M_DOWN)
     kv_block(MB + last, other(last))
     for e in range(MB):
@@ -564,7 +628,7 @@
         k.fup[w * r : w * r + rs, L:F] = slab[rs : 2 * rs]
     k.fup[C : C + 16] = jnp.zeros((16, F), F32)
     for w in range(W):
-        row = k.buf[M_QKV, w].astype(F32)[rs : rs + 1, C + VECS : C + VECS + 4 * r]
+        row = k.bufq[w].astype(F32)[z.brow : z.brow + 1, 0 : 4 * r]
         k.fup[C : C + 1, 4 * r * w : 4 * r * (w + 1)] = row
     k.wup[...] = k.fup[0:C].astype(BF16)
     k.wupt[...] = k.fup[...].T.astype(BF16)
@@ -636,25 +700,30 @@
         k.vin[1, i] = (dy1 * n1).astype(BF16)
         k.vin[2, i] = dy1.astype(BF16)
 
+    def sums(q):
+        if q == M_QKV:
+            return k.pkq, k.got1q, k.sent2q, k.got2q, k.o_Q
+        return k.pk.at[q], k.got1.at[q], k.sent2.at[q], k.got2.at[q], k.o_G.at[q]
+
     def s1_send(q, e, i):
         dt = lax.rem(d + e, nd)
         return rcopy(
-            k.pk.at[q, i * nd + dt], k.got1.at[q, e - 1, i], k.s1_ss.at[q, e - 1, i], k.s1_rs.at[q, e - 1, i],
+            sums(q)[0].at[i * nd + dt], sums(q)[1].at[e - 1, i], k.s1_ss.at[q, e - 1, i], k.s1_rs.at[q, e - 1, i],
             (b, dt, h),
         )
 
     def s2_send(q, i):
         bt = lax.rem(b + i, nb)
-        return rcopy(k.sent2.at[q, bt], k.got2.at[q, b], k.s2_ss.at[q, i], k.s2_rs.at[q, i], (bt, d, h))
+        return rcopy(sums(q)[2].at[bt], sums(q)[3].at[b], k.s2_ss.at[q, i], k.s2_rs.at[q, i], (bt, d, h))
 
     def scatter_start(q):
         for e in range(1, nd):
             loop(nb, lambda i: s1_send(q, e, i).start())
 
     def scatter_sum(q, bt):
-        part = k.pk[q, bt * nd + d].astype(F32)
+        part = sums(q)[0][bt * nd + d].astype(F32)
         for e in range(1, nd):
-            src = k.got1.at[q, e - 1, bt]
+            src = sums(q)[1].at[e - 1, bt]
             rcopy(src, src, k.s1_ss.at[q, e - 1, bt], k.s1_rs.at[q, e - 1, bt], (b, d, h)).wait_recv()
             part = part + src[...].astype(F32)
         return part
@@ -662,17 +731,17 @@
     def scatter_forward(q):
         def one(i):
             bt = lax.rem(b + i + 1, nb)
-            k.sent2[q, bt] = scatter_sum(q, bt).astype(BF16)
+            sums(q)[2][bt] = scatter_sum(q, bt).astype(BF16)
             s2_send(q, i + 1).start()
 
         loop(nb - 1, one)
-        k.o_G[q] = scatter_sum(q, b)
+        sums(q)[4][...] = scatter_sum(q, b)
 
     def scatter_end(q):
         def one(i):
-            src = k.got2.at[q, lax.rem(b + nb - i - 1, nb)]
+            src = sums(q)[3].at[lax.rem(b + nb - i - 1, nb)]
             rcopy(src, src, k.s2_ss.at[q, i + 1], k.s2_rs.at[q, i + 1], (b, d, h)).wait_recv()
-            k.o_G[q] += src[...].astype(F32)
+            sums(q)[4][...] += src[...].astype(F32)
 
         loop(nb - 1, one)
         loop(nb - 1, lambda i: s2_send(q, i + 1).wait_send())
@@ -720,10 +789,18 @@
     k.gout[0:F] = g
     pack_halves(M_OUT, k.gout)
     ug = mm_nt(jnp.ones((16, z.Q), BF16), k.du[...])
-    k.gq[...] = jnp.zeros_like(k.gq)
+    k.gst[...] = jnp.zeros_like(k.gst)
     for w in range(W):
-        k.gq[w * r : w * r + 1, C + VECS : C + VECS + 4 * r] = ug[0:1, 4 * r * w : 4 * r * (w + 1)]
-    k.gkv[...] = jnp.zeros_like(k.gkv)
+        k.gst[w, z.brow : z.brow + 1, 0 : 4 * r] = ug[0:1, 4 * r * w : 4 * r * (w + 1)]
+
+    def pack_vec(j):
+        row, at = vec_at(j)
+        for w in range(W):
+            k.gst[w, row : row + 1, at : at + r] = k.vg[j : j + 1, w * r : (w + 1) * r]
+
+    for j in (V_BO, V_G1, V_S1, V_BD, V_G2, V_S2):
+        pack_vec(j)
+    k.gall[...] = jnp.zeros_like(k.gall)
 
     for p in range(1, nh):
         src = k.wob.at[xor(p)]
@@ -735,8 +812,8 @@
     for j in range(nh):
         k.wor[:, j * C : (j + 1) * C] = k.fod[j * C : (j + 1) * C].astype(BF16)
 
+    scatter_forward(M_DOWN)
     head_pass(p_net, 0)
-    scatter_forward(M_DOWN)
     for i in range(1, MB):
         head_pass(p_net, i)
 
@@ -782,7 +859,7 @@
         return found
 
     def tokens_part(j, dkv):
-        k.gkv[0:C] += mm_nt(k.xb[j], dkv)
+        k.gall[0:C, 0:L] += mm_nt(k.xb[j], dkv)
         vec_grad(V_BV, dkv[C:L])
         return mm(k.wkv[...], dkv)
 
@@ -824,11 +901,19 @@
             rows = slice(a * HEAD_DIM, (a + 1) * HEAD_DIM)
             k.dq[rows, i * R : (i + 1) * R] = (k.dqacc[i, a] * HEAD_DIM**-0.5).astype(BF16)
         vec_grad(V_BQ, cols(k.dq, i))
-    k.gq[0:C, 0:C] = mm_nt(k.xq[...], k.dq[...])
-    k.gq[0:C, C : C + VECS] = k.vg[...].T
+    k.gall[0:C, L : 3 * C] = mm_nt(k.xq[...], k.dq[...])
+    pack_vec(V_BQ)
+    pack_vec(V_BV)
 
     for w in range(W):
-        k.pk[M_QKV, w] = rows_of([k.gkv[w * r : w * r + rs], k.gq[w * r : w * r + rs]])
+        for n in range(3):
+
+            def put(row, at, rows, row2, column, size):
+                src = k.gall[w * r + row2 : w * r + row2 + rows, n * C + column : n * C + column + size]
+                k.gst[w, row : row + rows, at : at + size] = src
+
+            place(n, put)
+        k.pkq[w] = k.gst[w].astype(BF16)
     scatter_start(M_QKV)
 
     def t_send(e):
@@ -855,17 +940,8 @@
     scatter_forward(M_QKV)
 
     k.o_tg[m_t] = tokens_total(0)
-    for q in (M_DOWN, M_UP, M_OUT, M_QKV):
+    for q in (M_DOWN, M_UP, M_OUT):
         scatter_end(q)
-    for e in range(1, MB):
-        m = later(e)
-        for out, ss, rs_ in ((k.o_tg, k.t_ss, k.t_rs), (k.o_mo, k.mo_ss, k.mo_rs)):
-            rcopy(out.at[m], out.at[m], ss.at[e], rs_.at[m], (b, d, h)).wait_recv()
-        for send in (c_send, x_send, mo_send, t_send):
-            send(e).wait_send()
-    for e in range(MB):
-        loop(S - 1, lambda f: x_pass(e, f + 1).wait_send())
-    loop(nb - MB, lambda n: tp_send(n).wait_send())
     for q in range(4):
         gather_drain(q)
     for p in range(1, nh):
@@ -875,9 +951,26 @@
             head_send(p_net, i, p).wait_send()
             for e in range(3):
                 st_send(e, i, p).wait_send()
-
-
-def finish_kernel(z, mo, tg, G, *outs):
+    for e in range(MB):
+        for c in range(2):
+            loop(S - 1, lambda f: x_pass(e, f + 1, c).wait_send())
+    loop(nb - MB, lambda n: tp_send(n).wait_send())
+    for e in range(1, MB):
+        m = later(e)
+        rcopy(k.o_mo.at[m], k.o_mo.at[m], k.mo_ss.at[e], k.mo_rs.at[m], (b, d, h)).wait_recv()
+        for send in (c_send, mo_send):
+            send(e).wait_send()
+        for c in range(2):
+            x_send(e, c).wait_send()
+
+    for e in range(1, MB):
+        m = later(e)
+        rcopy(k.o_tg.at[m], k.o_tg.at[m], k.t_ss.at[e], k.t_rs.at[m], (b, d, h)).wait_recv()
+        t_send(e).wait_send()
+    scatter_end(M_QKV)
+
+
+def finish_kernel(z, mo, tg, G, GQ, *outs):
     (mixed, dtok, dwq, dbq, dwk, dwv, dbv, dwo, dbo, dg1, ds1, dwup, dbu, dwdn, dbd, dg2, ds2, both) = outs
     r, rs, C, L = z.r, z.rs, z.C, z.L
     for m in range(z.MB):
@@ -892,18 +985,25 @@
         put_rows(z, mo[m].astype(F32), put_mixed)
         put_rows(z, tg[m].astype(F32), put_grad)
     mixed[...] = both[...].astype(BF16)
-    dwk[0] = G[M_QKV, 0:r, 0:C]
-    dwv[0] = G[M_QKV, 0:r, C:L]
-    dwq[0] = G[M_QKV, rs : rs + r, 0:C]
+    for n, ref in enumerate((dwk, dwv, dwq)):
+        column = 0
+        for block, at, size in pieces(C, n):
+            if block < z.full:
+                ref[0, :, column : column + size] = GQ[block * rs : block * rs + r, at : at + size]
+            else:
+                for where, row, rows in z.bits:
+                    part = GQ[z.left : z.left + rows, at + where : at + where + size]
+                    ref[0, row : row + rows, column : column + size] = part
+            column += size
     dwup[0, :, 0:L] = G[M_UP, 0:r]
     dwup[0, :, L : 2 * L] = G[M_UP, rs : rs + r]
     for q, ref in ((M_OUT, dwo), (M_DOWN, dwdn.at[0])):
         ref[0 : 2 * r] = G[q, 0 : 2 * r, 0:C]
         ref[2 * r : 4 * r] = G[q, 0 : 2 * r, C:L]
-    vecs = G[M_QKV, rs : 2 * rs, C : C + VECS].T
     for j, ref in enumerate((dbq, dbv, dbo, dg1, ds1, dbd, dg2, ds2)):
-        ref[...] = vecs[j : j + 1, 0:r]
-    dbu[...] = G[M_QKV, rs : rs + 1, C + VECS : C + VECS + 4 * r]
+        row, at = z.vrow + j // z.vper, j % z.vper * r
+        ref[...] = GQ[row : row + 1, at : at + r]
+    dbu[...] = GQ[z.brow : z.brow + 1, 0 : 4 * r]
 
 
 def solution(mesh):
@@ -938,7 +1038,8 @@
             out_shape=[
                 sds((z.MB, z.C, z.R), BF16),
                 sds((z.MB, z.C, z.R), BF16),
-                sds((4, z.rA, z.L), F32),
+                sds((3, z.rA, z.L), F32),
+                sds((z.rQ, 128), F32),
             ],
             in_specs=[smem] + [hbm] * len(operands),
             out_specs=[vmem] * len(OUTPUTS),

time: 68.9 us -> 66.9 us (0.971)
  Pallas kernels: 67.9 us -> 65.9 us
    pallas_call x1, Pallas kernels: 65.3 us -> 63.3 us  [body(): pl.pallas_call(lambda *refs: main_kernel(z, names, *refs), out_shape=[sds...]
where the time goes in v7:
time: 66.9 us; the launch traced here: 66.7 us
  Pallas kernels  65.9 us (99%)
  between operations  0.83 us (1%)
    pallas_call x1, Pallas kernels, body(): pl.pallas_call(lambda *refs: main_kernel(z, names, *refs), out_shape=[sds...  63.3 us
    pallas_call x1, Pallas kernels, body(): pl.pallas_call(lambda *refs: finish_kernel(z, *refs), out_shape=[sds((z.N...  2.55 us

profile of v7, /device:TPU:0, one launch (start us, length us, event | category | flops | bytes accessed | tf_op | source)
XLA Modules:
  0.0 66.7 jit_solution(3277496922466936879)
XLA Ops:
  0.7 63.3 %layer.1 = (bf16[2,192,256]{2,1,0:T(8,128)(2,1)}, bf16[2,192,256]{2,1,0:T(8,128)(2,1)}, f32[3,48,384]{2,1,0:T(8,128)}, f32[128,128]{1,0:T(8,128)}) custom-call(s32[2,1,4]{2,1,0:T(1,128)} %refs_0_.1, bf16[384,2,128]{2,1,0:T(2,128)(2,1)} %bitcast.10, bf16[384,2,128]{2,1,0:T(2,128)(2,1)} %bitcast.11, bf16[1,24,192]{2,1,0:T(8,128)(2,1)} %refs_3_.1, ...), custom_call_target="tpu_custom_call" | custom-call | tf_op jit(solution)/shard_map/layer/pallas_call | solution.py:1036
  64.0 2.6 %finish.1 = (bf16[384,2,128]{2,1,0:T(2,128)(2,1)}, f32[2,384,128]{2,1,0:T(8,128)}, f32[1,24,192]{2,1,0:T(8,128)}, f32[1,24]{1,0:T(1,128)}, f32[1,24,192]{2,1,0:T...) custom-call(bf16[2,192,256]{2,1,0:T(8,128)(2,1)} %get-tuple-element., ...), custom_call_target="tpu_custom_call" | custom-call | tf_op jit(solution)/shard_map/finish/pallas_call | solution.py:1053

commit v8 on v7

--- a/solution.py
+++ b/solution.py
@@ -250,12 +250,14 @@
     def other(n):
         return lax.rem(s_me + 1 + n // MB, S) + lax.rem(m_t + n, MB) * S
 
-    fetch = [
-        pltpu.make_async_copy(getattr(k, name), getattr(k, "v_" + name), k.in_sem.at[n])
+    copies = {
+        name: pltpu.make_async_copy(getattr(k, name), getattr(k, "v_" + name), k.in_sem.at[n])
         for n, name in enumerate(INPUTS[1:])
-    ]
-    for copy in fetch:
-        copy.start()
+    }
+    rest = ["wo_in", "wdn_in", "wup_in", "cot"]
+    first = [name for name in INPUTS[1:] if name not in rest and name != "tok"]
+    for name in first + ["tok"] + rest:
+        copies[name].start()
 
     bar = pltpu.get_barrier_semaphore()
     peers = [(lax.rem(b + i, nb), d, h) for i in range(1, nb)]
@@ -264,11 +266,8 @@
     for peer in peers:
         pl.semaphore_signal(bar, inc=1, device_id=peer, device_id_type=MESH)
 
-    for copy in fetch:
-        copy.wait()
-
-    def pack(q):
-        k.buf[q, w_me] = k.fst[...].astype(BF16)
+    for name in first:
+        copies[name].wait()
 
     def place(n, put):
         column = 0
@@ -298,6 +297,97 @@
         k.fsq[row : row + 1, at : at + r] = ref[...].astype(F32)
     k.fsq[z.brow : z.brow + 1, 0 : 4 * r] = k.v_bu[...].astype(F32)
     k.bufq[w_me] = k.fsq[...].astype(BF16)
+    pl.semaphore_wait(bar, len(peers))
+
+    def shares(q):
+        return k.bufq if q == M_QKV else k.buf.at[q]
+
+    def g1(q, i):
+        own = shares(q).at[w_me]
+        return rcopy(own, own, k.g1_ss.at[q, i], k.g1_rs.at[q, i], (lax.rem(b + i, nb), d, h))
+
+    def g1_wait(q, i):
+        src = shares(q).at[lax.rem(b + nb - i, nb) * nd + d]
+        rcopy(src, src, k.g1_ss.at[q, i], k.g1_rs.at[q, i], (b, d, h)).wait_recv()
+
+    def g2(q, e, i):
+        src = shares(q).at[lax.rem(b + nb - i, nb) * nd + d]
+        return rcopy(src, src, k.g2_ss.at[q, e - 1, i], k.g2_rs.at[q, e - 1, i], (b, lax.rem(d + e, nd), h))
+
+    def g2_wait(q, e, i):
+        src = shares(q).at[lax.rem(b + nb - i, nb) * nd + lax.rem(d + nd - e, nd)]
+        rcopy(src, src, k.g2_ss.at[q, e - 1, i], k.g2_rs.at[q, e - 1, i], (b, d, h)).wait_recv()
+
+    def gather_start(q):
+        for e in range(1, nd):
+            g2(q, e, 0).start()
+        loop(nb - 1, lambda i: g1(q, i + 1).start())
+
+    def gather_forward(q):
+        def one(i):
+            g1_wait(q, i + 1)
+            for e in range(1, nd):
+                g2(q, e, i + 1).start()
+
+        loop(nb - 1, one)
+
+    def gather_wait(q):
+        for e in range(1, nd):
+            loop(nb, lambda i: g2_wait(q, e, i))
+
+    def gather_drain(q):
+        if q != M_QKV:
+            loop(nb - 1, lambda i: g1(q, i + 1).wait_send())
+        for e in range(1, nd):
+            loop(nb, lambda i: g2(q, e, i).wait_send())
+
+    def in_step(n):
+        pl.semaphore_signal(k.sync.at[n], inc=1, device_id=(b, d, xor(1)), device_id_type=MESH)
+        pl.semaphore_wait(k.sync.at[n], 1)
+
+    gather_start(M_QKV)
+
+    def load_blocks(name, n, dst):
+        copies[name].wait()
+        both = getattr(k, "v_" + name)[...].astype(F32)
+        for m in range(MB):
+            k.flat[n * MB + m] = both[:, m]
+            dst[m] = columns_of(z, k.flat.at[n * MB + m]).astype(BF16)
+
+    load_blocks("tok", 0, k.xs)
+    k.xb[b] = k.xs[m_t]
+
+    halves = [pl.ds(0, C // 2), pl.ds(C // 2, C // 2)]
+
+    def x_send(e, c):
+        m = later(e)
+        dst = k.xb.at[b, halves[c]]
+        return rcopy(k.xs.at[m, halves[c]], dst, k.x_ss.at[e, c], k.x_rs.at[b, c], (m * S + s_me, d, h))
+
+    def x_pass(e, f, c):
+        src = k.xb.at[home(e), halves[c]]
+        return rcopy(src, src, k.xf_ss.at[e, f, c], k.x_rs.at[home(e), c], (m_t * S + mate(f), d, h))
+
+    def x_wait(j, c):
+        src = k.xb.at[j, halves[c]]
+        rcopy(src, src, k.x_ss.at[0, c], k.x_rs.at[j, c], (b, d, h)).wait_recv()
+
+    loop(nb - 1, lambda i: g1(M_QKV, i + 1).wait_send())
+    in_step(0)
+    for c in range(2):
+        for e in range(1, MB):
+            x_send(e, c).start()
+    for c in range(2):
+        loop(S - 1, lambda f: x_pass(0, f + 1, c).start())
+
+    load_blocks("cot", 1, k.cs)
+    k.cb[0] = k.cs[m_t]
+    for name in rest[:-1]:
+        copies[name].wait()
+
+    def pack(q):
+        k.buf[q, w_me] = k.fst[...].astype(BF16)
+
     k.fst[...] = jnp.zeros_like(k.fst)
     for q, src in ((M_OUT, k.v_wo_in[...]), (M_DOWN, k.v_wdn_in[0])):
         src = src.astype(F32)
@@ -307,87 +397,6 @@
     k.fst[0:r] = k.v_wup_in[0, :, 0:L].astype(F32)
     k.fst[rs : rs + r] = k.v_wup_in[0, :, L : 2 * L].astype(F32)
     pack(M_UP)
-
-    for n, (src, dst) in enumerate(((k.v_tok, k.xs), (k.v_cot, k.cs))):
-        both = src[...].astype(F32)
-        for m in range(MB):
-            k.flat[n * MB + m] = both[:, m]
-            dst[m] = columns_of(z, k.flat.at[n * MB + m]).astype(BF16)
-    k.xb[b] = k.xs[m_t]
-    k.cb[0] = k.cs[m_t]
-
-    pl.semaphore_wait(bar, len(peers))
-
-    def shares(q):
-        return k.bufq if q == M_QKV else k.buf.at[q]
-
-    def g1(q, i):
-        own = shares(q).at[w_me]
-        return rcopy(own, own, k.g1_ss.at[q, i], k.g1_rs.at[q, i], (lax.rem(b + i, nb), d, h))
-
-    def g1_wait(q, i):
-        src = shares(q).at[lax.rem(b + nb - i, nb) * nd + d]
-        rcopy(src, src, k.g1_ss.at[q, i], k.g1_rs.at[q, i], (b, d, h)).wait_recv()
-
-    def g2(q, e, i):
-        src = shares(q).at[lax.rem(b + nb - i, nb) * nd + d]
-        return rcopy(src, src, k.g2_ss.at[q, e - 1, i], k.g2_rs.at[q, e - 1, i], (b, lax.rem(d + e, nd), h))
-
-    def g2_wait(q, e, i):
-        src = shares(q).at[lax.rem(b + nb - i, nb) * nd + lax.rem(d + nd - e, nd)]
-        rcopy(src, src, k.g2_ss.at[q, e - 1, i], k.g2_rs.at[q, e - 1, i], (b, d, h)).wait_recv()
-
-    def gather_start(q):
-        for e in range(1, nd):
-            g2(q, e, 0).start()
-        loop(nb - 1, lambda i: g1(q, i + 1).start())
-
-    def gather_forward(q):
-        def one(i):
-            g1_wait(q, i + 1)
-            for e in range(1, nd):
-                g2(q, e, i + 1).start()
-
-        loop(nb - 1, one)
-
-    def gather_wait(q):
-        for e in range(1, nd):
-            loop(nb, lambda i: g2_wait(q, e, i))
-
-    def gather_drain(q):
-        if q != M_QKV:
-            loop(nb - 1, lambda i: g1(q, i + 1).wait_send())
-        for e in range(1, nd):
-            loop(nb, lambda i: g2(q, e, i).wait_send())
-
-    def in_step(n):
-        pl.semaphore_signal(k.sync.at[n], inc=1, device_id=(b, d, xor(1)), device_id_type=MESH)
-        pl.semaphore_wait(k.sync.at[n], 1)
-
-    gather_start(M_QKV)
-
-    halves = [pl.ds(0, C // 2), pl.ds(C // 2, C // 2)]
-
-    def x_send(e, c):
-        m = later(e)
-        dst = k.xb.at[b, halves[c]]
-        return rcopy(k.xs.at[m, halves[c]], dst, k.x_ss.at[e, c], k.x_rs.at[b, c], (m * S + s_me, d, h))
-
-    def x_pass(e, f, c):
-        src = k.xb.at[home(e), halves[c]]
-        return rcopy(src, src, k.xf_ss.at[e, f, c], k.x_rs.at[home(e), c], (m_t * S + mate(f), d, h))
-
-    def x_wait(j, c):
-        src = k.xb.at[j, halves[c]]
-        rcopy(src, src, k.x_ss.at[0, c], k.x_rs.at[j, c], (b, d, h)).wait_recv()
-
-    loop(nb - 1, lambda i: g1(M_QKV, i + 1).wait_send())
-    in_step(0)
-    for c in range(2):
-        for e in range(1, MB):
-            x_send(e, c).start()
-    for c in range(2):
-        loop(S - 1, lambda f: x_pass(0, f + 1, c).start())
 
     gather_forward(M_QKV)
 
@@ -549,8 +558,9 @@
         heads_done(e)
 
     gather_forward(M_OUT)
+    head_pass(o_net, 0)
     gather_forward(M_UP)
-    for e in range(MB):
+    for e in range(1, MB):
         head_pass(o_net, e)
     gather_wait(M_OUT)
 

time: 66.9 us -> 66.5 us (level)
  no operation moved by 1% of the time
where the time goes in v8:
time: 66.5 us; the launch traced here: 66.2 us
  Pallas kernels  65.4 us (98%)
  between operations  0.83 us (1%)
    pallas_call x1, Pallas kernels, body(): pl.pallas_call(lambda *refs: main_kernel(z, names, *refs), out_shape=[sds...  62.8 us
    pallas_call x1, Pallas kernels, body(): pl.pallas_call(lambda *refs: finish_kernel(z, *refs), out_shape=[sds((z.N...  2.55 us

profile of v8, /device:TPU:0, one launch (start us, length us, event | category | flops | bytes accessed | tf_op | source)
XLA Modules:
  0.0 66.2 jit_solution(5645684901082315120)
XLA Ops:
  0.7 62.8 %layer.1 = (bf16[2,192,256]{2,1,0:T(8,128)(2,1)}, bf16[2,192,256]{2,1,0:T(8,128)(2,1)}, f32[3,48,384]{2,1,0:T(8,128)}, f32[128,128]{1,0:T(8,128)}) custom-call(s32[2,1,4]{2,1,0:T(1,128)} %refs_0_.1, bf16[384,2,128]{2,1,0:T(2,128)(2,1)} %bitcast.10, bf16[384,2,128]{2,1,0:T(2,128)(2,1)} %bitcast.11, bf16[1,24,192]{2,1,0:T(8,128)(2,1)} %refs_3_.1, ...), custom_call_target="tpu_custom_call" | custom-call | tf_op jit(solution)/shard_map/layer/pallas_call | solution.py:1046
  63.5 2.6 %finish.1 = (bf16[384,2,128]{2,1,0:T(2,128)(2,1)}, f32[2,384,128]{2,1,0:T(8,128)}, f32[1,24,192]{2,1,0:T(8,128)}, f32[1,24]{1,0:T(1,128)}, f32[1,24,192]{2,1,0:T...) custom-call(bf16[2,192,256]{2,1,0:T(8,128)(2,1)} %get-tuple-element., ...), custom_call_target="tpu_custom_call" | custom-call | tf_op jit(solution)/shard_map/finish/pallas_call | solution.py:1063

commit v9 on v8

--- a/solution.py
+++ b/solution.py
@@ -192,34 +192,34 @@
         got1q=v((dd, nb, z.rQ, 128), BF16),
         sent2q=v((nb, z.rQ, 128), BF16),
         got2q=v((nb, z.rQ, 128), BF16),
-        sync=pltpu.SemaphoreType.REGULAR((2,)),
-        x_ss=dma((MB, 2)),
-        xf_ss=dma((MB, z.S, 2)),
-        x_rs=dma((nb, 2)),
-        c_ss=dma((MB,)),
+        sync=pltpu.SemaphoreType.REGULAR,
+        x_ss=dma,
+        xf_ss=dma,
+        x_rs=dma((MB, 2)),
+        xp_rs=dma((nb,)),
+        c_ss=dma,
         c_rs=dma((MB,)),
-        g1_ss=dma((4, nb)),
-        g1_rs=dma((4, nb)),
-        g2_ss=dma((4, dd, nb)),
-        g2_rs=dma((4, dd, nb)),
-        o_ss=dma((MB, nh)),
-        o_rs=dma((MB, nh)),
-        p_ss=dma((MB, nh)),
-        p_rs=dma((MB, nh)),
-        w_ss=dma((nh,)),
-        w_rs=dma((nh,)),
-        st_ss=dma((3, MB, nh)),
-        st_rs=dma((3, MB, nh)),
-        mo_ss=dma((MB,)),
+        g1_ss=dma((4,)),
+        g1_rs=dma((4, max(nb - 1, 1))),
+        g2_ss=dma((4,)),
+        g2_rs=dma((4,)),
+        o_ss=dma,
+        o_rs=dma((MB, 2)),
+        w_ss=dma,
+        w_rs=dma,
+        st_ss=dma((3,)),
+        st_rs=dma((3, MB)),
+        p_ss=dma,
+        p_rs=dma((MB, 2)),
+        mo_ss=dma,
         mo_rs=dma((MB,)),
-        tp_ss=dma((nb,)),
+        tp_ss=dma,
         tp_rs=dma((MB, z.S)),
-        t_ss=dma((MB,)),
+        t_ss=dma,
         t_rs=dma((MB,)),
-        s1_ss=dma((4, dd, nb)),
+        s_ss=dma((4,)),
         s1_rs=dma((4, dd, nb)),
-        s2_ss=dma((4, nb)),
-        s2_rs=dma((4, nb)),
+        s2_rs=dma((4,)),
         **{"v_" + name: v(a.shape, a.dtype) for name, a in zip(INPUTS[1:], inputs)},
     )
 
@@ -304,19 +304,15 @@
 
     def g1(q, i):
         own = shares(q).at[w_me]
-        return rcopy(own, own, k.g1_ss.at[q, i], k.g1_rs.at[q, i], (lax.rem(b + i, nb), d, h))
+        return rcopy(own, own, k.g1_ss.at[q], k.g1_rs.at[q, i - 1], (lax.rem(b + i, nb), d, h))
 
     def g1_wait(q, i):
         src = shares(q).at[lax.rem(b + nb - i, nb) * nd + d]
-        rcopy(src, src, k.g1_ss.at[q, i], k.g1_rs.at[q, i], (b, d, h)).wait_recv()
+        rcopy(src, src, k.g1_ss.at[q], k.g1_rs.at[q, i - 1], (b, d, h)).wait_recv()
 
     def g2(q, e, i):
         src = shares(q).at[lax.rem(b + nb - i, nb) * nd + d]
-        return rcopy(src, src, k.g2_ss.at[q, e - 1, i], k.g2_rs.at[q, e - 1, i], (b, lax.rem(d + e, nd), h))
-
-    def g2_wait(q, e, i):
-        src = shares(q).at[lax.rem(b + nb - i, nb) * nd + lax.rem(d + nd - e, nd)]
-        rcopy(src, src, k.g2_ss.at[q, e - 1, i], k.g2_rs.at[q, e - 1, i], (b, d, h)).wait_recv()
+        return rcopy(src, src, k.g2_ss.at[q], k.g2_rs.at[q], (b, lax.rem(d + e, nd), h))
 
     def gather_start(q):
         for e in range(1, nd):
@@ -332,18 +328,18 @@
         loop(nb - 1, one)
 
     def gather_wait(q):
-        for e in range(1, nd):
-            loop(nb, lambda i: g2_wait(q, e, i))
+        some = shares(q).at[pl.ds(0, nb * (nd - 1))]
+        rcopy(some, some, k.g2_ss.at[q], k.g2_rs.at[q], (b, d, h)).wait_recv()
+
+    def gather_sent(q):
+        some = shares(q).at[pl.ds(0, nb - 1)]
+        rcopy(some, some, k.g1_ss.at[q], k.g1_rs.at[q, 0], (b, d, h)).wait_send()
 
     def gather_drain(q):
         if q != M_QKV:
-            loop(nb - 1, lambda i: g1(q, i + 1).wait_send())
-        for e in range(1, nd):
-            loop(nb, lambda i: g2(q, e, i).wait_send())
-
-    def in_step(n):
-        pl.semaphore_signal(k.sync.at[n], inc=1, device_id=(b, d, xor(1)), device_id_type=MESH)
-        pl.semaphore_wait(k.sync.at[n], 1)
+            gather_sent(q)
+        some = shares(q).at[pl.ds(0, nb * (nd - 1))]
+        rcopy(some, some, k.g2_ss.at[q], k.g2_rs.at[q], (b, d, h)).wait_send()
 
     gather_start(M_QKV)
 
@@ -359,21 +355,28 @@
 
     halves = [pl.ds(0, C // 2), pl.ds(C // 2, C // 2)]
 
+    def slot_at(m):
+        return lax.rem(m_t + MB - m, MB)
+
     def x_send(e, c):
         m = later(e)
         dst = k.xb.at[b, halves[c]]
-        return rcopy(k.xs.at[m, halves[c]], dst, k.x_ss.at[e, c], k.x_rs.at[b, c], (m * S + s_me, d, h))
+        return rcopy(k.xs.at[m, halves[c]], dst, k.x_ss, k.x_rs.at[slot_at(m), c], (m * S + s_me, d, h))
 
     def x_pass(e, f, c):
         src = k.xb.at[home(e), halves[c]]
-        return rcopy(src, src, k.xf_ss.at[e, f, c], k.x_rs.at[home(e), c], (m_t * S + mate(f), d, h))
-
-    def x_wait(j, c):
-        src = k.xb.at[j, halves[c]]
-        rcopy(src, src, k.x_ss.at[0, c], k.x_rs.at[j, c], (b, d, h)).wait_recv()
-
-    loop(nb - 1, lambda i: g1(M_QKV, i + 1).wait_send())
-    in_step(0)
+        return rcopy(src, src, k.xf_ss, k.xp_rs.at[home(e)], (m_t * S + mate(f), d, h))
+
+    def x_wait(e, c):
+        src = k.xb.at[home(e), halves[c]]
+        rcopy(src, src, k.x_ss, k.x_rs.at[e, c], (b, d, h)).wait_recv()
+
+    def xp_wait(j):
+        rcopy(k.xb.at[j], k.xb.at[j], k.xf_ss, k.xp_rs.at[j], (b, d, h)).wait_recv()
+
+    gather_sent(M_QKV)
+    pl.semaphore_signal(k.sync, inc=1, device_id=(b, d, xor(1)), device_id_type=MESH)
+    pl.semaphore_wait(k.sync, 1)
     for c in range(2):
         for e in range(1, MB):
             x_send(e, c).start()
@@ -445,25 +448,28 @@
     def head_send(net, i, p):
         buf, ss, rs_ = net
         src, to = (h, xor(p)) if p <= half else (xor(half), xor(p - half))
-        return rcopy(buf.at[i, src], buf.at[i, src], ss.at[i, p], rs_.at[i, p], (b, d, to))
-
-    def head_wait(net, i, p):
-        buf, ss, rs_ = net
-        rcopy(buf.at[i, xor(p)], buf.at[i, xor(p)], ss.at[i, p], rs_.at[i, p], (b, d, h)).wait_recv()
+        return rcopy(buf.at[i, src], buf.at[i, src], ss, rs_.at[i, 0 if p == half else 1], (b, d, to))
 
     def head_start(net, i):
         for p in range(half, 0, -1):
             head_send(net, i, p).start()
 
     def head_pass(net, i):
-        head_wait(net, i, half)
+        buf, ss, rs_ = net
+        src = buf.at[i, xor(half)]
+        rcopy(src, src, ss, rs_.at[i, 0], (b, d, h)).wait_recv()
         for p in range(half + 1, nh):
             head_send(net, i, p).start()
 
     def head_end(net, i):
-        for p in range(1, nh):
-            if p != half:
-                head_wait(net, i, p)
+        buf, ss, rs_ = net
+        some = buf.at[i, pl.ds(0, nh - 2)]
+        rcopy(some, some, ss, rs_.at[i, 1], (b, d, h)).wait_recv()
+
+    def head_drain(net):
+        buf, ss, rs_ = net
+        some = buf.at[:, pl.ds(0, nh - 1)]
+        rcopy(some, some, ss, rs_.at[0, 0], (b, d, h)).wait_send()
 
     o_net = (k.oall, k.o_ss, k.o_rs)
     p_net = (k.pall, k.p_ss, k.p_rs)
@@ -523,7 +529,7 @@
 
     for c in range(2):
         for e in range(1, MB):
-            x_wait(home(e), c)
+            x_wait(e, c)
             loop(S - 1, lambda f: x_pass(e, f + 1, c).start())
     gather_start(M_OUT)
     gather_start(M_UP)
@@ -534,8 +540,7 @@
         attend([(e, t) for e in range(MB)])
 
     def attend_other(n):
-        for c in range(2):
-            x_wait(other(n), c)
+        xp_wait(other(n))
         kv_block(MB + n, other(n))
         attend([(e, MB + n) for e in range(MB)])
 
@@ -549,8 +554,7 @@
 
     last = nb - MB - 1
     loop(last, attend_other)
-    for c in range(2):
-        x_wait(other(last), c)
+    xp_wait(other(last))
     gather_start(M_DOWN)
     kv_block(MB + last, other(last))
     for e in range(MB):
@@ -568,7 +572,7 @@
 
     def w_send(p):
         src = k.buf.at[M_OUT, pl.ds(xor(p) * per, per)]
-        return rcopy(src, k.wob.at[h], k.w_ss.at[p], k.w_rs.at[p], (b, d, xor(p)))
+        return rcopy(src, k.wob.at[h], k.w_ss, k.w_rs, (b, d, xor(p)))
 
     for p in range(1, nh):
         w_send(p).start()
@@ -586,8 +590,8 @@
 
     def c_send(e):
         m = later(e)
-        slot = lax.rem(m_t + MB - m, MB)
-        return rcopy(k.cs.at[m], k.cb.at[slot], k.c_ss.at[e], k.c_rs.at[slot], (m * S + s_me, d, h))
+        slot = slot_at(m)
+        return rcopy(k.cs.at[m], k.cb.at[slot], k.c_ss, k.c_rs.at[slot], (m * S + s_me, d, h))
 
     for e in range(1, MB):
         c_send(e).start()
@@ -596,7 +600,7 @@
 
     def st_send(e, i, p):
         own = k.stats.at[e, i, h]
-        return rcopy(own, own, k.st_ss.at[e, i, p], k.st_rs.at[e, i, p], (b, d, xor(p)))
+        return rcopy(own, own, k.st_ss.at[e], k.st_rs.at[e, i], (b, d, xor(p)))
 
     def reduce_start(e, i, rows):
         for j, v in enumerate(rows):
@@ -610,9 +614,8 @@
             st_send(e, i, p).start()
 
     def reduce_end(e, i, n):
-        for p in range(1, nh):
-            src = k.stats.at[e, i, xor(p)]
-            rcopy(src, src, k.st_ss.at[e, i, p], k.st_rs.at[e, i, p], (b, d, h)).wait_recv()
+        some = k.stats.at[e, i, pl.ds(0, nh - 1)]
+        rcopy(some, some, k.st_ss.at[e], k.st_rs.at[e, i], (b, d, h)).wait_recv()
         total = k.stats[e, i, 0]
         for j in range(1, nh):
             total = total + k.stats[e, i, j]
@@ -668,7 +671,7 @@
         k.h2[i] = h2
 
         if i > 0:
-            rcopy(k.cb.at[i], k.cb.at[i], k.c_ss.at[0], k.c_rs.at[i], (b, d, h)).wait_recv()
+            rcopy(k.cb.at[i], k.cb.at[i], k.c_ss, k.c_rs.at[i], (b, d, h)).wait_recv()
         dn2 = k.cb[i].astype(F32) * vec(V_G2)
         reduce_start(1, i, (h2, h2 * h2, dn2, dn2 * h2))
         k.up[i], k.gel[i] = u, cdf
@@ -682,7 +685,7 @@
         k.vg[j : j + 1] += mm_nt(ones, x)[0:1]
 
     def mo_send(i):
-        return rcopy(k.mo.at[i], k.o_mo.at[m_t], k.mo_ss.at[i], k.mo_rs.at[m_t], (home(i), d, h))
+        return rcopy(k.mo.at[i], k.o_mo.at[m_t], k.mo_ss, k.mo_rs.at[m_t], (home(i), d, h))
 
     for i in range(MB):
         mean, square, dmean, dsquare = reduce_end(1, i, 4)
@@ -718,13 +721,13 @@
     def s1_send(q, e, i):
         dt = lax.rem(d + e, nd)
         return rcopy(
-            sums(q)[0].at[i * nd + dt], sums(q)[1].at[e - 1, i], k.s1_ss.at[q, e - 1, i], k.s1_rs.at[q, e - 1, i],
+            sums(q)[0].at[i * nd + dt], sums(q)[1].at[e - 1, i], k.s_ss.at[q], k.s1_rs.at[q, e - 1, i],
             (b, dt, h),
         )
 
     def s2_send(q, i):
         bt = lax.rem(b + i, nb)
-        return rcopy(sums(q)[2].at[bt], sums(q)[3].at[b], k.s2_ss.at[q, i], k.s2_rs.at[q, i], (bt, d, h))
+        return rcopy(sums(q)[2].at[bt], sums(q)[3].at[b], k.s_ss.at[q], k.s2_rs.at[q], (bt, d, h))
 
     def scatter_start(q):
         for e in range(1, nd):
@@ -734,7 +737,7 @@
         part = sums(q)[0][bt * nd + d].astype(F32)
         for e in range(1, nd):
             src = sums(q)[1].at[e - 1, bt]
-            rcopy(src, src, k.s1_ss.at[q, e - 1, bt], k.s1_rs.at[q, e - 1, bt], (b, d, h)).wait_recv()
+            rcopy(src, src, k.s_ss.at[q], k.s1_rs.at[q, e - 1, bt], (b, d, h)).wait_recv()
             part = part + src[...].astype(F32)
         return part
 
@@ -748,15 +751,15 @@
         sums(q)[4][...] = scatter_sum(q, b)
 
     def scatter_end(q):
+        some = sums(q)[3].at[pl.ds(0, nb - 1)]
+        rcopy(some, some, k.s_ss.at[q], k.s2_rs.at[q], (b, d, h)).wait_recv()
+
         def one(i):
-            src = sums(q)[3].at[lax.rem(b + nb - i - 1, nb)]
-            rcopy(src, src, k.s2_ss.at[q, i + 1], k.s2_rs.at[q, i + 1], (b, d, h)).wait_recv()
-            sums(q)[4][...] += src[...].astype(F32)
+            sums(q)[4][...] += sums(q)[3][lax.rem(b + nb - i - 1, nb)].astype(F32)
 
         loop(nb - 1, one)
-        loop(nb - 1, lambda i: s2_send(q, i + 1).wait_send())
-        for e in range(1, nd):
-            loop(nb, lambda i: s1_send(q, e, i).wait_send())
+        some = sums(q)[0].at[pl.ds(0, W - 1)]
+        rcopy(some, some, k.s_ss.at[q], k.s2_rs.at[q], (b, d, h)).wait_send()
 
     def rows_of(parts):
         rows = jnp.concatenate(parts, axis=0)
@@ -812,9 +815,8 @@
         pack_vec(j)
     k.gall[...] = jnp.zeros_like(k.gall)
 
-    for p in range(1, nh):
-        src = k.wob.at[xor(p)]
-        rcopy(src, src, k.w_ss.at[p], k.w_rs.at[p], (b, d, h)).wait_recv()
+    some_rows = k.wob.at[pl.ds(0, nh - 1)]
+    rcopy(some_rows, some_rows, k.w_ss, k.w_rs, (b, d, h)).wait_recv()
     k.wob[h] = k.buf[M_OUT, pl.ds(h * per, per)]
     for j in range(nh):
         for n in range(per):
@@ -876,7 +878,7 @@
     def tp_send(n):
         dst = k.tgr.at[n % MB, s_me]
         to = lax.rem(s_me + 1 + n // MB, S)
-        return rcopy(k.tgs.at[n], dst, k.tp_ss.at[n], k.tp_rs.at[n % MB, s_me], (m_t * S + to, d, h))
+        return rcopy(k.tgs.at[n], dst, k.tp_ss, k.tp_rs.at[n % MB, s_me], (m_t * S + to, d, h))
 
     def send_part(n, dkv):
         k.tgs[n] = tokens_part(other(n), dkv.astype(BF16)).astype(BF16)
@@ -927,14 +929,14 @@
     scatter_start(M_QKV)
 
     def t_send(e):
-        return rcopy(k.tgx.at[e], k.o_tg.at[m_t], k.t_ss.at[e], k.t_rs.at[m_t], (home(e), d, h))
+        return rcopy(k.tgx.at[e], k.o_tg.at[m_t], k.t_ss, k.t_rs.at[m_t], (home(e), d, h))
 
     def tokens_total(e):
         k.tgo[e] += k.dh1[e] + mm(k.wq[...], cols(k.dq, e))
 
         def add(f):
             src = k.tgr.at[e, mate(f + 1)]
-            rcopy(src, src, k.tp_ss.at[0], k.tp_rs.at[e, mate(f + 1)], (b, d, h)).wait_recv()
+            rcopy(src, src, k.tp_ss, k.tp_rs.at[e, mate(f + 1)], (b, d, h)).wait_recv()
             k.tgo[e] += src[...].astype(F32)
 
         loop(S - 1, add)
@@ -954,29 +956,27 @@
         scatter_end(q)
     for q in range(4):
         gather_drain(q)
-    for p in range(1, nh):
-        w_send(p).wait_send()
-        for i in range(MB):
-            head_send(o_net, i, p).wait_send()
-            head_send(p_net, i, p).wait_send()
-            for e in range(3):
-                st_send(e, i, p).wait_send()
-    for e in range(MB):
-        for c in range(2):
-            loop(S - 1, lambda f: x_pass(e, f + 1, c).wait_send())
-    loop(nb - MB, lambda n: tp_send(n).wait_send())
+    def drain(some, ss, rs_):
+        rcopy(some, some, ss, rs_, (b, d, h)).wait_send()
+
+    drain(some_rows, k.w_ss, k.w_rs)
+    head_drain(o_net)
+    head_drain(p_net)
+    for e in range(3):
+        drain(k.stats.at[e, :, pl.ds(0, nh - 1)], k.st_ss.at[e], k.st_rs.at[e, 0])
+    drain(k.xs.at[pl.ds(0, MB - 1)], k.x_ss, k.x_rs.at[0, 0])
+    drain(k.xb.at[pl.ds(0, MB * (S - 1))], k.xf_ss, k.xp_rs.at[0])
+    drain(k.cs.at[pl.ds(0, MB - 1)], k.c_ss, k.c_rs.at[0])
+    drain(k.mo.at[pl.ds(0, MB - 1)], k.mo_ss, k.mo_rs.at[0])
+    drain(k.tgs.at[pl.ds(0, nb - MB)], k.tp_ss, k.tp_rs.at[0, 0])
     for e in range(1, MB):
         m = later(e)
-        rcopy(k.o_mo.at[m], k.o_mo.at[m], k.mo_ss.at[e], k.mo_rs.at[m], (b, d, h)).wait_recv()
-        for send in (c_send, mo_send):
-            send(e).wait_send()
-        for c in range(2):
-            x_send(e, c).wait_send()
+        rcopy(k.o_mo.at[m], k.o_mo.at[m], k.mo_ss, k.mo_rs.at[m], (b, d, h)).wait_recv()
 
     for e in range(1, MB):
         m = later(e)
-        rcopy(k.o_tg.at[m], k.o_tg.at[m], k.t_ss.at[e], k.t_rs.at[m], (b, d, h)).wait_recv()
-        t_send(e).wait_send()
+        rcopy(k.o_tg.at[m], k.o_tg.at[m], k.t_ss, k.t_rs.at[m], (b, d, h)).wait_recv()
+    drain(k.tgx.at[pl.ds(0, MB - 1)], k.t_ss, k.t_rs.at[0])
     scatter_end(M_QKV)
 
 

time: 66.5 us -> 65 us (0.977)
  Pallas kernels: 65.4 us -> 63.9 us
    pallas_call x1, Pallas kernels: 62.8 us -> 61.4 us  [body(): pl.pallas_call(lambda *refs: main_kernel(z, names, *refs), out_shape=[sds...]
where the time goes in v9:
time: 65 us; the launch traced here: 64.8 us
  Pallas kernels  63.9 us (98%)
  between operations  0.83 us (1%)
    pallas_call x1, Pallas kernels, body(): pl.pallas_call(lambda *refs: main_kernel(z, names, *refs), out_shape=[sds...  61.4 us
    pallas_call x1, Pallas kernels, body(): pl.pallas_call(lambda *refs: finish_kernel(z, *refs), out_shape=[sds((z.N...  2.55 us

profile of v9, /device:TPU:0, one launch (start us, length us, event | category | flops | bytes accessed | tf_op | source)
XLA Modules:
  0.0 64.8 jit_solution(16113632897558494858)
XLA Ops:
  0.7 61.4 %layer.1 = (bf16[2,192,256]{2,1,0:T(8,128)(2,1)}, bf16[2,192,256]{2,1,0:T(8,128)(2,1)}, f32[3,48,384]{2,1,0:T(8,128)}, f32[128,128]{1,0:T(8,128)}) custom-call(s32[2,1,4]{2,1,0:T(1,128)} %refs_0_.1, bf16[384,2,128]{2,1,0:T(2,128)(2,1)} %bitcast.10, bf16[384,2,128]{2,1,0:T(2,128)(2,1)} %bitcast.11, bf16[1,24,192]{2,1,0:T(8,128)(2,1)} %refs_3_.1, ...), custom_call_target="tpu_custom_call" | custom-call | tf_op jit(solution)/shard_map/layer/pallas_call | solution.py:1046
  62.1 2.6 %finish.1 = (bf16[384,2,128]{2,1,0:T(2,128)(2,1)}, f32[2,384,128]{2,1,0:T(8,128)}, f32[1,24,192]{2,1,0:T(8,128)}, f32[1,24]{1,0:T(1,128)}, f32[1,24,192]{2,1,0:T...) custom-call(bf16[2,192,256]{2,1,0:T(8,128)(2,1)} %get-tuple-element., ...), custom_call_target="tpu_custom_call" | custom-call | tf_op jit(solution)/shard_map/finish/pallas_call | solution.py:1063

commit v10 on v9

--- a/solution.py
+++ b/solution.py
@@ -118,7 +118,7 @@
     nb, W, L, R, C, F, Q, H, MB, rA, nh = z.nb, z.W, z.L, z.R, z.C, z.F, z.Q, z.H, z.MB, z.rA, z.nh
     dd = max(z.nd - 1, 1)
     return dict(
-        in_sem=dma((len(INPUTS) - 1,)),
+        in_sem=dma((len(INPUTS),)),
         flat=v((2 * MB, z.N, 128), F32),
         xs=v((MB, C, R), BF16),
         xb=v((nb, C, R), BF16),
@@ -218,9 +218,11 @@
         t_ss=dma,
         t_rs=dma((MB,)),
         s_ss=dma((4,)),
-        s1_rs=dma((4, dd, nb)),
+        s1_rs=dma((3,)),
+        s1q_rs=dma((dd, nb)),
         s2_rs=dma((4,)),
-        **{"v_" + name: v(a.shape, a.dtype) for name, a in zip(INPUTS[1:], inputs)},
+        v_lens=pltpu.SMEM(inputs[0].shape, inputs[0].dtype),
+        **{"v_" + name: v(a.shape, a.dtype) for name, a in zip(INPUTS[1:], inputs[1:])},
     )
 
 
@@ -252,10 +254,10 @@
 
     copies = {
         name: pltpu.make_async_copy(getattr(k, name), getattr(k, "v_" + name), k.in_sem.at[n])
-        for n, name in enumerate(INPUTS[1:])
+        for n, name in enumerate(INPUTS)
     }
-    rest = ["wo_in", "wdn_in", "wup_in", "cot"]
-    first = [name for name in INPUTS[1:] if name not in rest and name != "tok"]
+    rest = ["wo_in", "wdn_in", "wup_in", "lens", "cot"]
+    first = [name for name in INPUTS if name not in rest and name != "tok"]
     for name in first + ["tok"] + rest:
         copies[name].start()
 
@@ -441,7 +443,7 @@
         doc = jnp.zeros((16, R), jnp.int32)
         end = jnp.int32(0)
         for n in range(z.ND):
-            end = end + k.lens[m_t, 0, n]
+            end = end + k.v_lens[m_t, 0, n]
             doc = doc + (j * R + token >= end).astype(jnp.int32)
         return row16 == doc
 
@@ -718,10 +720,13 @@
             return k.pkq, k.got1q, k.sent2q, k.got2q, k.o_Q
         return k.pk.at[q], k.got1.at[q], k.sent2.at[q], k.got2.at[q], k.o_G.at[q]
 
+    def s1_sem(q, e, i):
+        return k.s1q_rs.at[e - 1, i] if q == M_QKV else k.s1_rs.at[q]
+
     def s1_send(q, e, i):
         dt = lax.rem(d + e, nd)
         return rcopy(
-            sums(q)[0].at[i * nd + dt], sums(q)[1].at[e - 1, i], k.s_ss.at[q], k.s1_rs.at[q, e - 1, i],
+            sums(q)[0].at[i * nd + dt], sums(q)[1].at[e - 1, i], k.s_ss.at[q], s1_sem(q, e, i),
             (b, dt, h),
         )
 
@@ -737,11 +742,15 @@
         part = sums(q)[0][bt * nd + d].astype(F32)
         for e in range(1, nd):
             src = sums(q)[1].at[e - 1, bt]
-            rcopy(src, src, k.s_ss.at[q], k.s1_rs.at[q, e - 1, bt], (b, d, h)).wait_recv()
+            if q == M_QKV:
+                rcopy(src, src, k.s_ss.at[q], s1_sem(q, e, bt), (b, d, h)).wait_recv()
             part = part + src[...].astype(F32)
         return part
 
     def scatter_forward(q):
+        if q != M_QKV:
+            rcopy(sums(q)[1], sums(q)[1], k.s_ss.at[q], s1_sem(q, 1, 0), (b, d, h)).wait_recv()
+
         def one(i):
             bt = lax.rem(b + i + 1, nb)
             sums(q)[2][bt] = scatter_sum(q, bt).astype(BF16)
@@ -1033,13 +1042,12 @@
             return a.reshape(z.MB, z.N, 128).transpose(1, 0, 2)
 
         operands = (
-            as_rows(tokens), as_rows(cotangent), query_weight, query_bias, key_weight, value_weight, value_bias,
+            doc_lengths, as_rows(tokens), as_rows(cotangent), query_weight, query_bias, key_weight, value_weight, value_bias,
             out_weight, out_bias, first_gain, first_shift, up_weight, up_bias, down_weight, down_bias, second_gain,
             second_shift,
         )
         scratch = main_scratch(z, operands)
         vmem = pl.BlockSpec(memory_space=pltpu.VMEM)
-        smem = pl.BlockSpec(memory_space=pltpu.SMEM)
         hbm = pl.BlockSpec(memory_space=pltpu.HBM)
         names = INPUTS + OUTPUTS + list(scratch)
         sds = jax.ShapeDtypeStruct
@@ -1051,14 +1059,14 @@
                 sds((3, z.rA, z.L), F32),
                 sds((z.rQ, 128), F32),
             ],
-            in_specs=[smem] + [hbm] * len(operands),
+            in_specs=[hbm] * len(operands),
             out_specs=[vmem] * len(OUTPUTS),
             scratch_shapes=list(scratch.values()),
             compiler_params=pltpu.CompilerParams(
                 collective_id=0, has_side_effects=True, vmem_limit_bytes=63 << 20
             ),
             name="layer",
-        )(doc_lengths, *operands)
+        )(*operands)
         mat, vec = sds((1, z.r, z.C), F32), sds((1, z.r), F32)
         outs = pl.pallas_call(
             lambda *refs: finish_kernel(z, *refs),

time: 65 us -> 64.3 us (0.989)
  Pallas kernels: 63.9 us -> 63.2 us
    pallas_call x1, Pallas kernels: 61.4 us -> 60.7 us  [body(): pl.pallas_call(lambda *refs: main_kernel(z, names, *refs), out_shape=[sds...]
where the time goes in v10:
time: 64.3 us; the launch traced here: 64 us
  Pallas kernels  63.2 us (98%)
  between operations  0.83 us (1%)
    pallas_call x1, Pallas kernels, body(): pl.pallas_call(lambda *refs: main_kernel(z, names, *refs), out_shape=[sds...  60.7 us
    pallas_call x1, Pallas kernels, body(): pl.pallas_call(lambda *refs: finish_kernel(z, *refs), out_shape=[sds((z.N...  2.55 us

profile of v10, /device:TPU:0, one launch (start us, length us, event | category | flops | bytes accessed | tf_op | source)
XLA Modules:
  0.0 64.0 jit_solution(16504738163298148863)
XLA Ops:
  0.7 60.7 %layer.1 = (bf16[2,192,256]{2,1,0:T(8,128)(2,1)}, bf16[2,192,256]{2,1,0:T(8,128)(2,1)}, f32[3,48,384]{2,1,0:T(8,128)}, f32[128,128]{1,0:T(8,128)}) custom-call(s32[2,1,4]{2,1,0:T(1,128)} %refs_0_.1, bf16[384,2,128]{2,1,0:T(2,128)(2,1)} %bitcast.10, bf16[384,2,128]{2,1,0:T(2,128)(2,1)} %bitcast.11, bf16[1,24,192]{2,1,0:T(8,128)(2,1)} %refs_3_.1, ...), custom_call_target="tpu_custom_call" | custom-call | tf_op jit(solution)/shard_map/layer/pallas_call | solution.py:1054
  61.3 2.6 %finish.1 = (bf16[384,2,128]{2,1,0:T(2,128)(2,1)}, f32[2,384,128]{2,1,0:T(8,128)}, f32[1,24,192]{2,1,0:T(8,128)}, f32[1,24]{1,0:T(1,128)}, f32[1,24,192]{2,1,0:T...) custom-call(bf16[2,192,256]{2,1,0:T(8,128)(2,1)} %get-tuple-element., ...), custom_call_target="tpu_custom_call" | custom-call | tf_op jit(solution)/shard_map/finish/pallas_call | solution.py:1071

commit v11 on v10

--- a/solution.py
+++ b/solution.py
@@ -109,6 +109,8 @@
     "lens", "tok", "cot", "wq_in", "bq", "wk_in", "wv_in", "bv", "wo_in", "bo", "g1", "s1", "wup_in", "bu",
     "wdn_in", "bd", "g2", "s2",
 ]
+MATS = ["wk_in", "wv_in", "wq_in"]
+VECS = ["bq", "bv", "bo", "g1", "s1", "bd", "g2", "s2"]
 OUTPUTS = ["o_mo", "o_tg", "o_G", "o_Q"]
 
 
@@ -118,7 +120,7 @@
     nb, W, L, R, C, F, Q, H, MB, rA, nh = z.nb, z.W, z.L, z.R, z.C, z.F, z.Q, z.H, z.MB, z.rA, z.nh
     dd = max(z.nd - 1, 1)
     return dict(
-        in_sem=dma((len(INPUTS),)),
+        in_sem=dma((len(INPUTS) - len(MATS) - len(VECS) + 2,)),
         flat=v((2 * MB, z.N, 128), F32),
         xs=v((MB, C, R), BF16),
         xb=v((nb, C, R), BF16),
@@ -222,7 +224,9 @@
         s1q_rs=dma((dd, nb)),
         s2_rs=dma((4,)),
         v_lens=pltpu.SMEM(inputs[0].shape, inputs[0].dtype),
-        **{"v_" + name: v(a.shape, a.dtype) for name, a in zip(INPUTS[1:], inputs[1:])},
+        v_mats=v((len(MATS), 1, z.r, C), BF16),
+        v_vecs=v((len(VECS), 1, z.r), BF16),
+        **{"v_" + x: v(a.shape, a.dtype) for x, a in zip(INPUTS[1:], inputs[1:]) if x not in MATS + VECS},
     )
 
 
@@ -252,13 +256,16 @@
     def other(n):
         return lax.rem(s_me + 1 + n // MB, S) + lax.rem(m_t + n, MB) * S
 
+    single = [name for name in INPUTS if name not in MATS + VECS]
     copies = {
-        name: pltpu.make_async_copy(getattr(k, name), getattr(k, "v_" + name), k.in_sem.at[n])
-        for n, name in enumerate(INPUTS)
+        name: pltpu.make_async_copy(getattr(k, name), getattr(k, "v_" + name), k.in_sem.at[n + 2])
+        for n, name in enumerate(single)
     }
     rest = ["wo_in", "wdn_in", "wup_in", "lens", "cot"]
-    first = [name for name in INPUTS if name not in rest and name != "tok"]
-    for name in first + ["tok"] + rest:
+    for n, (names_, dst) in enumerate(((MATS, k.v_mats), (VECS, k.v_vecs))):
+        for i, name in enumerate(names_):
+            pltpu.make_async_copy(getattr(k, name), dst.at[i], k.in_sem.at[n]).start()
+    for name in ["bu", "tok"] + rest:
         copies[name].start()
 
     bar = pltpu.get_barrier_semaphore()
@@ -268,8 +275,9 @@
     for peer in peers:
         pl.semaphore_signal(bar, inc=1, device_id=peer, device_id_type=MESH)
 
-    for name in first:
-        copies[name].wait()
+    for n, dst in enumerate((k.v_mats, k.v_vecs)):
+        pltpu.make_async_copy(dst, dst, k.in_sem.at[n]).wait()
+    copies["bu"].wait()
 
     def place(n, put):
         column = 0
@@ -281,22 +289,20 @@
                     put(z.left, at + where, rows, row, column, size)
             column += size
 
-    vectors = (k.v_bq, k.v_bv, k.v_bo, k.v_g1, k.v_s1, k.v_bd, k.v_g2, k.v_s2)
-
     def vec_at(j):
         return z.vrow + j // z.vper, j % z.vper * r
 
     k.fsq[...] = jnp.zeros_like(k.fsq)
-    for n, src in enumerate((k.v_wk_in[0], k.v_wv_in[0], k.v_wq_in[0])):
-        src = src.astype(F32)
+    for n in range(len(MATS)):
+        src = k.v_mats[n, 0].astype(F32)
 
         def put(row, at, rows, row2, column, size):
             k.fsq[row : row + rows, at : at + size] = src[row2 : row2 + rows, column : column + size]
 
         place(n, put)
-    for j, ref in enumerate(vectors):
+    for j in range(len(VECS)):
         row, at = vec_at(j)
-        k.fsq[row : row + 1, at : at + r] = ref[...].astype(F32)
+        k.fsq[row : row + 1, at : at + r] = k.v_vecs[j].astype(F32)
     k.fsq[z.brow : z.brow + 1, 0 : 4 * r] = k.v_bu[...].astype(F32)
     k.bufq[w_me] = k.fsq[...].astype(BF16)
     pl.semaphore_wait(bar, len(peers))
@@ -317,9 +323,9 @@
         return rcopy(src, src, k.g2_ss.at[q], k.g2_rs.at[q], (b, lax.rem(d + e, nd), h))
 
     def gather_start(q):
+        loop(nb - 1, lambda i: g1(q, i + 1).start())
         for e in range(1, nd):
             g2(q, e, 0).start()
-        loop(nb - 1, lambda i: g1(q, i + 1).start())
 
     def gather_forward(q):
         def one(i):

time: 64.3 us -> 64.2 us (level)
  no operation moved by 1% of the time
where the time goes in v11:
time: 64.2 us; the launch traced here: 64 us
  Pallas kernels  63.1 us (98%)
  between operations  0.83 us (1%)
    pallas_call x1, Pallas kernels, body(): pl.pallas_call(lambda *refs: main_kernel(z, names, *refs), out_shape=[sds...  60.6 us
    pallas_call x1, Pallas kernels, body(): pl.pallas_call(lambda *refs: finish_kernel(z, *refs), out_shape=[sds((z.N...  2.55 us

profile of v11, /device:TPU:0, one launch (start us, length us, event | category | flops | bytes accessed | tf_op | source)
XLA Modules:
  0.0 64.0 jit_solution(16122589712512251053)
XLA Ops:
  0.7 60.6 %layer.1 = (bf16[2,192,256]{2,1,0:T(8,128)(2,1)}, bf16[2,192,256]{2,1,0:T(8,128)(2,1)}, f32[3,48,384]{2,1,0:T(8,128)}, f32[128,128]{1,0:T(8,128)}) custom-call(s32[2,1,4]{2,1,0:T(1,128)} %refs_0_.1, bf16[384,2,128]{2,1,0:T(2,128)(2,1)} %bitcast.10, bf16[384,2,128]{2,1,0:T(2,128)(2,1)} %bitcast.11, bf16[1,24,192]{2,1,0:T(8,128)(2,1)} %refs_3_.1, ...), custom_call_target="tpu_custom_call" | custom-call | tf_op jit(solution)/shard_map/layer/pallas_call | solution.py:1060
  61.3 2.6 %finish.1 = (bf16[384,2,128]{2,1,0:T(2,128)(2,1)}, f32[2,384,128]{2,1,0:T(8,128)}, f32[1,24,192]{2,1,0:T(8,128)}, f32[1,24]{1,0:T(1,128)}, f32[1,24,192]{2,1,0:T...) custom-call(bf16[2,192,256]{2,1,0:T(8,128)(2,1)} %get-tuple-element., ...), custom_call_target="tpu_custom_call" | custom-call | tf_op jit(solution)/shard_map/finish/pallas_call | solution.py:1077
